TPU v7x, 256 devices: a whole 4x4x8 slice. The times are simulated.
256 devices in a mesh: seq: 64 (over z, x, core), head: 4 (over y).
Axes of the slice: x: 4, y: 4, z: 8, core: 2. Of those that a mesh axis runs over, the one named last changes fastest.
Arguments:
- query_key: bfloat16 [32768, 128], P('seq'), may hold values from -1.5 to 1.5
- values: bfloat16 [32768, 5120], P('seq', 'head'), may hold values from -0.119628906 to 0.119628906
- cotangent: bfloat16 [32768, 5120], P('seq', 'head'), may hold values from -0.119628906 to 0.119628906
- level_gain: float32 [16, 15, 80], P(None, None, 'head'), may hold values from 0.1 to 1
- level_code: int32 [512], P('seq'), may hold values from 0 to 15
Outputs:
- mixed: bfloat16 [32768, 5120], P('seq', 'head')
- grad_qk: float32 [32768, 128], P('seq')
- grad_values: bfloat16 [32768, 5120], P('seq', 'head')
Inputs may be any that keep to these rules, and one draw needn't show every extreme that they name: `level_code`: each span's row of the weight table.
All inputs are finite; a program needn't handle non-finite values.
Results may differ from a plain program's by a relative error of at most 0.005.
Values sent between devices are 32-bit elements; how exact they have to be, the bound alone decides.
No kernel may reach another device: no remote copies, remote signals or barrier semaphores. Data moves between devices by JAX's collectives and lax.ppermute only.
A program may use at most 128 MiB of HBM per device.

v0:
```python
import jax
import jax.numpy as jnp
from jax import lax
from jax.sharding import PartitionSpec as P

HEAD_DIM = 64
CH = 64


precise = lax.Precision.HIGHEST


def partner_2(value, axis, bit):
    mask = 2**bit
    pairs = [(source, source ^ mask) for source in range(lax.axis_size(axis))]
    return lax.ppermute(value, axis, pairs)


def bit_length(numbers, top_bits):
    bit_total = jnp.zeros_like(numbers)
    for bit_power in range(top_bits):
        bit_total = bit_total + (numbers >= 1 << bit_power).astype(jnp.int32)
    return bit_total


def local_levels(span_count):
    span_ids = jnp.arange(span_count, dtype=jnp.int32)
    return bit_length(span_ids[:, None] ^ span_ids[None, :], 8)


def local(query_key, values, cotangent, level_gain, level_code):
    tok_rows, state_dim = query_key.shape
    head_cols = values.shape[1]
    codes, levels, group_heads = level_gain.shape
    span_count = tok_rows // CH
    span_levels = span_count.bit_length() - 1
    seq_levels = lax.axis_size("seq").bit_length() - 1
    position = lax.axis_index("seq")
    picked = (level_code[:, None] == jnp.arange(codes, dtype=jnp.int32)[None, :]).astype(
        jnp.float32
    )
    level_weight = jnp.dot(
        picked, level_gain.reshape(codes, levels * group_heads), precision=precise
    ).reshape(span_count, levels, group_heads)
    cross_cols = jnp.repeat(
        level_weight[:, span_levels + 1 : span_levels + 1 + seq_levels, :], HEAD_DIM, axis=-1
    )
    own_state = lax.dot_general(
        query_key, values, (((0,), (0,)), ((), ())), preferred_element_type=jnp.float32
    )
    q_spans = query_key.reshape(span_count, CH, state_dim)
    c_spans = cotangent.reshape(span_count, CH, head_cols)
    span_grad = jnp.einsum("cti,ctj->cij", q_spans, c_spans, preferred_element_type=jnp.float32)
    level_grad = jnp.einsum("cij,clj->lij", span_grad, cross_cols, precision=precise)
    siblings = []
    adjoint = jnp.zeros_like(own_state)
    block_sum = own_state
    level_carry = level_grad
    for level_bit in range(seq_levels):
        partner = partner_2(block_sum, "seq", level_bit)
        upper_half = position >> level_bit & 1 == 1
        siblings.append(jnp.where(upper_half, partner, 0.0))
        block_sum = block_sum + partner
    for level_bit in range(seq_levels):
        partner_grad = partner_2(level_carry, "seq", level_bit)
        upper_half = position >> level_bit & 1 == 1
        adjoint = adjoint + jnp.where(upper_half, 0.0, partner_grad[0])
        level_carry = (level_carry + partner_grad)[1:]
    sibling = jnp.stack(siblings)
    span_state = jnp.einsum("clj,lij->cij", cross_cols, sibling, precision=precise).astype(
        jnp.bfloat16
    )
    adjoint_bf = adjoint.astype(jnp.bfloat16)
    scores = lax.dot_general(
        query_key, query_key, (((1,), (1,)), ((), ())), preferred_element_type=jnp.float32
    )
    onehot = (
        local_levels(span_count)[:, :, None]
        == jnp.arange(span_levels + 1, dtype=jnp.int32)[None, None, :]
    ).astype(jnp.float32)
    local_weight = jnp.einsum(
        "abk,akg->gab", onehot, level_weight[:, : span_levels + 1, :], precision=precise
    )
    causal = jnp.tril(jnp.ones((tok_rows, tok_rows), dtype=bool))
    pair_cols = 2 * HEAD_DIM

    def head_pair(pair_index, running):
        inner_out, dv_inner, d_score = running
        col_start = pair_index * pair_cols
        val_pair = lax.dynamic_slice_in_dim(values, col_start, pair_cols, 1).reshape(
            tok_rows, 2, HEAD_DIM
        )
        cot_pair = lax.dynamic_slice_in_dim(cotangent, col_start, pair_cols, 1).reshape(
            tok_rows, 2, HEAD_DIM
        )
        pair_weight = lax.dynamic_slice_in_dim(local_weight, pair_index * 2, 2, 0)
        weight = jnp.broadcast_to(
            pair_weight[:, :, None, :, None], (2, span_count, CH, span_count, CH)
        ).reshape(2, tok_rows, tok_rows)
        mixing = jnp.where(causal, weight * scores, 0.0).astype(jnp.bfloat16)
        part_out = jnp.einsum(
            "gts,sgp->tgp", mixing, val_pair, preferred_element_type=jnp.float32
        ).reshape(tok_rows, pair_cols)
        d_mix = jnp.einsum("tgp,sgp->gts", cot_pair, val_pair, preferred_element_type=jnp.float32)
        d_score = d_score + jnp.sum(jnp.where(causal, weight * d_mix, 0.0), axis=0)
        part_dv = jnp.einsum(
            "gts,tgp->sgp", mixing, cot_pair, preferred_element_type=jnp.float32
        ).reshape(tok_rows, pair_cols)
        inner_out = lax.dynamic_update_slice_in_dim(inner_out, part_out, col_start, 1)
        dv_inner = lax.dynamic_update_slice_in_dim(dv_inner, part_dv, col_start, 1)
        return (inner_out, dv_inner, d_score)

    start_state = (
        jnp.zeros((tok_rows, head_cols), jnp.float32),
        jnp.zeros((tok_rows, head_cols), jnp.float32),
        jnp.zeros((tok_rows, tok_rows), jnp.float32),
    )
    inner_out, dv_inner, d_score = lax.fori_loop(0, group_heads // 2, head_pair, start_state)
    outer_out = jnp.einsum(
        "cti,cij->ctj", q_spans, span_state, preferred_element_type=jnp.float32
    ).reshape(tok_rows, head_cols)
    mixed = (inner_out + outer_out).astype(jnp.bfloat16)
    dq_outer = jnp.einsum(
        "ctj,cij->cti", c_spans, span_state, preferred_element_type=jnp.float32
    ).reshape(tok_rows, state_dim)
    dv_outer = jnp.dot(query_key, adjoint_bf, preferred_element_type=jnp.float32)
    dk_outer = lax.dot_general(
        values, adjoint_bf, (((1,), (1,)), ((), ())), preferred_element_type=jnp.float32
    )
    q_float = query_key.astype(jnp.float32)
    dq_inner = jnp.dot(d_score, q_float, precision=precise) + lax.dot_general(
        d_score, q_float, (((0,), (0,)), ((), ())), precision=precise
    )
    head_part = dq_inner + dq_outer + dk_outer
    grad_qk = lax.psum(head_part, "head")
    grad_values = (dv_inner + dv_outer).astype(jnp.bfloat16)
    return (mixed, grad_qk, grad_values)


def solution(mesh):
    placed = (P("seq", None), P("seq", "head"), P("seq", "head"), P(None, None, "head"), P("seq"))
    return jax.shard_map(
        local,
        mesh=mesh,
        in_specs=placed,
        out_specs=(P("seq", "head"), P("seq", None), P("seq", "head")),
        check_vma=False,
    )
```

profile of v0, /device:TPU:1, one launch (start us, length us, event | category | flops | bytes accessed | tf_op | source)
XLA Modules:
  0.0 711.8 jit_solution(9387156875039487626)
XLA Ops:
  8.1 4.5 fusion.36
  12.6 6.3 copy.78
  24.0 10.4 %fusion.37 = f32[1280,6,128]{2,1,0:T(8,128)} fusion(f32[8,6,1280]{0,1,2:T(8,128)S(1)} %bitcast.108, f32[8,128,1280]{1,0,2:T(8,128)S(1)} %copy-done.4), kind=kOutput, calls=%fused_computation.70 | convolution fusion | flops 94371840 | bytes 9420800 | tf_op jit(solution)/shard_map/cij,clj->lij/dot_general | solution.py:54
  34.4 5.7 copy.79
  43.3 6.6 collective-permute-done.6
  49.9 3.8 slice_add_fusion
  53.8 72.1 %collective-permute-done.7 = f32[5,128,1280]{2,1,0:T(8,128)S(1)} collective-permute-done((f32[5,128,1280]{2,1,0:T(8,128)S(1)}, f32[5,128,1280]{2,1,0:T(8,128)S(1)}, u32[]{:S(2)}, u32[]{:S(2)}) %collective-permute-start.7) | collective-permute-done | bytes 3276832 | tf_op jit(solution)/shard_map/ppermute | solution.py:16
  136.7 63.0 %collective-permute-done.1 = f32[128,1280]{1,0:T(8,128)S(1)} collective-permute-done((f32[128,1280]{1,0:T(8,128)S(1)}, f32[128,1280]{1,0:T(8,128)S(1)}, u32[]{:S(2)}, u32[]{:S(2)}) %collective-permute-start.1) | collective-permute-done | bytes 655392 | tf_op jit(solution)/shard_map/ppermute | solution.py:16
  203.6 3.7 slice_add_fusion.2
  211.2 230.9 %while.19 = (s32[]{:T(128)}, f32[512,1280]{1,0:T(8,128)}, f32[512,1280]{0,1:T(8,128)}, f32[512,512]{1,0:T(8,128)}, bf16[512,1280]{1,0:T(8,128)(2,1)S(1)}, /*inde...) while((s32[]{:T(128)}, f32[512,1280]{1,0:T(8,128)}, ...), condition=%wide.region_2.3_spmd.clone.clone, body=%wide.region_0.2_spmd.clone.clone.sunk | while | flops 204996608 | bytes 29099832 | solution.py:118
  216.7 3.4 reshape.141
  308.5 3.4 reshape.141
  354.8 3.4 reshape.141
  378.0 3.4 reshape.141
  424.4 3.4 reshape.141
  451.4 20.6 %collective-permute-done.3 = f32[128,1280]{1,0:T(8,128)S(1)} collective-permute-done((f32[128,1280]{1,0:T(8,128)S(1)}, f32[128,1280]{1,0:T(8,128)S(1)}, u32[]{:S(2)}, u32[]{:S(2)}) %collective-permute-start.3) | collective-permute-done | bytes 655392 | tf_op jit(solution)/shard_map/ppermute | solution.py:16
  474.0 59.3 %collective-permute-done.4 = f32[128,1280]{1,0:T(8,128)S(1)} collective-permute-done((f32[128,1280]{1,0:T(8,128)S(1)}, f32[128,1280]{1,0:T(8,128)S(1)}, u32[]{:S(2)}, u32[]{:S(2)}) %collective-permute-start.4) | collective-permute-done | bytes 655392 | tf_op jit(solution)/shard_map/ppermute | solution.py:16
  533.4 5.5 collective-permute-start.5
  541.0 26.5 %collective-permute-done.5 = f32[128,1280]{1,0:T(8,128)S(1)} collective-permute-done((f32[128,1280]{1,0:T(8,128)S(1)}, f32[128,1280]{1,0:T(8,128)S(1)}, u32[]{:S(2)}, u32[]{:S(2)}) %collective-permute-start.5) | collective-permute-done | bytes 655392 | tf_op jit(solution)/shard_map/ppermute | solution.py:16
  567.5 26.9 %collective-permute-done.11 = f32[1,128,1280]{2,1,0:T(8,128)S(1)} collective-permute-done((f32[1,128,1280]{2,1,0:T(8,128)S(1)}, f32[1,128,1280]{2,1,0:T(8,128)S(1)}, u32[]{:S(2)}, u32[]{:S(2)}) %collective-permute-start.11) | collective-permute-done | bytes 655392 | tf_op jit(solution)/shard_map/ppermute | solution.py:16
  597.4 5.7 copy.73
  603.1 13.7 %convert_bitcast_fusion = bf16[8,128,1280]{1,0,2:T(8,128)(2,1)} fusion(f32[6,128,1280]{1,0,2:T(8,128)} %copy.73, f32[8,6,1280]{0,1,2:T(8,128)} %bitcast.109), kind=kOutput, calls=%fused_computation.17 | convolution fusion | flops 95682560 | bytes 6799360 | tf_op jit(solution)/shard_map/clj,lij->cij/dot_general | solution.py:70
  616.8 3.8 copy.75
  632.4 70.8 %all-reduce.2.cloned.1.call-done = f32[512,128]{1,0:T(8,128)} async-done(((f32[512,128]{1,0:T(8,128)}), f32[512,128]{1,0:T(8,128)}) %all-reduce.2.cloned.1.call-update) | async-done | bytes 262160 | tf_op jit(solution)/shard_map/psum | solution.py:135
  (274 shorter events, 270.9 us)
Async XLA Ops:
  7.2 696.1 %all-reduce.2.cloned.1.call-start = ((), (), s32[]{:S(2)}) async-start(), calls=%async_computation | async-start | bytes 524288 | tf_op jit(solution)/shard_map/psum | solution.py:135
  12.6 6.3 copy-start.16
  12.6 6.6 copy-start.17
  19.6 4.4 copy-start.4
  19.9 2.7 copy-start.2
  40.0 9.9 %collective-permute-start.6 = (f32[6,128,1280]{2,1,0:T(8,128)}, f32[6,128,1280]{2,1,0:T(8,128)S(1)}, u32[]{:S(2)}, u32[]{:S(2)}) collective-permute-start(f32[6,128,1280]{2,1,0:T(8,128)} %bitcast.116), channel_id=1, source_target_pairs={{0,4},{4,0},{8,12},{12,8},{16,20},{20,16},{24,28},{28,24},{32,36},... | collective-permute-start | bytes 11796488 | tf_op jit(solution)/shard_map/ppermute | solution.py:16
  49.9 3.8 copy-start.10
  53.7 75.8 %copy-start.7 = (bf16[512,1280]{1,0:T(8,128)(2,1)S(1)}, bf16[512,1280]{1,0:T(8,128)(2,1)}, u32[]{:S(2)}) copy-start(bf16[512,1280]{1,0:T(8,128)(2,1)} %param.8) | copy-start | bytes 3932164
  53.7 72.2 %collective-permute-start.7 = (f32[5,128,1280]{2,1,0:T(8,128)S(1)}, f32[5,128,1280]{2,1,0:T(8,128)S(1)}, u32[]{:S(2)}, u32[]{:S(2)}) collective-permute-start(f32[5,128,1280]{2,1,0:T(8,128)S(1)} %slice_add_fusion), channel_id=1, source_target_pairs={{0,8},{4,12},{8,0},{12,4},{16,24},{20,28},{24,16},{28,20},{32,40},... | collective-permute-start | bytes 9830408 | tf_op jit(solution)/shard_map/ppermute | solution.py:16
  128.4 75.2 %collective-permute-start.8 = (f32[4,128,1280]{2,1,0:T(8,128)}, f32[4,128,1280]{2,1,0:T(8,128)}, u32[]{:S(2)}, u32[]{:S(2)}) collective-permute-start(f32[4,128,1280]{2,1,0:T(8,128)} %slice_add_fusion.1), channel_id=1, source_target_pairs={{0,16},{4,20},{8,24},{12,28},{16,0},{20,4},{24,8},{28,12},{32,48},... | collective-permute-start | bytes 7864328 | tf_op jit(solution)/shard_map/ppermute | solution.py:16
  129.8 3.3 collective-permute-start
  134.0 65.7 %collective-permute-start.1 = (f32[128,1280]{1,0:T(8,128)S(1)}, f32[128,1280]{1,0:T(8,128)S(1)}, u32[]{:S(2)}, u32[]{:S(2)}) collective-permute-start(f32[128,1280]{1,0:T(8,128)S(1)} %add.163), channel_id=1, source_target_pairs={{0,8},{4,12},{8,0},{12,4},{16,24},{20,28},{24,16},{28,20},{32,40},... | collective-permute-start | bytes 1966088 | tf_op jit(solution)/shard_map/ppermute | solution.py:16
  199.7 7.6 %copy-start.12 = (f32[128,1280]{1,0:T(8,128)}, f32[128,1280]{1,0:T(8,128)S(1)}, u32[]{:S(2)}) copy-start(f32[128,1280]{1,0:T(8,128)S(1)} %collective-permute-done.1) | copy-start | bytes 1966084
  200.7 243.3 %collective-permute-start.2 = (f32[128,1280]{1,0:T(8,128)}, f32[128,1280]{1,0:T(8,128)}, u32[]{:S(2)}, u32[]{:S(2)}) collective-permute-start(f32[128,1280]{1,0:T(8,128)} %add.164), channel_id=1, source_target_pairs={{0,16},{4,20},{8,24},{12,28},{16,0},{20,4},{24,8},{28,12},{32,48},... | collective-permute-start | bytes 1966088 | tf_op jit(solution)/shard_map/ppermute | solution.py:16
  207.3 239.2 %collective-permute-start.9 = (f32[3,128,1280]{2,1,0:T(8,128)}, f32[3,128,1280]{2,1,0:T(8,128)}, u32[]{:S(2)}, u32[]{:S(2)}) collective-permute-start(f32[3,128,1280]{2,1,0:T(8,128)} %slice_add_fusion.2), channel_id=1, source_target_pairs={{0,32},{4,36},{8,40},{12,44},{16,48},{20,52},{24,56},{28,60},{32,0... | collective-permute-start | bytes 5898248 | tf_op jit(solution)/shard_map/ppermute | solution.py:16
  444.0 6.5 copy-start.15
  445.4 26.6 %collective-permute-start.3 = (f32[128,1280]{1,0:T(8,128)S(1)}, f32[128,1280]{1,0:T(8,128)S(1)}, u32[]{:S(2)}, u32[]{:S(2)}) collective-permute-start(f32[128,1280]{1,0:T(8,128)S(1)} %add.165), channel_id=1, source_target_pairs={{0,32},{4,36},{8,40},{12,44},{16,48},{20,52},{24,56},{28,60},{32,0... | collective-permute-start | bytes 1966088 | tf_op jit(solution)/shard_map/ppermute | solution.py:16
  448.4 23.8 %copy-start.13 = (f32[128,1280]{1,0:T(8,128)S(1)}, f32[128,1280]{1,0:T(8,128)}, u32[]{:S(2)}) copy-start(f32[128,1280]{1,0:T(8,128)} %copy-done.12) | copy-start | bytes 1966084
  448.4 90.5 %collective-permute-start.10 = (f32[2,128,1280]{2,1,0:T(8,128)S(1)}, f32[2,128,1280]{2,1,0:T(8,128)S(1)}, u32[]{:S(2)}, u32[]{:S(2)}) collective-permute-start(f32[2,128,1280]{2,1,0:T(8,128)S(1)} %slice_add_fusion.3), channel_id=1, source_target_pairs={{0,64},{4,68},{8,72},{12,76},{16,80},{20,84},{24,88},{28,92},{32,9... | collective-permute-start | bytes 3932168 | tf_op jit(solution)/shard_map/ppermute | solution.py:16
  472.0 61.3 %collective-permute-start.4 = (f32[128,1280]{1,0:T(8,128)S(1)}, f32[128,1280]{1,0:T(8,128)S(1)}, u32[]{:S(2)}, u32[]{:S(2)}) collective-permute-start(f32[128,1280]{1,0:T(8,128)S(1)} %add.166), channel_id=1, source_target_pairs={{0,64},{4,68},{8,72},{12,76},{16,80},{20,84},{24,88},{28,92},{32,9... | collective-permute-start | bytes 1966088 | tf_op jit(solution)/shard_map/ppermute | solution.py:16
  533.4 34.1 %collective-permute-start.5 = (f32[128,1280]{1,0:T(8,128)S(1)}, f32[128,1280]{1,0:T(8,128)S(1)}, u32[]{:S(2)}, u32[]{:S(2)}) collective-permute-start(f32[128,1280]{1,0:T(8,128)S(1)} %add.167), channel_id=1, source_target_pairs={{0,128},{4,132},{8,136},{12,140},{16,144},{20,148},{24,152},{28,15... | collective-permute-start | bytes 1966088 | tf_op jit(solution)/shard_map/ppermute | solution.py:16
  538.9 55.5 %collective-permute-start.11 = (f32[1,128,1280]{2,1,0:T(8,128)S(1)}, f32[1,128,1280]{2,1,0:T(8,128)S(1)}, u32[]{:S(2)}, u32[]{:S(2)}) collective-permute-start(f32[1,128,1280]{2,1,0:T(8,128)S(1)} %slice_add_fusion.4), channel_id=1, source_target_pairs={{0,128},{4,132},{8,136},{12,140},{16,144},{20,148},{24,152},{28,15... | collective-permute-start | bytes 1966088 | tf_op jit(solution)/shard_map/ppermute | solution.py:16
  622.9 3.0 copy-start.9
  627.2 3.2 copy-start.6
  (25 other events, 51.0 us)
Sparse Core Ops, SparseCore 0:
  627.3 75.9 all-reduce.1
where the time goes:
time: 717 us; the launch traced here: 712 us
  waiting for transfers between devices  348 us (49%)
  local copies, waits for them, and re-layouts  184 us (26%)
  matrix products  80 us (11%)
  other arithmetic  66.8 us (9%)
  starting transfers between devices  18.8 us (3%)
  between operations  14.3 us (2%)
    ppermute x12, waiting for transfers between devices, partner_2(): return lax.ppermute(value, axis, pairs)  277 us
    psum x1, waiting for transfers between devices, local(): grad_qk = lax.psum(head_part, 'head')  70.8 us
    dynamic_update_slice x20, local copies, waits for them, and re-layouts, head_pair(): lax.dynamic_update_slice_in_dim(inner_out, part_out, col_start, 1)  35 us
    reshape x10, local copies, waits for them, and re-layouts, head_pair(): weight = jnp.broadcast_to(pair_weight[:, :, None, :, None], (2, span_coun...  34.2 us
    dynamic_slice x20, local copies, waits for them, and re-layouts, head_pair(): lax.dynamic_slice_in_dim(cotangent, col_start, pair_cols, 1)  32.4 us
    broadcast_in_dim x10, local copies, waits for them, and re-layouts, head_pair(): jnp.broadcast_to(pair_weight[:, :, None, :, None], (2, span_count, CH, sp...  24 us
    add x10, other arithmetic, head_pair(): d_score = d_score + jnp.sum(jnp.where(causal, weight * d_mix, 0.0), axis=0)  23.9 us
    ppermute x12, starting transfers between devices, partner_2(): return lax.ppermute(value, axis, pairs)  18.7 us
  transfers between devices with their start and end apart: 13, of which 9 were waited for; matrix products, arithmetic and copies ran while one was open for 36% of the time, Pallas kernels for 0%

commit v1 on v0

v1 whole, which is shorter than its diff:
```python
import jax
import jax.numpy as jnp
from jax import lax
from jax.experimental import pallas as pl
from jax.experimental.pallas import tpu as pltpu
from jax.sharding import PartitionSpec as P

HEAD_DIM = 64
CH = 64
TOK = 512
STATE = 128
COLS = 1280
HEADS = COLS // HEAD_DIM
BLK = 256
STEPS = COLS // BLK
SPANS = TOK // CH
USED = 10
TILE = 256
BF = jnp.bfloat16
F32 = jnp.float32
ROW, CORE, XMASK, ZLOW = 8, 1, 3, 1

LOCAL = ((0, 0, 0), (0, 0, 1), (0, 0, 2), (1, 1, 0), (1, 1, 1), (1, 1, 2), (1, 0, 3))


def send(value, mask, axis="seq"):
    pairs = [(source, source ^ mask) for source in range(lax.axis_size(axis))]
    return lax.ppermute(value, axis, pairs)


def dot(a, b, over_a, over_b):
    return lax.dot_general(a, b, (((over_a,), (over_b,)), ((), ())), preferred_element_type=F32)


def coords():
    position = lax.axis_index("seq")
    return position, position & CORE, (position >> 1) & XMASK, (position >> 3) & ZLOW


def params():
    return pltpu.CompilerParams(
        dimension_semantics=("arbitrary",), vmem_limit_bytes=48 * 1024 * 1024
    )


def cols(*lead):
    rank = len(lead)
    return pl.BlockSpec(lead + (BLK,), lambda j: (0,) * rank + (j,))


def whole(*shape):
    return pl.BlockSpec(shape, lambda j: (0,) * len(shape))


def cost(macs, moved):
    return pl.CostEstimate(flops=2 * macs, bytes_accessed=moved, transcendentals=0)


def write_scaled(z_ref, index, w_ref, level, e_ref):
    for a in range(SPANS):
        rows = slice(a * CH, (a + 1) * CH)
        z_ref[index, rows, :] = (w_ref[level, a : a + 1, :] * e_ref[rows, :].astype(F32)).astype(BF)


def level_operand(z_ref, index, k, position, w_ref, v_ref, e_ref):
    upper = (position >> (k - 1)) & 1

    @pl.when(upper == 1)
    def _():
        write_scaled(z_ref, index, w_ref, k + 3, e_ref)

    @pl.when(upper == 0)
    def _():
        z_ref[index] = v_ref[...]


def far_kernel(code_ref, gain_ref, q_ref, v_ref, e_ref, w_ref, z_ref, own_ref, oth_ref, qt, lw, res):
    position, core, x, z0 = coords()
    step = pl.program_id(0)

    @pl.when(step == 0)
    def _():
        qt[...] = q_ref[...].T
        lw[...] = jnp.zeros_like(lw)
        for a in range(SPANS):
            lw[0:15, a, 0:HEADS] = gain_ref[code_ref[a]]

    weights = lw[...].reshape(16 * SPANS, 128)
    head = lax.broadcasted_iota(jnp.int32, (128, BLK), 0)
    col = lax.broadcasted_iota(jnp.int32, (128, BLK), 1) + step * BLK
    spread = (head == col // HEAD_DIM).astype(BF)
    high = weights.astype(BF)
    rest = weights - high.astype(F32)
    middle = rest.astype(BF)
    low = (rest - middle.astype(F32)).astype(BF)
    wide = dot(high, spread, 1, 0) + (dot(middle, spread, 1, 0) + dot(low, spread, 1, 0))
    w_ref[...] = wide.reshape(16, SPANS, BLK)[:USED]
    for index, k in enumerate((4, 5, 6)):
        level_operand(z_ref, index, k, position, w_ref, v_ref, e_ref)
        res[...] = dot(qt[...], z_ref[index], 1, 0).reshape(16, ROW, BLK)
        for xr in range(4):
            for zr in range(2):
                slot = 4 + zr if k == 4 else 2 * zr + (k - 5)
                place = ((xr ^ x) << 1) | (zr if k == 4 else zr ^ z0)
                own_ref[xr, slot] = res[(core << 3) | place]
                oth_ref[xr, slot] = res[((core ^ 1) << 3) | place]


def far_states(code, gain, q, v, e):
    return pl.pallas_call(
        far_kernel,
        grid=(STEPS,),
        in_specs=[
            pl.BlockSpec(memory_space=pltpu.SMEM),
            whole(16, 15, HEADS),
            whole(TOK, STATE),
            cols(TOK),
            cols(TOK),
        ],
        out_specs=[cols(USED, SPANS), cols(3, TOK), cols(4, 6, ROW), cols(4, 6, ROW)],
        out_shape=[
            jax.ShapeDtypeStruct((USED, SPANS, COLS), F32),
            jax.ShapeDtypeStruct((3, TOK, COLS), BF),
            jax.ShapeDtypeStruct((4, 6, ROW, COLS), F32),
            jax.ShapeDtypeStruct((4, 6, ROW, COLS), F32),
        ],
        scratch_shapes=[
            pltpu.VMEM((STATE, TOK), BF),
            pltpu.VMEM((16, SPANS, 128), F32),
            pltpu.VMEM((16, ROW, BLK), F32),
        ],
        compiler_params=params(),
        cost_estimate=cost(3 * TOK * STATE * COLS, 9 << 20),
        name="far_states",
    )(code, gain, q, v, e)


def near_kernel(q_ref, v_ref, e_ref, w_ref, z_ref, x_ref, own_ref, oth_ref, qt, res):
    position, core, x, z0 = coords()

    @pl.when(pl.program_id(0) == 0)
    def _():
        qt[...] = q_ref[...].T

    for index, k in enumerate((2, 3, 1)):
        level_operand(z_ref, index, k, position, w_ref, v_ref, e_ref)
        if k == 1:
            x_ref[...] = dot(qt[...], z_ref[index], 1, 0)
        else:
            res[...] = dot(qt[...], z_ref[index], 1, 0).reshape(2, STATE // 2, BLK)
            own_ref[k - 2] = res[core]
            oth_ref[k - 2] = res[core ^ 1]


def near_states(q, v, e, w):
    half = STATE // 2
    return pl.pallas_call(
        near_kernel,
        grid=(STEPS,),
        in_specs=[whole(TOK, STATE), cols(TOK), cols(TOK), cols(USED, SPANS)],
        out_specs=[cols(3, TOK), cols(STATE), cols(2, half), cols(2, half)],
        out_shape=[
            jax.ShapeDtypeStruct((3, TOK, COLS), BF),
            jax.ShapeDtypeStruct((STATE, COLS), F32),
            jax.ShapeDtypeStruct((2, half, COLS), F32),
            jax.ShapeDtypeStruct((2, half, COLS), F32),
        ],
        scratch_shapes=[pltpu.VMEM((STATE, TOK), BF), pltpu.VMEM((2, half, BLK), F32)],
        compiler_params=params(),
        cost_estimate=cost(3 * TOK * STATE * COLS, 9 << 20),
        name="near_states",
    )(q, v, e, w)


def kept(level, flip):
    rows = lax.broadcasted_iota(jnp.int32, (TILE, TILE), 1 if flip else 0)
    keys = lax.broadcasted_iota(jnp.int32, (TILE, TILE), 0 if flip else 1)
    a, b = rows // CH, keys // CH
    if level == 0:
        return (a == b) & (keys <= rows)
    return ((a ^ b) >> (level - 1) == 1) & (a > b)


def local_kernel(q_ref, v_ref, e_ref, w_ref, m_ref, d_ref, dq_ref, score, flipped, grad, z):
    step = pl.program_id(0)

    @pl.when(step == 0)
    def _():
        grad[...] = jnp.zeros_like(grad)
        for index, (t, s, level) in enumerate(LOCAL):
            qt_rows = q_ref[t * TILE : (t + 1) * TILE, :]
            qs_rows = q_ref[s * TILE : (s + 1) * TILE, :]
            direct = dot(qt_rows, qs_rows, 1, 1)
            swapped = dot(qs_rows, qt_rows, 1, 1)
            if level < 3:
                direct = jnp.where(kept(level, False), direct, 0.0)
                swapped = jnp.where(kept(level, True), swapped, 0.0)
            score[index] = direct.astype(BF)
            flipped[index] = swapped.astype(BF)

    mixed = [None, None]
    d_val = [None, None]
    per = TILE // CH
    for index, (t, s, level) in enumerate(LOCAL):
        vals = v_ref[s * TILE : (s + 1) * TILE, :]
        for a in range(per):
            rows = slice(t * TILE + a * CH, t * TILE + (a + 1) * CH)
            w_row = w_ref[level, t * per + a : t * per + a + 1, :]
            z[index, a * CH : (a + 1) * CH, :] = (w_row * e_ref[rows, :].astype(F32)).astype(BF)
        out = dot(score[index], vals, 1, 0)
        w_rows = jnp.concatenate(
            [
                jnp.broadcast_to(w_ref[level, t * per + a : t * per + a + 1, :], (CH, BLK))
                for a in range(per)
            ],
            axis=0,
        )
        out = w_rows * out
        back = dot(flipped[index], z[index], 1, 0)
        mixed[t] = out if mixed[t] is None else mixed[t] + out
        d_val[s] = back if d_val[s] is None else d_val[s] + back
        grad[index] += dot(z[index], vals, 1, 1)
    for i in range(2):
        m_ref[i * TILE : (i + 1) * TILE, :] = mixed[i]
        d_ref[i * TILE : (i + 1) * TILE, :] = d_val[i]

    @pl.when(step == STEPS - 1)
    def _():
        q = [q_ref[i * TILE : (i + 1) * TILE, :] for i in range(2)]
        cross = grad[6].astype(BF)
        extra = [dot(cross, q[1], 0, 0), dot(cross, q[0], 1, 0)]
        for i in range(2):
            total = jnp.zeros((TILE, TILE), F32)
            for level in range(3):
                total = total + jnp.where(kept(level, False), grad[3 * i + level], 0.0)
            total = total.astype(BF)
            part = dot(total, q[i], 1, 0) + dot(total, q[i], 0, 0)
            dq_ref[i * TILE : (i + 1) * TILE, :] = part + extra[i]


def local_part(q, v, e, w):
    return pl.pallas_call(
        local_kernel,
        grid=(STEPS,),
        in_specs=[whole(TOK, STATE), cols(TOK), cols(TOK), cols(USED, SPANS)],
        out_specs=[cols(TOK), cols(TOK), whole(TOK, STATE)],
        out_shape=[
            jax.ShapeDtypeStruct((TOK, COLS), F32),
            jax.ShapeDtypeStruct((TOK, COLS), F32),
            jax.ShapeDtypeStruct((TOK, STATE), F32),
        ],
        scratch_shapes=[
            pltpu.VMEM((7, TILE, TILE), BF),
            pltpu.VMEM((7, TILE, TILE), BF),
            pltpu.VMEM((7, TILE, TILE), F32),
            pltpu.VMEM((7, TILE, BLK), BF),
        ],
        compiler_params=params(),
        cost_estimate=cost(21 * TILE * TILE * COLS, 9 << 20),
        name="local_part",
    )(q, v, e, w)


def add_outer(q_ref, w_ref, k, position, state, m_ref, d_ref, first, m_in, d_in):
    upper = (position >> (k - 1)) & 1
    out = dot(q_ref[...], state, 1, 0)
    to_value = (1 - upper).astype(F32)
    to_mixed = upper.astype(F32)
    for a in range(SPANS):
        rows = slice(a * CH, (a + 1) * CH)
        w_row = w_ref[k + 3, a : a + 1, :] * to_mixed
        m_old = m_in[rows, :] if first else m_ref[rows, :]
        d_old = d_in[rows, :] if first else d_ref[rows, :]
        m_ref[rows, :] = m_old + w_row * out[rows, :]
        d_ref[rows, :] = d_old + to_value * out[rows, :]


def mid_kernel(*refs):
    (q_ref, w_ref, m_in, d_in, dq_in, zn_ref, zf_ref, y1_ref, y23_ref, y23o_ref, y4_ref, y4o_ref) = refs[:12]
    m_ref, d_ref, dq_ref, y = refs[12:]
    position, core, x, z0 = coords()
    step = pl.program_id(0)

    @pl.when(step == 0)
    def _():
        dq_ref[...] = dq_in[...]

    for index, k in enumerate((2, 3)):
        y[index, core] = y23_ref[index]
        y[index, core ^ 1] = y23o_ref[index]
    for xr in range(4):
        part = (x ^ xr) * 16
        rows = pl.ds(pl.multiple_of(part, 16), 16)
        y[2, core, rows, :] = y4_ref[xr].reshape(16, BLK)
        y[2, core ^ 1, rows, :] = y4o_ref[xr].reshape(16, BLK)
    grads = None
    for index, k in enumerate((2, 3, 4, 1)):
        state = (y1_ref[...] if k == 1 else y[index].reshape(STATE, BLK)).astype(BF)
        z = zf_ref[0] if k == 4 else zn_ref[2 if k == 1 else index]
        add_outer(q_ref, w_ref, k, position, state, m_ref, d_ref, index == 0, m_in, d_in)
        part = dot(z, state, 1, 1)
        grads = part if grads is None else grads + part
    dq_ref[...] += grads


def mid_part(q, w, m, d, dq, zn, zf, y1, y23, y23o, y4, y4o):
    half = STATE // 2
    return pl.pallas_call(
        mid_kernel,
        grid=(STEPS,),
        in_specs=[
            whole(TOK, STATE),
            cols(USED, SPANS),
            cols(TOK),
            cols(TOK),
            whole(TOK, STATE),
            cols(3, TOK),
            cols(1, TOK),
            cols(STATE),
            cols(2, half),
            cols(2, half),
            cols(4, 2, ROW),
            cols(4, 2, ROW),
        ],
        out_specs=[cols(TOK), cols(TOK), whole(TOK, STATE)],
        out_shape=[
            jax.ShapeDtypeStruct((TOK, COLS), F32),
            jax.ShapeDtypeStruct((TOK, COLS), F32),
            jax.ShapeDtypeStruct((TOK, STATE), F32),
        ],
        scratch_shapes=[pltpu.VMEM((3, 2, half, BLK), F32)],
        compiler_params=params(),
        cost_estimate=cost(8 * TOK * STATE * COLS, 18 << 20),
        name="mid_part",
    )(q, w, m, d, dq, zn, zf, y1, y23, y23o, y4, y4o)


def gather_far(y, refs):
    position, core, x, z0 = coords()
    for cr in range(2):
        for xr in range(4):
            for zr in range(2):
                place = ((cr ^ core) << 3) | ((xr ^ x) << 1) | (zr ^ z0)
                for index in range(2):
                    y[index, place] = refs[4 * cr + xr][2 * zr + index]


def score_kernel(*refs):
    dq_in, z_ref = refs[:2]
    dq_ref, y = refs[10:]

    @pl.when(pl.program_id(0) == 0)
    def _():
        dq_ref[...] = dq_in[...]

    gather_far(y, refs[2:10])
    grads = None
    for index in range(2):
        state = y[index].reshape(STATE, BLK).astype(BF)
        part = dot(z_ref[1 + index], state, 1, 1)
        grads = part if grads is None else grads + part
    dq_ref[...] += grads


def score_part(dq, zf, pieces):
    return pl.pallas_call(
        score_kernel,
        grid=(STEPS,),
        in_specs=[whole(TOK, STATE), cols(3, TOK)] + [cols(4, ROW)] * 8,
        out_specs=whole(TOK, STATE),
        out_shape=jax.ShapeDtypeStruct((TOK, STATE), F32),
        scratch_shapes=[pltpu.VMEM((2, 16, ROW, BLK), F32)],
        compiler_params=params(),
        cost_estimate=cost(2 * TOK * STATE * COLS, 5 << 20),
        name="score_part",
    )(dq, zf, *pieces)


def last_kernel(*refs):
    q_ref, w_ref, m_in, d_in = refs[:4]
    mixed_ref, dv_ref, m_ref, d_ref, y = refs[12:]
    position, core, x, z0 = coords()
    gather_far(y, refs[4:12])
    for index, k in enumerate((5, 6)):
        state = y[index].reshape(STATE, BLK).astype(BF)
        add_outer(q_ref, w_ref, k, position, state, m_ref, d_ref, index == 0, m_in, d_in)
    mixed_ref[...] = m_ref[...].astype(BF)
    dv_ref[...] = d_ref[...].astype(BF)


def last_part(q, w, m, d, pieces):
    return pl.pallas_call(
        last_kernel,
        grid=(STEPS,),
        in_specs=[whole(TOK, STATE), cols(USED, SPANS), cols(TOK), cols(TOK)] + [cols(4, ROW)] * 8,
        out_specs=[cols(TOK), cols(TOK)],
        out_shape=[
            jax.ShapeDtypeStruct((TOK, COLS), BF),
            jax.ShapeDtypeStruct((TOK, COLS), BF),
        ],
        scratch_shapes=[
            pltpu.VMEM((TOK, BLK), F32),
            pltpu.VMEM((TOK, BLK), F32),
            pltpu.VMEM((2, 16, ROW, BLK), F32),
        ],
        compiler_params=params(),
        cost_estimate=cost(2 * TOK * STATE * COLS, 10 << 20),
        name="last_part",
    )(q, w, m, d, *pieces)


def local(q, v, e, gain, code):
    w, zf, own_f, oth_f = far_states(code, gain, q, v, e)
    got_f = send(oth_f, 1)
    zn, x1, own_n, oth_n = near_states(q, v, e, w)
    got_n = send(oth_n, 1)
    y1 = send(x1, 1)

    chip = [own_f[j] + got_f[j] for j in range(4)]
    slices = [send(chip[j], 2 * j) for j in (1, 2, 3)]
    m, d, dq = local_part(q, v, e, w)
    near = [own_n[i] + got_n[i] for i in range(2)]
    piece = chip[0] + slices[0] + slices[1] + slices[2]
    piece, near = lax.optimization_barrier((piece, near))

    low = send(piece[2:6], 8)
    y2 = send(near[0], 2)
    y3 = send(near[1], 4) + send(near[1], 6)
    y4 = low[2:4]
    five = piece[0] + low[0]
    six = piece[1] + low[1]
    y5 = send(five, 16)
    y6 = send(six, 32) + send(six, 48)
    y4s = jnp.stack([y4] + [send(y4, 2 * j) for j in (1, 2, 3)])
    y4o = send(y4s, 1)
    y23 = jnp.stack([y2, y3])
    y23o = send(y23, 1)

    half = jnp.stack([y5, y6])
    quad = jnp.concatenate([half, send(half, 8)])
    pieces = [quad] + [send(quad, 2 * j) for j in (1, 2, 3)]
    pieces = pieces + [send(p, 1) for p in pieces]
    m, d, dq = mid_part(q, w, m, d, dq, zn, zf, y1, y23, y23o, y4s, y4o)
    dq = score_part(dq, zf, pieces)
    parts = [dq] + [send(dq, h, "head") for h in (1, 2, 3)]
    mixed, grad_values = last_part(q, w, m, d, pieces)
    grad_qk = (parts[0] + parts[1]) + (parts[2] + parts[3])
    return mixed, grad_qk, grad_values


def solution(mesh):
    placed = (P("seq", None), P("seq", "head"), P("seq", "head"), P(None, None, "head"), P("seq"))
    return jax.shard_map(
        local,
        mesh=mesh,
        in_specs=placed,
        out_specs=(P("seq", "head"), P("seq", None), P("seq", "head")),
        check_vma=False,
    )
```

time: 717 us -> 123 us (0.17)
  waiting for transfers between devices: 348 us -> 35.5 us
  local copies, waits for them, and re-layouts: 184 us -> 6.67 us
  matrix products: 80 us -> 0 us
  other arithmetic: 66.8 us -> 1.17 us
  Pallas kernels: 0 us -> 36.5 us
  starting transfers between devices: 18.8 us -> 42.4 us
  between operations: 14.3 us -> 0.77 us
    ppermute x12 -> x29, waiting for transfers between devices: 277 us -> 35.5 us  [send(): return lax.ppermute(value, axis, pairs)]
    dot_general x43 -> x0, matrix products: 80 us -> none  [the longest x10 17 us: head_pair(): jnp.einsum('tgp,sgp->gts', cot_pair, val_pair, preferred_element_type=jnp...]
    psum x1 -> x0, waiting for transfers between devices: 70.8 us -> none  [local(): grad_qk = lax.psum(head_part, 'head')]
    dynamic_slice x40 -> x0, local copies, waits for them, and re-layouts: 47.1 us -> none  [the longest x20 32.4 us: head_pair(): lax.dynamic_slice_in_dim(cotangent, col_start, pair_cols, 1)]
    dynamic_update_slice x30 -> x0, local copies, waits for them, and re-layouts: 42.4 us -> none  [the longest x20 35 us: head_pair(): lax.dynamic_update_slice_in_dim(inner_out, part_out, col_start, 1)]
    add x21 -> x5, other arithmetic: 38.3 us -> 1.03 us  [the longest x1 0.76 us: local(): grad_qk = parts[0] + parts[1] + (parts[2] + parts[3])]
    pallas_call x0 -> x6, Pallas kernels: none -> 36.5 us  [the longest x1 9.62 us: mid_part(): pl.pallas_call(mid_kernel, grid=(STEPS,), in_specs=[whole(TOK, STATE), co...]
    reshape x11 -> x0, local copies, waits for them, and re-layouts: 34.3 us -> none  [the longest x10 34.2 us: head_pair(): weight = jnp.broadcast_to(pair_weight[:, :, None, :, None], (2, span_coun...]
  transfers between devices with their start and end apart: 13 -> 29, of which waited for: 9 -> 11; matrix products, arithmetic and copies ran while one was open for 36% -> 0% of each run, Pallas kernels for 0% -> 22%
where the time goes in v1:
time: 123 us
  starting transfers between devices  42.4 us (34%)
  Pallas kernels  36.5 us (30%)
  waiting for transfers between devices  35.5 us (29%)
  local copies, waits for them, and re-layouts  6.67 us (5%)
    ppermute x29, starting transfers between devices, send(): return lax.ppermute(value, axis, pairs)  42.4 us
    ppermute x29, waiting for transfers between devices, send(): return lax.ppermute(value, axis, pairs)  35.5 us
    pallas_call x1, Pallas kernels, mid_part(): pl.pallas_call(mid_kernel, grid=(STEPS,), in_specs=[whole(TOK, STATE), co...  9.62 us
    pallas_call x1, Pallas kernels, far_states(): pl.pallas_call(far_kernel, grid=(STEPS,), in_specs=[pl.BlockSpec(memory_s...  7.06 us
    pallas_call x1, Pallas kernels, local_part(): pl.pallas_call(local_kernel, grid=(STEPS,), in_specs=[whole(TOK, STATE),...  6.91 us
    unnamed x21, local copies, waits for them, and re-layouts  6.65 us
    pallas_call x1, Pallas kernels, last_part(): pl.pallas_call(last_kernel, grid=(STEPS,), in_specs=[whole(TOK, STATE), c...  5.42 us
    pallas_call x1, Pallas kernels, near_states(): pl.pallas_call(near_kernel, grid=(STEPS,), in_specs=[whole(TOK, STATE), c...  5.17 us
  transfers between devices with their start and end apart: 29, of which 11 were waited for; matrix products, arithmetic and copies ran while one was open for 0% of the time, Pallas kernels for 22%

profile of v1, /device:TPU:1, one launch (start us, length us, event | category | flops | bytes accessed | tf_op | source)
XLA Modules:
  0.0 123.0 jit_solution(14057498967347801124)
XLA Ops:
  5.8 7.1 %far_states.1 = (f32[10,8,1280]{2,1,0:T(8,128)S(1)}, bf16[3,512,1280]{2,1,0:T(8,128)(2,1)}, f32[4,6,8,1280]{3,2,1,0:T(8,128)S(1)}, f32[4,6,8,1280]{3,2,1,0:T(8,128)S(1)}) custom-call(s32[8]{0:T(128)S(1)} %copy-done.9, f32[16,15,20]{2,1,0:T(8,128)S(1)} %copy.8.gain_ref, bf16[512,128]{1,0:T(8,128)(2,1)S(1)} %copy-done.7, bf16[512,1280]{1,0:T(8,128)(2,1)S(1)} %copy-done.1, ...), custom_call_target="tpu_custom_call" | custom-call | flops 503316480 | bytes 9437184 | tf_op jit(solution)/shard_map/far_states/pallas_call | solution.py:110
  12.8 3.2 %collective-permute-start.1 = (f32[4,6,8,1280]{3,2,1,0:T(8,128)S(1)}, f32[4,6,8,1280]{3,2,1,0:T(8,128)S(1)}, u32[]{:S(2)}, u32[]{:S(2)}) collective-permute-start(f32[4,6,8,1280]{3,2,1,0:T(8,128)S(1)} %get-tuple-element.30), channel_id=1, source_target_pairs={{0,4},{4,0},{8,12},{12,8},{16,20},{20,16},{24,28},{28,24},{32,36},... | collective-permute-start | bytes 2949128 | tf_op jit(solution)/shard_map/ppermute | solution.py:28
  16.1 5.2 %near_states.1 = (bf16[3,512,1280]{2,1,0:T(8,128)(2,1)}, f32[128,1280]{1,0:T(8,128)S(1)}, f32[2,64,1280]{2,1,0:T(8,128)S(1)}, f32[2,64,1280]{2,1,0:T(8,128)S(1)}) custom-call(bf16[512,128]{1,0:T(8,128)(2,1)S(1)} %copy-done.7, bf16[512,1280]{1,0:T(8,128)(2,1)S(1)} %copy-done.2, bf16[512,1280]{1,0:T(8,128)(2,1)S(1)} %copy-done.4, ...), custom_call_target="tpu_custom_call" | custom-call | flops 503316480 | bytes 9437184 | tf_op jit(solution)/shard_map/near_states/pallas_call | solution.py:157
  22.9 1.8 %collective-permute-start.2 = (f32[6,8,1280]{2,1,0:T(8,128)S(1)}, f32[6,8,1280]{2,1,0:T(8,128)S(1)}, u32[]{:S(2)}, u32[]{:S(2)}) collective-permute-start(f32[6,8,1280]{2,1,0:T(8,128)S(1)} %get-tuple-element.41), channel_id=1, source_target_pairs={{0,8},{4,12},{8,0},{12,4},{16,24},{20,28},{24,16},{28,20},{32,40},... | collective-permute-start | bytes 737288 | tf_op jit(solution)/shard_map/ppermute | solution.py:28
  24.8 10.1 %collective-permute-done.4 = f32[6,8,1280]{2,1,0:T(8,128)S(1)} collective-permute-done((f32[6,8,1280]{2,1,0:T(8,128)S(1)}, f32[6,8,1280]{2,1,0:T(8,128)S(1)}, u32[]{:S(2)}, u32[]{:S(2)}) %collective-permute-start.4) | collective-permute-done | bytes 245792 | tf_op jit(solution)/shard_map/ppermute | solution.py:28
  35.8 2.5 %collective-permute-start.7 = (f32[64,1280]{1,0:T(8,128)S(1)}, f32[64,1280]{1,0:T(8,128)S(1)}, u32[]{:S(2)}, u32[]{:S(2)}) collective-permute-start(f32[64,1280]{1,0:T(8,128)S(1)} %get-tuple-element.34), channel_id=1, source_target_pairs={{0,16},{4,20},{8,24},{12,28},{16,0},{20,4},{24,8},{28,12},{32,48},... | collective-permute-start | bytes 983048 | tf_op jit(solution)/shard_map/ppermute | solution.py:28
  39.7 5.8 %collective-permute-start.16 = (f32[8,1280]{1,0:T(8,128)S(1)}, f32[8,1280]{1,0:T(8,128)S(1)}, u32[]{:S(2)}, u32[]{:S(2)}) collective-permute-start(f32[8,1280]{1,0:T(8,128)S(1)} %get-tuple-element.47), channel_id=1, source_target_pairs={{0,128},{4,132},{8,136},{12,140},{16,144},{20,148},{24,152},{28,15... | collective-permute-start | bytes 122888 | tf_op jit(solution)/shard_map/ppermute | solution.py:28
  45.7 2.3 %collective-permute-start.13 = (f32[2,8,1280]{2,1,0:T(8,128)S(1)}, f32[2,8,1280]{2,1,0:T(8,128)S(1)}, u32[]{:S(2)}, u32[]{:S(2)}) collective-permute-start(f32[2,8,1280]{2,1,0:T(8,128)S(1)} %get-tuple-element.49), channel_id=1, source_target_pairs={{0,24},{4,28},{8,16},{12,20},{16,8},{20,12},{24,0},{28,4},{32,56},... | collective-permute-start | bytes 245768 | tf_op jit(solution)/shard_map/ppermute | solution.py:28
  48.0 1.6 %collective-permute-start.12 = (f32[2,8,1280]{2,1,0:T(8,128)S(1)}, f32[2,8,1280]{2,1,0:T(8,128)S(1)}, u32[]{:S(2)}, u32[]{:S(2)}) collective-permute-start(f32[2,8,1280]{2,1,0:T(8,128)S(1)} %get-tuple-element.49), channel_id=1, source_target_pairs={{0,16},{4,20},{8,24},{12,28},{16,0},{20,4},{24,8},{28,12},{32,48},... | collective-permute-start | bytes 245768 | tf_op jit(solution)/shard_map/ppermute | solution.py:28
  52.0 2.8 %collective-permute-done.15 = f32[8,1280]{1,0:T(8,128)S(1)} collective-permute-done((f32[8,1280]{1,0:T(8,128)S(1)}, f32[8,1280]{1,0:T(8,128)S(1)}, u32[]{:S(2)}, u32[]{:S(2)}) %collective-permute-start.15) | collective-permute-done | bytes 40992 | tf_op jit(solution)/shard_map/ppermute | solution.py:28
  55.3 2.2 %collective-permute-done.13 = f32[2,8,1280]{2,1,0:T(8,128)S(1)} collective-permute-done((f32[2,8,1280]{2,1,0:T(8,128)S(1)}, f32[2,8,1280]{2,1,0:T(8,128)S(1)}, u32[]{:S(2)}, u32[]{:S(2)}) %collective-permute-start.13) | collective-permute-done | bytes 81952 | tf_op jit(solution)/shard_map/ppermute | solution.py:28
  57.5 3.6 %collective-permute-start = (f32[128,1280]{1,0:T(8,128)S(1)}, f32[128,1280]{1,0:T(8,128)S(1)}, u32[]{:S(2)}, u32[]{:S(2)}) collective-permute-start(f32[128,1280]{1,0:T(8,128)S(1)} %get-tuple-element.28), channel_id=1, source_target_pairs={{0,4},{4,0},{8,12},{12,8},{16,20},{20,16},{24,28},{28,24},{32,36},... | collective-permute-start | bytes 1966088 | tf_op jit(solution)/shard_map/ppermute | solution.py:28
  62.6 3.0 %collective-permute-start.14 = (f32[4,2,8,1280]{3,2,1,0:T(8,128)S(1)}, f32[4,2,8,1280]{3,2,1,0:T(8,128)S(1)}, u32[]{:S(2)}, u32[]{:S(2)}) collective-permute-start(f32[4,2,8,1280]{3,2,1,0:T(8,128)S(1)} %pad_maximum_fusion.1.refs_10_), channel_id=1, source_target_pairs={{0,4},{4,0},{8,12},{12,8},{16,20},{20,16},{24,28},{28,24},{32,36},... | collective-permute-start | bytes 983048 | tf_op jit(solution)/shard_map/ppermute | solution.py:28
  65.6 4.8 %collective-permute-done.6 = f32[64,1280]{1,0:T(8,128)S(1)} collective-permute-done((f32[64,1280]{1,0:T(8,128)S(1)}, f32[64,1280]{1,0:T(8,128)S(1)}, u32[]{:S(2)}, u32[]{:S(2)}) %collective-permute-start.6) | collective-permute-done | bytes 327712 | tf_op jit(solution)/shard_map/ppermute | solution.py:28
  72.6 2.4 %collective-permute-start.20 = (f32[4,8,1280]{2,1,0:T(8,128)S(1)}, f32[4,8,1280]{2,1,0:T(8,128)S(1)}, u32[]{:S(2)}, u32[]{:S(2)}) collective-permute-start(f32[4,8,1280]{2,1,0:T(8,128)S(1)} %pad_maximum_fusion.2.refs_4_.refs_2_), channel_id=1, source_target_pairs={{0,16},{4,20},{8,24},{12,28},{16,0},{20,4},{24,8},{28,12},{32,48},... | collective-permute-start | bytes 491528 | tf_op jit(solution)/shard_map/ppermute | solution.py:28
  75.6 1.9 %collective-permute-done.19.refs_5_.refs_3_ = f32[4,8,1280]{2,1,0:T(8,128)S(1)} collective-permute-done((f32[4,8,1280]{2,1,0:T(8,128)S(1)}, f32[4,8,1280]{2,1,0:T(8,128)S(1)}, u32[]{:S(2)}, u32[]{:S(2)}) %collective-permute-start.19) | collective-permute-done | bytes 163872 | tf_op jit(solution)/shard_map/ppermute | solution.py:28
  78.7 4.2 %collective-permute-done.20.refs_6_.refs_4_ = f32[4,8,1280]{2,1,0:T(8,128)S(1)} collective-permute-done((f32[4,8,1280]{2,1,0:T(8,128)S(1)}, f32[4,8,1280]{2,1,0:T(8,128)S(1)}, u32[]{:S(2)}, u32[]{:S(2)}) %collective-permute-start.20) | collective-permute-done | bytes 163872 | tf_op jit(solution)/shard_map/ppermute | solution.py:28
  86.4 6.9 %local_part.1 = (f32[512,1280]{1,0:T(8,128)S(1)}, f32[512,1280]{1,0:T(8,128)}, f32[512,128]{1,0:T(8,128)S(1)}) custom-call(bf16[512,128]{1,0:T(8,128)(2,1)S(1)} %copy-done.8, bf16[512,1280]{1,0:T(8,128)(2,1)S(1)} %copy-done.2, bf16[512,1280]{1,0:T(8,128)(2,1)S(1)} %copy-done.4, f32[10,8,1280]{2,1,0:T(8,128)S(1)} %get-tuple-element.22.w_ref.refs_1_), custom_call_target="tpu_custom_call" | custom-call | flops 3523215360 | bytes 9437184 | tf_op jit(solution)/shard_map/local_part/pallas_call | solution.py:242
  93.3 1.5 %copy-done.6 = f32[512,1280]{1,0:T(8,128)} copy-done((f32[512,1280]{1,0:T(8,128)}, f32[512,1280]{1,0:T(8,128)S(1)}, u32[]{:S(2)}) %copy-start.6) | copy-done | bytes 2621464
  94.8 9.6 %mid_part.1 = (f32[512,1280]{1,0:T(8,128)}, f32[512,1280]{1,0:T(8,128)}, f32[512,128]{1,0:T(8,128)S(1)}) custom-call(bf16[512,128]{1,0:T(8,128)(2,1)S(1)} %copy-done.8, f32[10,8,1280]{2,1,0:T(8,128)S(1)} %get-tuple-element.22.w_ref.refs_1_, f32[512,1280]{1,0:T(8,128)} %copy-done.6, f32[512,1280]{1,0:T(8,128)} %get-tuple-element.24.refs_3_, ...), custom_call_target="tpu_custom_call" | custom-call | flops 1342177280 | bytes 18874368 | tf_op jit(solution)/shard_map/mid_part/pallas_call | solution.py:308
  104.5 2.3 %score_part.1 = f32[512,128]{1,0:T(8,128)S(1)} custom-call(f32[512,128]{1,0:T(8,128)S(1)} %get-tuple-element.39.refs_0_, bf16[3,512,1280]{2,1,0:T(8,128)(2,1)S(1)} %copy-done, f32[4,8,1280]{2,1,0:T(8,128)S(1)} %pad_maximum_fusion.2.refs_4_.refs_2_, f32[4,8,1280]{2,1,0:T(8,128)S(1)} %collective-permute-done.19.refs_5_.refs_3_, ...), custom_call_target="tpu_custom_call" | custom-call | flops 335544320 | bytes 5242880 | tf_op jit(solution)/shard_map/score_part/pallas_call | solution.py:366
  106.8 3.0 %collective-permute-start.27 = (f32[512,128]{1,0:T(8,128)S(1)}, f32[512,128]{1,0:T(8,128)S(1)}, u32[]{:S(2)}, u32[]{:S(2)}) collective-permute-start(f32[512,128]{1,0:T(8,128)S(1)} %score_part.1), channel_id=1, source_target_pairs={{0,2},{1,3},{2,0},{3,1},{4,6},{5,7},{6,4},{7,5},{8,10},{9,11},{10,... | collective-permute-start | bytes 786440 | tf_op jit(solution)/shard_map/ppermute | solution.py:28
  110.6 5.4 %last_part.1 = (bf16[512,1280]{1,0:T(8,128)(2,1)}, bf16[512,1280]{1,0:T(8,128)(2,1)}) custom-call(bf16[512,128]{1,0:T(8,128)(2,1)S(1)} %copy-done.8, f32[10,8,1280]{2,1,0:T(8,128)S(1)} %get-tuple-element.22.w_ref.refs_1_, f32[512,1280]{1,0:T(8,128)S(1)} %copy-done.5, f32[512,1280]{1,0:T(8,128)} %get-tuple-element.37.refs_3_, ...), custom_call_target="tpu_custom_call" | custom-call | flops 335544320 | bytes 10485760 | tf_op jit(solution)/shard_map/last_part/pallas_call | solution.py:392
  116.0 6.2 %collective-permute-done.28 = f32[512,128]{1,0:T(8,128)S(1)} collective-permute-done((f32[512,128]{1,0:T(8,128)S(1)}, f32[512,128]{1,0:T(8,128)S(1)}, u32[]{:S(2)}, u32[]{:S(2)}) %collective-permute-start.28) | collective-permute-done | bytes 262176 | tf_op jit(solution)/shard_map/ppermute | solution.py:28
  (74 shorter events, 22.7 us)
Async XLA Ops:
  12.8 8.4 %collective-permute-start.1 = (f32[4,6,8,1280]{3,2,1,0:T(8,128)S(1)}, f32[4,6,8,1280]{3,2,1,0:T(8,128)S(1)}, u32[]{:S(2)}, u32[]{:S(2)}) collective-permute-start(f32[4,6,8,1280]{3,2,1,0:T(8,128)S(1)} %get-tuple-element.30), channel_id=1, source_target_pairs={{0,4},{4,0},{8,12},{12,8},{16,20},{20,16},{24,28},{28,24},{32,36},... | collective-permute-start | bytes 2949128 | tf_op jit(solution)/shard_map/ppermute | solution.py:28
  21.4 13.6 %collective-permute-start.4 = (f32[6,8,1280]{2,1,0:T(8,128)S(1)}, f32[6,8,1280]{2,1,0:T(8,128)S(1)}, u32[]{:S(2)}, u32[]{:S(2)}) collective-permute-start(f32[6,8,1280]{2,1,0:T(8,128)S(1)} %get-tuple-element.42), channel_id=1, source_target_pairs={{0,24},{4,28},{8,16},{12,20},{16,8},{20,12},{24,0},{28,4},{32,56},... | collective-permute-start | bytes 737288 | tf_op jit(solution)/shard_map/ppermute | solution.py:28
  22.5 12.5 %collective-permute-start.3 = (f32[6,8,1280]{2,1,0:T(8,128)S(1)}, f32[6,8,1280]{2,1,0:T(8,128)S(1)}, u32[]{:S(2)}, u32[]{:S(2)}) collective-permute-start(f32[6,8,1280]{2,1,0:T(8,128)S(1)} %get-tuple-element.43), channel_id=1, source_target_pairs={{0,16},{4,20},{8,24},{12,28},{16,0},{20,4},{24,8},{28,12},{32,48},... | collective-permute-start | bytes 737288 | tf_op jit(solution)/shard_map/ppermute | solution.py:28
  22.9 12.4 %collective-permute-start.2 = (f32[6,8,1280]{2,1,0:T(8,128)S(1)}, f32[6,8,1280]{2,1,0:T(8,128)S(1)}, u32[]{:S(2)}, u32[]{:S(2)}) collective-permute-start(f32[6,8,1280]{2,1,0:T(8,128)S(1)} %get-tuple-element.41), channel_id=1, source_target_pairs={{0,8},{4,12},{8,0},{12,4},{16,24},{20,28},{24,16},{28,20},{32,40},... | collective-permute-start | bytes 737288 | tf_op jit(solution)/shard_map/ppermute | solution.py:28
  35.8 26.8 %collective-permute-start.7 = (f32[64,1280]{1,0:T(8,128)S(1)}, f32[64,1280]{1,0:T(8,128)S(1)}, u32[]{:S(2)}, u32[]{:S(2)}) collective-permute-start(f32[64,1280]{1,0:T(8,128)S(1)} %get-tuple-element.34), channel_id=1, source_target_pairs={{0,16},{4,20},{8,24},{12,28},{16,0},{20,4},{24,8},{28,12},{32,48},... | collective-permute-start | bytes 983048 | tf_op jit(solution)/shard_map/ppermute | solution.py:28
  38.3 27.3 %collective-permute-start.8 = (f32[64,1280]{1,0:T(8,128)S(1)}, f32[64,1280]{1,0:T(8,128)S(1)}, u32[]{:S(2)}, u32[]{:S(2)}) collective-permute-start(f32[64,1280]{1,0:T(8,128)S(1)} %get-tuple-element.34), channel_id=1, source_target_pairs={{0,24},{4,28},{8,16},{12,20},{16,8},{20,12},{24,0},{28,4},{32,56},... | collective-permute-start | bytes 983048 | tf_op jit(solution)/shard_map/ppermute | solution.py:28
  39.7 8.4 %collective-permute-start.16 = (f32[8,1280]{1,0:T(8,128)S(1)}, f32[8,1280]{1,0:T(8,128)S(1)}, u32[]{:S(2)}, u32[]{:S(2)}) collective-permute-start(f32[8,1280]{1,0:T(8,128)S(1)} %get-tuple-element.47), channel_id=1, source_target_pairs={{0,128},{4,132},{8,136},{12,140},{16,144},{20,148},{24,152},{28,15... | collective-permute-start | bytes 122888 | tf_op jit(solution)/shard_map/ppermute | solution.py:28
  45.7 11.8 %collective-permute-start.13 = (f32[2,8,1280]{2,1,0:T(8,128)S(1)}, f32[2,8,1280]{2,1,0:T(8,128)S(1)}, u32[]{:S(2)}, u32[]{:S(2)}) collective-permute-start(f32[2,8,1280]{2,1,0:T(8,128)S(1)} %get-tuple-element.49), channel_id=1, source_target_pairs={{0,24},{4,28},{8,16},{12,20},{16,8},{20,12},{24,0},{28,4},{32,56},... | collective-permute-start | bytes 245768 | tf_op jit(solution)/shard_map/ppermute | solution.py:28
  48.0 13.1 %collective-permute-start.12 = (f32[2,8,1280]{2,1,0:T(8,128)S(1)}, f32[2,8,1280]{2,1,0:T(8,128)S(1)}, u32[]{:S(2)}, u32[]{:S(2)}) collective-permute-start(f32[2,8,1280]{2,1,0:T(8,128)S(1)} %get-tuple-element.49), channel_id=1, source_target_pairs={{0,16},{4,20},{8,24},{12,28},{16,0},{20,4},{24,8},{28,12},{32,48},... | collective-permute-start | bytes 245768 | tf_op jit(solution)/shard_map/ppermute | solution.py:28
  54.8 6.5 %collective-permute-start.11 = (f32[2,8,1280]{2,1,0:T(8,128)S(1)}, f32[2,8,1280]{2,1,0:T(8,128)S(1)}, u32[]{:S(2)}, u32[]{:S(2)}) collective-permute-start(f32[2,8,1280]{2,1,0:T(8,128)S(1)} %get-tuple-element.49), channel_id=1, source_target_pairs={{0,8},{4,12},{8,0},{12,4},{16,24},{20,28},{24,16},{28,20},{32,40},... | collective-permute-start | bytes 245768 | tf_op jit(solution)/shard_map/ppermute | solution.py:28
  57.5 17.5 %collective-permute-start = (f32[128,1280]{1,0:T(8,128)S(1)}, f32[128,1280]{1,0:T(8,128)S(1)}, u32[]{:S(2)}, u32[]{:S(2)}) collective-permute-start(f32[128,1280]{1,0:T(8,128)S(1)} %get-tuple-element.28), channel_id=1, source_target_pairs={{0,4},{4,0},{8,12},{12,8},{16,20},{20,16},{24,28},{28,24},{32,36},... | collective-permute-start | bytes 1966088 | tf_op jit(solution)/shard_map/ppermute | solution.py:28
  61.1 9.3 %collective-permute-start.6 = (f32[64,1280]{1,0:T(8,128)S(1)}, f32[64,1280]{1,0:T(8,128)S(1)}, u32[]{:S(2)}, u32[]{:S(2)}) collective-permute-start(f32[64,1280]{1,0:T(8,128)S(1)} %get-tuple-element.33), channel_id=1, source_target_pairs={{0,8},{4,12},{8,0},{12,4},{16,24},{20,28},{24,16},{28,20},{32,40},... | collective-permute-start | bytes 983048 | tf_op jit(solution)/shard_map/ppermute | solution.py:28
  61.3 10.3 %collective-permute-start.18 = (f32[2,8,1280]{2,1,0:T(8,128)S(1)}, f32[2,8,1280]{2,1,0:T(8,128)S(1)}, u32[]{:S(2)}, u32[]{:S(2)}) collective-permute-start(f32[2,8,1280]{2,1,0:T(8,128)S(1)} %pad_maximum_fusion.3), channel_id=1, source_target_pairs={{0,32},{4,36},{8,40},{12,44},{16,48},{20,52},{24,56},{28,60},{32,0... | collective-permute-start | bytes 245768 | tf_op jit(solution)/shard_map/ppermute | solution.py:28
  62.6 23.8 %collective-permute-start.14 = (f32[4,2,8,1280]{3,2,1,0:T(8,128)S(1)}, f32[4,2,8,1280]{3,2,1,0:T(8,128)S(1)}, u32[]{:S(2)}, u32[]{:S(2)}) collective-permute-start(f32[4,2,8,1280]{3,2,1,0:T(8,128)S(1)} %pad_maximum_fusion.1.refs_10_), channel_id=1, source_target_pairs={{0,4},{4,0},{8,12},{12,8},{16,20},{20,16},{24,28},{28,24},{32,36},... | collective-permute-start | bytes 983048 | tf_op jit(solution)/shard_map/ppermute | solution.py:28
  70.4 24.4 %collective-permute-start.9 = (f32[2,64,1280]{2,1,0:T(8,128)S(1)}, f32[2,64,1280]{2,1,0:T(8,128)S(1)}, u32[]{:S(2)}, u32[]{:S(2)}) collective-permute-start(f32[2,64,1280]{2,1,0:T(8,128)S(1)} %pad_maximum_fusion.refs_8_), channel_id=1, source_target_pairs={{0,4},{4,0},{8,12},{12,8},{16,20},{20,16},{24,28},{28,24},{32,36},... | collective-permute-start | bytes 1966088 | tf_op jit(solution)/shard_map/ppermute | solution.py:28
  72.6 10.3 %collective-permute-start.20 = (f32[4,8,1280]{2,1,0:T(8,128)S(1)}, f32[4,8,1280]{2,1,0:T(8,128)S(1)}, u32[]{:S(2)}, u32[]{:S(2)}) collective-permute-start(f32[4,8,1280]{2,1,0:T(8,128)S(1)} %pad_maximum_fusion.2.refs_4_.refs_2_), channel_id=1, source_target_pairs={{0,16},{4,20},{8,24},{12,28},{16,0},{20,4},{24,8},{28,12},{32,48},... | collective-permute-start | bytes 491528 | tf_op jit(solution)/shard_map/ppermute | solution.py:28
  75.0 10.2 %collective-permute-start.21 = (f32[4,8,1280]{2,1,0:T(8,128)S(1)}, f32[4,8,1280]{2,1,0:T(8,128)S(1)}, u32[]{:S(2)}, u32[]{:S(2)}) collective-permute-start(f32[4,8,1280]{2,1,0:T(8,128)S(1)} %pad_maximum_fusion.2.refs_4_.refs_2_), channel_id=1, source_target_pairs={{0,24},{4,28},{8,16},{12,20},{16,8},{20,12},{24,0},{28,4},{32,56},... | collective-permute-start | bytes 491528 | tf_op jit(solution)/shard_map/ppermute | solution.py:28
  77.5 26.9 %collective-permute-start.22 = (f32[4,8,1280]{2,1,0:T(8,128)S(1)}, f32[4,8,1280]{2,1,0:T(8,128)S(1)}, u32[]{:S(2)}, u32[]{:S(2)}) collective-permute-start(f32[4,8,1280]{2,1,0:T(8,128)S(1)} %pad_maximum_fusion.2.refs_4_.refs_2_), channel_id=1, source_target_pairs={{0,4},{4,0},{8,12},{12,8},{16,20},{20,16},{24,28},{28,24},{32,36},... | collective-permute-start | bytes 491528 | tf_op jit(solution)/shard_map/ppermute | solution.py:28
  82.9 21.5 %collective-permute-start.23 = (f32[4,8,1280]{2,1,0:T(8,128)S(1)}, f32[4,8,1280]{2,1,0:T(8,128)S(1)}, u32[]{:S(2)}, u32[]{:S(2)}) collective-permute-start(f32[4,8,1280]{2,1,0:T(8,128)S(1)} %collective-permute-done.19.refs_5_.refs_3_), channel_id=1, source_target_pairs={{0,4},{4,0},{8,12},{12,8},{16,20},{20,16},{24,28},{28,24},{32,36},... | collective-permute-start | bytes 491528 | tf_op jit(solution)/shard_map/ppermute | solution.py:28
  85.2 19.2 %collective-permute-start.24 = (f32[4,8,1280]{2,1,0:T(8,128)S(1)}, f32[4,8,1280]{2,1,0:T(8,128)S(1)}, u32[]{:S(2)}, u32[]{:S(2)}) collective-permute-start(f32[4,8,1280]{2,1,0:T(8,128)S(1)} %collective-permute-done.20.refs_6_.refs_4_), channel_id=1, source_target_pairs={{0,4},{4,0},{8,12},{12,8},{16,20},{20,16},{24,28},{28,24},{32,36},... | collective-permute-start | bytes 491528 | tf_op jit(solution)/shard_map/ppermute | solution.py:28
  86.4 18.1 %collective-permute-start.25 = (f32[4,8,1280]{2,1,0:T(8,128)S(1)}, f32[4,8,1280]{2,1,0:T(8,128)S(1)}, u32[]{:S(2)}, u32[]{:S(2)}) collective-permute-start(f32[4,8,1280]{2,1,0:T(8,128)S(1)} %collective-permute-done.21.refs_7_.refs_5_), channel_id=1, source_target_pairs={{0,4},{4,0},{8,12},{12,8},{16,20},{20,16},{24,28},{28,24},{32,36},... | collective-permute-start | bytes 491528 | tf_op jit(solution)/shard_map/ppermute | solution.py:28
  106.8 9.2 %collective-permute-start.27 = (f32[512,128]{1,0:T(8,128)S(1)}, f32[512,128]{1,0:T(8,128)S(1)}, u32[]{:S(2)}, u32[]{:S(2)}) collective-permute-start(f32[512,128]{1,0:T(8,128)S(1)} %score_part.1), channel_id=1, source_target_pairs={{0,2},{1,3},{2,0},{3,1},{4,6},{5,7},{6,4},{7,5},{8,10},{9,11},{10,... | collective-permute-start | bytes 786440 | tf_op jit(solution)/shard_map/ppermute | solution.py:28
  109.8 12.4 %collective-permute-start.28 = (f32[512,128]{1,0:T(8,128)S(1)}, f32[512,128]{1,0:T(8,128)S(1)}, u32[]{:S(2)}, u32[]{:S(2)}) collective-permute-start(f32[512,128]{1,0:T(8,128)S(1)} %score_part.1), channel_id=1, source_target_pairs={{0,3},{1,2},{2,1},{3,0},{4,7},{5,6},{6,5},{7,4},{8,11},{9,10},{10,... | collective-permute-start | bytes 786440 | tf_op jit(solution)/shard_map/ppermute | solution.py:28
  110.5 11.7 %collective-permute-start.26 = (f32[512,128]{1,0:T(8,128)S(1)}, f32[512,128]{1,0:T(8,128)S(1)}, u32[]{:S(2)}, u32[]{:S(2)}) collective-permute-start(f32[512,128]{1,0:T(8,128)S(1)} %score_part.1), channel_id=1, source_target_pairs={{0,1},{1,0},{2,3},{3,2},{4,5},{5,4},{6,7},{7,6},{8,9},{9,8},{10,11... | collective-permute-start | bytes 786440 | tf_op jit(solution)/shard_map/ppermute | solution.py:28
  (15 other events, 126.6 us)

commit v2 on v0

v2 whole, which is shorter than its diff:
```python
import functools

import jax
import jax.numpy as jnp
from jax import lax
from jax.experimental import pallas as pl
from jax.experimental.pallas import tpu as pltpu
from jax.sharding import PartitionSpec as P

HEAD_DIM = 64
CH = 64
TOK = 512
STATE = 128
COLS = 1280
HEADS = COLS // HEAD_DIM
BLK = 256
STEPS = COLS // BLK
SPANS = TOK // CH
USED = 10
TILE = 256
BF = jnp.bfloat16
F32 = jnp.float32
ROW, CORE, XMASK = 8, 1, 3
BLOCKS = tuple(slice(j * BLK, (j + 1) * BLK) for j in range(STEPS))

LOCAL = ((0, 0, 0), (0, 0, 1), (0, 0, 2), (1, 1, 0), (1, 1, 1), (1, 1, 2), (1, 0, 3))


def send(value, mask, axis="seq"):
    pairs = [(source, source ^ mask) for source in range(lax.axis_size(axis))]
    return lax.ppermute(value, axis, pairs)


def dot(a, b, over_a, over_b):
    return lax.dot_general(a, b, (((over_a,), (over_b,)), ((), ())), preferred_element_type=F32)


def coords():
    position = lax.axis_index("seq")
    return position, position & CORE, (position >> 1) & XMASK, (position >> 3) & CORE


def params(mib):
    return pltpu.CompilerParams(vmem_limit_bytes=mib * 1024 * 1024)


def cost(macs, moved):
    return pl.CostEstimate(flops=2 * macs, bytes_accessed=moved, transcendentals=0)


def shape(*dims, kind=F32):
    return jax.ShapeDtypeStruct(dims, kind)


VMEM = pl.BlockSpec(memory_space=pltpu.VMEM)
SMEM = pl.BlockSpec(memory_space=pltpu.SMEM)
HBM = pl.BlockSpec(memory_space=pltpu.HBM)


def level_operand(z_ref, index, k, position, w_ref, v_ref, e_ref, block):
    upper = (position >> (k - 1)) & 1

    @pl.when(upper == 1)
    def _():
        for a in range(SPANS):
            rows = slice(a * CH, (a + 1) * CH)
            scaled = w_ref[k + 3, a : a + 1, block] * e_ref[rows, block].astype(F32)
            z_ref[index, rows, block] = scaled.astype(BF)

    @pl.when(upper == 0)
    def _():
        z_ref[index, :, block] = v_ref[:, block]


def far_kernel(
    code_hbm, gain_hbm, q_hbm, v_hbm, e_hbm, w_ref, q_ref, v_ref, e_ref, z_ref, own_ref, oth_ref,
    code_ref, gain_ref, qt, lw, res, sems
):
    position, core, x, z0 = coords()
    first = []
    for i, (far, near) in enumerate(((code_hbm, code_ref), (gain_hbm, gain_ref), (q_hbm, q_ref))):
        copy = pltpu.make_async_copy(far, near, sems.at[2 * STEPS + i])
        copy.start()
        first.append(copy)
    copies = []
    for j, block in enumerate(BLOCKS):
        for i, (far, near) in enumerate(((v_hbm, v_ref), (e_hbm, e_ref))):
            copy = pltpu.make_async_copy(far.at[:, block], near.at[:, block], sems.at[2 * j + i])
            copy.start()
            copies.append(copy)
    lw[...] = jnp.zeros_like(lw)
    for copy in first:
        copy.wait()
    for a in range(SPANS):
        lw[0:15, a, 0:HEADS] = gain_ref[code_ref[a]]
    weights = lw[...].reshape(16 * SPANS, 128)[: USED * SPANS]
    high = weights.astype(BF)
    rest = weights - high.astype(F32)
    middle = rest.astype(BF)
    low = (rest - middle.astype(F32)).astype(BF)
    head = lax.broadcasted_iota(jnp.int32, (128, BLK), 0)
    for j, block in enumerate(BLOCKS):
        col = lax.broadcasted_iota(jnp.int32, (128, BLK), 1) + j * BLK
        spread = (head == col // HEAD_DIM).astype(BF)
        wide = dot(high, spread, 1, 0) + (dot(middle, spread, 1, 0) + dot(low, spread, 1, 0))
        w_ref[:, :, block] = wide.reshape(USED, SPANS, BLK)
    qt[...] = q_ref[...].T
    for j, block in enumerate(BLOCKS):
        copies[2 * j].wait()
        copies[2 * j + 1].wait()
        for index, k in enumerate((5, 6, 4)):
            level_operand(z_ref, index, k, position, w_ref, v_ref, e_ref, block)
            res[...] = dot(qt[...], z_ref[index, :, block], 1, 0).reshape(8, 2, ROW, BLK)
            for xr in range(4):
                for zr in range(2):
                    slot = 4 + zr if k == 4 else 2 * zr + index
                    half = zr if k == 4 else zr ^ z0
                    own_ref[xr, slot, :, block] = res[(core << 2) | (xr ^ x), half]
                    oth_ref[xr, slot, :, block] = res[((core ^ 1) << 2) | (xr ^ x), half]


def far_states(code, gain, q, v, e):
    return pl.pallas_call(
        far_kernel,
        in_specs=[HBM] * 5,
        out_specs=[VMEM] * 7,
        out_shape=[
            shape(USED, SPANS, COLS),
            shape(TOK, STATE, kind=BF),
            shape(TOK, COLS, kind=BF),
            shape(TOK, COLS, kind=BF),
            shape(3, TOK, COLS, kind=BF),
            shape(4, 6, ROW, COLS),
            shape(4, 6, ROW, COLS),
        ],
        scratch_shapes=[
            pltpu.SMEM((SPANS,), jnp.int32),
            pltpu.VMEM((16, 15, HEADS), F32),
            pltpu.VMEM((STATE, TOK), BF),
            pltpu.VMEM((16, SPANS, 128), F32),
            pltpu.VMEM((8, 2, ROW, BLK), F32),
            pltpu.SemaphoreType.DMA((2 * STEPS + 3,)),
        ],
        compiler_params=params(20),
        cost_estimate=cost(3 * TOK * STATE * COLS, 9 << 20),
        name="far_states",
    )(code, gain, q, v, e)


def near_kernel(q_ref, v_ref, e_ref, w_ref, z_ref, x_ref, own_ref, oth_ref, qt, res):
    position, core, x, z0 = coords()
    qt[...] = q_ref[...].T
    for index, k in enumerate((2, 3, 1)):
        for block in BLOCKS:
            level_operand(z_ref, index, k, position, w_ref, v_ref, e_ref, block)
            out = dot(qt[...], z_ref[index, :, block], 1, 0)
            if k == 1:
                x_ref[:, block] = out
            else:
                res[...] = out.reshape(2, STATE // 2, BLK)
                own_ref[k - 2, :, block] = res[core]
                oth_ref[k - 2, :, block] = res[core ^ 1]


def near_states(q, v, e, w):
    half = STATE // 2
    return pl.pallas_call(
        near_kernel,
        in_specs=[VMEM] * 4,
        out_specs=[VMEM] * 4,
        out_shape=[
            shape(3, TOK, COLS, kind=BF),
            shape(STATE, COLS),
            shape(2, half, COLS),
            shape(2, half, COLS),
        ],
        scratch_shapes=[pltpu.VMEM((STATE, TOK), BF), pltpu.VMEM((2, half, BLK), F32)],
        compiler_params=params(20),
        cost_estimate=cost(3 * TOK * STATE * COLS, 9 << 20),
        name="near_states",
    )(q, v, e, w)


def kept(level, flip):
    rows = lax.broadcasted_iota(jnp.int32, (TILE, TILE), 1 if flip else 0)
    keys = lax.broadcasted_iota(jnp.int32, (TILE, TILE), 0 if flip else 1)
    a, b = rows // CH, keys // CH
    if level == 0:
        return (a == b) & (keys <= rows)
    return ((a ^ b) >> (level - 1) == 1) & (a > b)


def add_outer(q_ref, w_ref, k, position, state, m_ref, d_ref, block):
    upper = (position >> (k - 1)) & 1

    @pl.when(upper == 1)
    def _():
        out = dot(q_ref[...], state, 1, 0)
        for a in range(SPANS):
            rows = slice(a * CH, (a + 1) * CH)
            m_ref[rows, block] += w_ref[k + 3, a : a + 1, block] * out[rows, :]

    @pl.when(upper == 0)
    def _():
        d_ref[:, block] += dot(q_ref[...], state, 1, 0)


def local_kernel(q_ref, v_ref, e_ref, w_ref, zn_ref, y1_ref, m_ref, d_ref, dq_ref, score, flipped, grad, z):
    position, core, x, z0 = coords()
    dq_ref[...] = jnp.zeros_like(dq_ref)
    grad[...] = jnp.zeros_like(grad)
    for index, (t, s, level) in enumerate(LOCAL):
        qt_rows = q_ref[t * TILE : (t + 1) * TILE, :]
        qs_rows = q_ref[s * TILE : (s + 1) * TILE, :]
        direct = dot(qt_rows, qs_rows, 1, 1)
        swapped = dot(qs_rows, qt_rows, 1, 1)
        if level < 3:
            direct = jnp.where(kept(level, False), direct, 0.0)
            swapped = jnp.where(kept(level, True), swapped, 0.0)
        score[index] = direct.astype(BF)
        flipped[index] = swapped.astype(BF)

    per = TILE // CH

    def one_block(j, carry):
        block = pl.ds(pl.multiple_of(j * BLK, BLK), BLK)
        mixed = [None, None]
        d_val = [None, None]
        for index, (t, s, level) in enumerate(LOCAL):
            vals = v_ref[s * TILE : (s + 1) * TILE, block]
            for a in range(per):
                rows = slice(t * TILE + a * CH, t * TILE + (a + 1) * CH)
                w_row = w_ref[level, t * per + a : t * per + a + 1, block]
                z[index, a * CH : (a + 1) * CH, :] = (w_row * e_ref[rows, block].astype(F32)).astype(BF)
            out = dot(score[index], vals, 1, 0)
            w_rows = jnp.concatenate(
                [
                    jnp.broadcast_to(w_ref[level, t * per + a : t * per + a + 1, block], (CH, BLK))
                    for a in range(per)
                ],
                axis=0,
            )
            out = w_rows * out
            back = dot(flipped[index], z[index], 1, 0)
            mixed[t] = out if mixed[t] is None else mixed[t] + out
            d_val[s] = back if d_val[s] is None else d_val[s] + back
            grad[index] += dot(z[index], vals, 1, 1)
        for i in range(2):
            m_ref[i * TILE : (i + 1) * TILE, block] = mixed[i]
            d_ref[i * TILE : (i + 1) * TILE, block] = d_val[i]
        state = y1_ref[:, block].astype(BF)
        add_outer(q_ref, w_ref, 1, position, state, m_ref, d_ref, block)
        dq_ref[...] += dot(zn_ref[2, :, block], state, 1, 1)
        return carry

    lax.fori_loop(0, STEPS, one_block, 0)
    q = [q_ref[i * TILE : (i + 1) * TILE, :] for i in range(2)]
    cross = grad[6].astype(BF)
    extra = [dot(cross, q[1], 0, 0), dot(cross, q[0], 1, 0)]
    for i in range(2):
        total = jnp.zeros((TILE, TILE), F32)
        for level in range(3):
            total = total + jnp.where(kept(level, False), grad[3 * i + level], 0.0)
        total = total.astype(BF)
        part = dot(total, q[i], 1, 0) + dot(total, q[i], 0, 0)
        dq_ref[i * TILE : (i + 1) * TILE, :] += part + extra[i]


def local_part(q, v, e, w, zn, y1):
    return pl.pallas_call(
        local_kernel,
        in_specs=[VMEM] * 6,
        out_specs=[VMEM] * 3,
        out_shape=[shape(TOK, COLS), shape(TOK, COLS), shape(TOK, STATE)],
        scratch_shapes=[
            pltpu.VMEM((7, TILE, TILE), BF),
            pltpu.VMEM((7, TILE, TILE), BF),
            pltpu.VMEM((7, TILE, TILE), F32),
            pltpu.VMEM((7, TILE, BLK), BF),
        ],
        compiler_params=params(20),
        cost_estimate=cost(25 * TILE * TILE * COLS, 9 << 20),
        name="local_part",
    )(q, v, e, w, zn, y1)


def mid_kernel(q_ref, w_ref, m_in, d_in, dq_in, z_ref, y2_ref, y3_ref, y23o_ref, m_ref, d_ref, dq_ref, y):
    position, core, x, z0 = coords()
    for index, ref in enumerate((y2_ref, y3_ref)):
        y[index, core] = ref[...].astype(BF)
        y[index, core ^ 1] = y23o_ref[index].astype(BF)
    grads = dq_in[...]
    for block in BLOCKS:
        m_ref[:, block] = m_in[:, block]
        d_ref[:, block] = d_in[:, block]
        for index, k in enumerate((2, 3)):
            state = y[index, :, :, block].reshape(STATE, BLK)
            add_outer(q_ref, w_ref, k, position, state, m_ref, d_ref, block)
            grads = grads + dot(z_ref[index, :, block], state, 1, 1)
    dq_ref[...] = grads


def mid_part(q, w, m, d, dq, z, y2, y3, y23o):
    return pl.pallas_call(
        mid_kernel,
        in_specs=[VMEM] * 9,
        out_specs=[VMEM] * 3,
        out_shape=[shape(TOK, COLS), shape(TOK, COLS), shape(TOK, STATE)],
        input_output_aliases={2: 0, 3: 1},
        scratch_shapes=[pltpu.VMEM((2, 2, STATE // 2, COLS), BF)],
        compiler_params=params(30),
        cost_estimate=cost(4 * TOK * STATE * COLS, 18 << 20),
        name="mid_part",
    )(q, w, m, d, dq, z, y2, y3, y23o)


def score_kernel(*refs):
    dq_in, z_ref = refs[:2]
    pieces = refs[2:10]
    parts, y, total = refs[10:14], refs[14], refs[15]
    position, core, x, z0 = coords()
    group = lax.axis_index("head")
    for cr in range(2):
        for xr in range(4):
            piece = pieces[4 * cr + xr]
            place = ((cr ^ core) << 2) | (xr ^ x)
            rows = pl.ds(pl.multiple_of(place * 16, 16), 16)
            for index in range(2):
                pair = [piece[2 * z0 + index], piece[2 * (1 - z0) + index]]
                y[index, rows, :] = jnp.concatenate(pair, axis=0).astype(BF)
            y[2, rows, :] = piece[4:6].reshape(16, COLS).astype(BF)
    grads = dq_in[...]
    for index in range(3):
        for block in BLOCKS:
            grads = grads + dot(z_ref[index, :, block], y[index, :, block], 1, 1)
    total[...] = grads.reshape(4, TOK // 4, STATE)
    for j in range(4):
        parts[j][...] = total[group ^ j]


def score_part(dq, z, pieces):
    part = shape(TOK // 4, STATE)
    return pl.pallas_call(
        score_kernel,
        in_specs=[VMEM] * 10,
        out_specs=[VMEM] * 5,
        out_shape=[part, part, part, part, shape(3, STATE, COLS, kind=BF)],
        scratch_shapes=[pltpu.VMEM((4, TOK // 4, STATE), F32)],
        compiler_params=params(20),
        cost_estimate=cost(3 * TOK * STATE * COLS, 5 << 20),
        name="score_part",
    )(dq, z, *pieces)


def join_kernel(a_ref, b_ref, c_ref, d_ref, out_ref):
    group = lax.axis_index("head")
    for j, ref in enumerate((a_ref, b_ref, c_ref, d_ref)):
        rows = pl.ds(pl.multiple_of((group ^ j) * (TOK // 4), TOK // 4), TOK // 4)
        out_ref[rows, :] = ref[...]


def join(parts):
    return pl.pallas_call(
        join_kernel,
        in_specs=[VMEM] * 4,
        out_specs=VMEM,
        out_shape=shape(TOK, STATE),
        compiler_params=params(8),
        cost_estimate=cost(0, 1 << 19),
        name="join",
    )(*parts)


def last_kernel(keep, q_ref, w_ref, in_ref, y_ref, out_ref, acc):
    position, core, x, z0 = coords()
    for block in BLOCKS:
        acc[:, block] = in_ref[:, block]
        for index, k in enumerate((5, 6, 4)):

            @pl.when((position >> (k - 1)) & 1 == keep)
            def _():
                out = dot(q_ref[...], y_ref[index, :, block], 1, 0)
                if keep == 0:
                    acc[:, block] += out
                else:
                    for a in range(SPANS):
                        rows = slice(a * CH, (a + 1) * CH)
                        acc[rows, block] += w_ref[k + 3, a : a + 1, block] * out[rows, :]

        out_ref[:, block] = acc[:, block].astype(BF)


def last_part(keep, q, w, before, y):
    return pl.pallas_call(
        functools.partial(last_kernel, keep),
        in_specs=[VMEM] * 4,
        out_specs=VMEM,
        out_shape=shape(TOK, COLS, kind=BF),
        scratch_shapes=[pltpu.VMEM((TOK, COLS), F32)],
        compiler_params=params(20),
        cost_estimate=cost(3 * TOK * STATE * COLS // 2, 5 << 20),
        name="last_mixed" if keep else "last_values",
    )(q, w, before, y)


def local(q_hbm, v_hbm, e_hbm, gain, code):
    tie = lax.optimization_barrier
    w, q, v, e, zf, own_f, oth_f = far_states(code, gain, q_hbm, v_hbm, e_hbm)
    got_f = send(oth_f, 1)
    zn, x1, own_n, oth_n = near_states(q, v, e, w)

    chip = [own_f[j] + got_f[j] for j in range(4)]
    chip, oth_n, x1 = tie((chip, oth_n, x1))
    slices = [send(chip[j], 2 * j) for j in (1, 2, 3)]
    got_n = send(oth_n, 1)
    y1 = send(x1, 1)
    m, d, dq = local_part(q, v, e, w, zn, y1)
    near = [own_n[i] + got_n[i] for i in range(2)]
    slices, near, m, d, dq = tie((slices, near, m, d, dq))
    mine = [sum((s[i] for s in slices), chip[0][i]) for i in range(2)]
    other = sum((s[2:6] for s in slices), chip[0][2:6])

    low = send(other, 8)
    y2 = send(near[0], 2)
    y3 = [send(near[1], 4), send(near[1], 6)]
    five = mine[0] + low[0]
    six = mine[1] + low[1]
    y5 = send(five, 16)
    y6 = send(six, 32) + send(six, 48)
    half = jnp.stack([y5, y6])
    rest = send(half, 8)
    rest, y2, y3 = tie((rest, y2, y3))
    quad = jnp.concatenate([half, rest, low[2:4]])
    y3 = y3[0] + y3[1]
    quad, y2, y3, dq = tie((quad, y2, y3, dq))
    pieces = [quad] + [send(quad, 2 * j) for j in (1, 2, 3)]
    y23o = send(jnp.stack([y2, y3]), 1)
    m, d, dq = mid_part(q, w, m, d, dq, zn, y2, y3, y23o)
    pieces, dq = tie((pieces, dq))
    pieces = pieces + [send(p, 1) for p in pieces]
    *parts, y = score_part(dq, zf, pieces)
    got = [send(parts[h], h, "head") for h in (1, 2, 3)]
    grad_values = last_part(0, q, w, d, y)
    got, grad_values = tie((got, grad_values))
    total = (parts[0] + got[0]) + (got[1] + got[2])
    total, m = tie((total, m))
    parts = [total] + [send(total, h, "head") for h in (1, 2, 3)]
    mixed = last_part(1, q, w, m, y)
    parts, mixed = tie((parts, mixed))
    return mixed, join(parts), grad_values


def solution(mesh):
    placed = (P("seq", None), P("seq", "head"), P("seq", "head"), P(None, None, "head"), P("seq"))
    return jax.shard_map(
        local,
        mesh=mesh,
        in_specs=placed,
        out_specs=(P("seq", "head"), P("seq", None), P("seq", "head")),
        check_vma=False,
    )
```

time: 717 us -> 103 us (0.14)
  waiting for transfers between devices: 348 us -> 30.7 us
  local copies, waits for them, and re-layouts: 184 us -> 5.14 us
  matrix products: 80 us -> 0 us
  other arithmetic: 66.8 us -> 0.4 us
  Pallas kernels: 0 us -> 29.3 us
  starting transfers between devices: 18.8 us -> 36.1 us
  between operations: 14.3 us -> 0.79 us
    ppermute x12 -> x28, waiting for transfers between devices: 277 us -> 30.7 us  [send(): return lax.ppermute(value, axis, pairs)]
    dot_general x43 -> x0, matrix products: 80 us -> none  [the longest x10 17 us: head_pair(): jnp.einsum('tgp,sgp->gts', cot_pair, val_pair, preferred_element_type=jnp...]
    psum x1 -> x0, waiting for transfers between devices: 70.8 us -> none  [local(): grad_qk = lax.psum(head_part, 'head')]
    dynamic_slice x40 -> x0, local copies, waits for them, and re-layouts: 47.1 us -> none  [the longest x20 32.4 us: head_pair(): lax.dynamic_slice_in_dim(cotangent, col_start, pair_cols, 1)]
    dynamic_update_slice x30 -> x0, local copies, waits for them, and re-layouts: 42.4 us -> none  [the longest x20 35 us: head_pair(): lax.dynamic_update_slice_in_dim(inner_out, part_out, col_start, 1)]
    add x21 -> x6, other arithmetic: 38.3 us -> 0.32 us  [the longest x1 0.14 us: local(): chip = [own_f[j] + got_f[j] for j in range(4)]]
    reshape x11 -> x0, local copies, waits for them, and re-layouts: 34.3 us -> none  [the longest x10 34.2 us: head_pair(): weight = jnp.broadcast_to(pair_weight[:, :, None, :, None], (2, span_coun...]
    pallas_call x0 -> x8, Pallas kernels: none -> 29.3 us  [the longest x1 7.78 us: local_part(): pl.pallas_call(local_kernel, in_specs=[VMEM] * 6, out_specs=[VMEM] * 3, o...]
  transfers between devices with their start and end apart: 13 -> 28, of which waited for: 9 -> 16; matrix products, arithmetic and copies ran while one was open for 36% -> 0% of each run, Pallas kernels for 0% -> 22%
where the time goes in v2:
time: 103 us; the launch traced here: 102 us
  starting transfers between devices  36.1 us (35%)
  waiting for transfers between devices  30.7 us (30%)
  Pallas kernels  29.3 us (28%)
  local copies, waits for them, and re-layouts  5.14 us (5%)
    ppermute x28, starting transfers between devices, send(): return lax.ppermute(value, axis, pairs)  36.1 us
    ppermute x28, waiting for transfers between devices, send(): return lax.ppermute(value, axis, pairs)  30.7 us
    pallas_call x1, Pallas kernels, local_part(): pl.pallas_call(local_kernel, in_specs=[VMEM] * 6, out_specs=[VMEM] * 3, o...  7.78 us
    pallas_call x2, Pallas kernels, last_part(): pl.pallas_call(functools.partial(last_kernel, keep), in_specs=[VMEM] * 4,...  5.95 us
    unnamed x9, local copies, waits for them, and re-layouts  5.13 us
    pallas_call x1, Pallas kernels, mid_part(): pl.pallas_call(mid_kernel, in_specs=[VMEM] * 9, out_specs=[VMEM] * 3, out...  4.94 us
    pallas_call x1, Pallas kernels, far_states(): pl.pallas_call(far_kernel, in_specs=[HBM] * 5, out_specs=[VMEM] * 7, out_...  4.73 us
    pallas_call x1, Pallas kernels, near_states(): pl.pallas_call(near_kernel, in_specs=[VMEM] * 4, out_specs=[VMEM] * 4, ou...  3.89 us
  transfers between devices with their start and end apart: 28, of which 16 were waited for; matrix products, arithmetic and copies ran while one was open for 0% of the time, Pallas kernels for 22%

profile of v2, /device:TPU:1, one launch (start us, length us, event | category | flops | bytes accessed | tf_op | source)
XLA Modules:
  0.0 102.4 jit_solution(12119066872088491435)
XLA Ops:
  5.8 4.7 %far_states.1 = (f32[10,8,1280]{2,1,0:T(8,128)S(1)}, bf16[512,128]{1,0:T(8,128)(2,1)S(1)}, bf16[512,1280]{1,0:T(8,128)(2,1)S(1)}, bf16[512,1280]{1,0:T(8,128)(2,...) custom-call(s32[8]{0:T(128)S(1)} %copy-done.3, ...), custom_call_target="tpu_custom_call" | custom-call | flops 503316480 | bytes 9437184 | tf_op jit(solution)/shard_map/far_states/pallas_call | solution.py:123
  10.5 3.3 %collective-permute-start = (f32[4,6,8,1280]{3,2,1,0:T(8,128)S(1)}, f32[4,6,8,1280]{3,2,1,0:T(8,128)S(1)}, u32[]{:S(2)}, u32[]{:S(2)}) collective-permute-start(f32[4,6,8,1280]{3,2,1,0:T(8,128)S(1)} %get-tuple-element.64), channel_id=1, source_target_pairs={{0,4},{4,0},{8,12},{12,8},{16,20},{20,16},{24,28},{28,24},{32,36},... | collective-permute-start | bytes 2949128 | tf_op jit(solution)/shard_map/ppermute | solution.py:31
  13.8 3.9 %near_states.1 = (bf16[3,512,1280]{2,1,0:T(8,128)(2,1)S(1)}, f32[128,1280]{1,0:T(8,128)S(1)}, f32[2,64,1280]{2,1,0:T(8,128)S(1)}, f32[2,64,1280]{2,1,0:T(8,128)S(1)}) custom-call(bf16[512,128]{1,0:T(8,128)(2,1)S(1)} %get-tuple-element.65.q_ref, bf16[512,1280]{1,0:T(8,128)(2,1)S(1)} %get-tuple-element.66.v_ref, ...), custom_call_target="tpu_custom_call" | custom-call | flops 503316480 | bytes 9437184 | tf_op jit(solution)/shard_map/near_states/pallas_call | solution.py:167
  18.5 2.2 %collective-permute-start.2 = (f32[6,8,1280]{2,1,0:T(8,128)S(1)}, f32[6,8,1280]{2,1,0:T(8,128)S(1)}, u32[]{:S(2)}, u32[]{:S(2)}) collective-permute-start(f32[6,8,1280]{2,1,0:T(8,128)S(1)} %get-tuple-element.73), channel_id=1, source_target_pairs={{0,16},{4,20},{8,24},{12,28},{16,0},{20,4},{24,8},{28,12},{32,48},... | collective-permute-start | bytes 737288 | tf_op jit(solution)/shard_map/ppermute | solution.py:31
  20.7 1.7 %collective-permute-start.3 = (f32[6,8,1280]{2,1,0:T(8,128)S(1)}, f32[6,8,1280]{2,1,0:T(8,128)S(1)}, u32[]{:S(2)}, u32[]{:S(2)}) collective-permute-start(f32[6,8,1280]{2,1,0:T(8,128)S(1)} %get-tuple-element.74), channel_id=1, source_target_pairs={{0,24},{4,28},{8,16},{12,20},{16,8},{20,12},{24,0},{28,4},{32,56},... | collective-permute-start | bytes 737288 | tf_op jit(solution)/shard_map/ppermute | solution.py:31
  22.5 7.8 %local_part.1 = (f32[512,1280]{1,0:T(8,128)S(1)}, f32[512,1280]{1,0:T(8,128)S(1)}, f32[512,128]{1,0:T(8,128)S(1)}) custom-call(bf16[512,128]{1,0:T(8,128)(2,1)S(1)} %get-tuple-element.65.q_ref, bf16[512,1280]{1,0:T(8,128)(2,1)S(1)} %get-tuple-element.66.v_ref, bf16[512,1280]{1,0:T(8,128)(2,1)S(1)} %get-tuple-element.67.e_ref, ...), custom_call_target="tpu_custom_call" | custom-call | flops 4194304000 | bytes 9437184 | tf_op jit(solution)/shard_map/local_part/pallas_call | solution.py:270
  30.3 1.8 %collective-permute-done.2 = f32[6,8,1280]{2,1,0:T(8,128)S(1)} collective-permute-done((f32[6,8,1280]{2,1,0:T(8,128)S(1)}, f32[6,8,1280]{2,1,0:T(8,128)S(1)}, u32[]{:S(2)}, u32[]{:S(2)}) %collective-permute-start.2) | collective-permute-done | bytes 245792 | tf_op jit(solution)/shard_map/ppermute | solution.py:31
  32.0 2.0 %collective-permute-done.3 = f32[6,8,1280]{2,1,0:T(8,128)S(1)} collective-permute-done((f32[6,8,1280]{2,1,0:T(8,128)S(1)}, f32[6,8,1280]{2,1,0:T(8,128)S(1)}, u32[]{:S(2)}, u32[]{:S(2)}) %collective-permute-start.3) | collective-permute-done | bytes 245792 | tf_op jit(solution)/shard_map/ppermute | solution.py:31
  34.1 1.8 %collective-permute-start.6 = (f32[4,8,1280]{2,1,0:T(8,128)S(1)}, f32[4,8,1280]{2,1,0:T(8,128)S(1)}, u32[]{:S(2)}, u32[]{:S(2)}) collective-permute-start(f32[4,8,1280]{2,1,0:T(8,128)S(1)} %slice_add_fusion.6), channel_id=1, source_target_pairs={{0,32},{4,36},{8,40},{12,44},{16,48},{20,52},{24,56},{28,60},{32,0... | collective-permute-start | bytes 491528 | tf_op jit(solution)/shard_map/ppermute | solution.py:31
  35.9 2.7 %collective-permute-done.6 = f32[4,8,1280]{2,1,0:T(8,128)S(1)} collective-permute-done((f32[4,8,1280]{2,1,0:T(8,128)S(1)}, f32[4,8,1280]{2,1,0:T(8,128)S(1)}, u32[]{:S(2)}, u32[]{:S(2)}) %collective-permute-start.6) | collective-permute-done | bytes 163872 | tf_op jit(solution)/shard_map/ppermute | solution.py:31
  38.6 6.8 %collective-permute-start.8 = (f32[8,1280]{1,0:T(8,128)S(1)}, f32[8,1280]{1,0:T(8,128)S(1)}, u32[]{:S(2)}, u32[]{:S(2)}) collective-permute-start(f32[8,1280]{1,0:T(8,128)S(1)} %get-tuple-element.130), channel_id=1, source_target_pairs={{0,128},{4,132},{8,136},{12,140},{16,144},{20,148},{24,152},{28,15... | collective-permute-start | bytes 122888 | tf_op jit(solution)/shard_map/ppermute | solution.py:31
  50.4 2.0 %collective-permute-done.7 = f32[8,1280]{1,0:T(8,128)S(1)} collective-permute-done((f32[8,1280]{1,0:T(8,128)S(1)}, f32[8,1280]{1,0:T(8,128)S(1)}, u32[]{:S(2)}, u32[]{:S(2)}) %collective-permute-start.7) | collective-permute-done | bytes 40992 | tf_op jit(solution)/shard_map/ppermute | solution.py:31
  53.0 3.0 %collective-permute-done.10 = f32[2,8,1280]{2,1,0:T(8,128)S(1)} collective-permute-done((f32[2,8,1280]{2,1,0:T(8,128)S(1)}, f32[2,8,1280]{2,1,0:T(8,128)S(1)}, u32[]{:S(2)}, u32[]{:S(2)}) %collective-permute-start.10) | collective-permute-done | bytes 81952 | tf_op jit(solution)/shard_map/ppermute | solution.py:31
  56.0 2.1 %collective-permute-done.11.y2_ref = f32[64,1280]{1,0:T(8,128)S(1)} collective-permute-done((f32[64,1280]{1,0:T(8,128)S(1)}, f32[64,1280]{1,0:T(8,128)S(1)}, u32[]{:S(2)}, u32[]{:S(2)}) %collective-permute-start.11) | collective-permute-done | bytes 327712 | tf_op jit(solution)/shard_map/ppermute | solution.py:31
  58.1 4.8 %collective-permute-done.13 = f32[64,1280]{1,0:T(8,128)S(1)} collective-permute-done((f32[64,1280]{1,0:T(8,128)S(1)}, f32[64,1280]{1,0:T(8,128)S(1)}, u32[]{:S(2)}, u32[]{:S(2)}) %collective-permute-start.13) | collective-permute-done | bytes 327712 | tf_op jit(solution)/shard_map/ppermute | solution.py:31
  64.0 1.8 %collective-permute-start.15 = (f32[6,8,1280]{2,1,0:T(8,128)S(1)}, f32[6,8,1280]{2,1,0:T(8,128)S(1)}, u32[]{:S(2)}, u32[]{:S(2)}) collective-permute-start(f32[6,8,1280]{2,1,0:T(8,128)S(1)} %pad_maximum_fusion.1.refs_2_), channel_id=1, source_target_pairs={{0,16},{4,20},{8,24},{12,28},{16,0},{20,4},{24,8},{28,12},{32,48},... | collective-permute-start | bytes 737288 | tf_op jit(solution)/shard_map/ppermute | solution.py:31
  65.8 2.1 %collective-permute-start.16 = (f32[6,8,1280]{2,1,0:T(8,128)S(1)}, f32[6,8,1280]{2,1,0:T(8,128)S(1)}, u32[]{:S(2)}, u32[]{:S(2)}) collective-permute-start(f32[6,8,1280]{2,1,0:T(8,128)S(1)} %pad_maximum_fusion.1.refs_2_), channel_id=1, source_target_pairs={{0,24},{4,28},{8,16},{12,20},{16,8},{20,12},{24,0},{28,4},{32,56},... | collective-permute-start | bytes 737288 | tf_op jit(solution)/shard_map/ppermute | solution.py:31
  67.9 4.9 %mid_part.1 = (f32[512,1280]{1,0:T(8,128)S(1)}, f32[512,1280]{1,0:T(8,128)S(1)}, f32[512,128]{1,0:T(8,128)S(1)}) custom-call(bf16[512,128]{1,0:T(8,128)(2,1)S(1)} %get-tuple-element.65.q_ref, f32[10,8,1280]{2,1,0:T(8,128)S(1)} %get-tuple-element.68.w_ref, f32[512,1280]{1,0:T(8,128)S(1)} %get-tuple-element.93.m_in, ...), custom_call_target="tpu_custom_call", output_to_operand_aliasing={{0}: (2, {}), {1}: (3, {})} | custom-call | flops 671088640 | bytes 18874368 | tf_op jit(solution)/shard_map/mid_part/pallas_call | solution.py:304
  72.8 4.3 %collective-permute-done.15.refs_4_ = f32[6,8,1280]{2,1,0:T(8,128)S(1)} collective-permute-done((f32[6,8,1280]{2,1,0:T(8,128)S(1)}, f32[6,8,1280]{2,1,0:T(8,128)S(1)}, u32[]{:S(2)}, u32[]{:S(2)}) %collective-permute-start.15) | collective-permute-done | bytes 245792 | tf_op jit(solution)/shard_map/ppermute | solution.py:31
  77.2 2.0 %collective-permute-done.16.refs_5_ = f32[6,8,1280]{2,1,0:T(8,128)S(1)} collective-permute-done((f32[6,8,1280]{2,1,0:T(8,128)S(1)}, f32[6,8,1280]{2,1,0:T(8,128)S(1)}, u32[]{:S(2)}, u32[]{:S(2)}) %collective-permute-start.16) | collective-permute-done | bytes 245792 | tf_op jit(solution)/shard_map/ppermute | solution.py:31
  85.8 2.6 %collective-permute-start.23 = (f32[128,128]{1,0:T(8,128)S(1)}, f32[128,128]{1,0:T(8,128)S(1)}, u32[]{:S(2)}, u32[]{:S(2)}) collective-permute-start(f32[128,128]{1,0:T(8,128)S(1)} %get-tuple-element.107), channel_id=1, source_target_pairs={{0,2},{1,3},{2,0},{3,1},{4,6},{5,7},{6,4},{7,5},{8,10},{9,11},{10,... | collective-permute-start | bytes 196616 | tf_op jit(solution)/shard_map/ppermute | solution.py:31
  88.4 4.5 %last_values.1 = bf16[512,1280]{1,0:T(8,128)(2,1)} custom-call(bf16[512,128]{1,0:T(8,128)(2,1)S(1)} %get-tuple-element.65.q_ref, f32[10,8,1280]{2,1,0:T(8,128)S(1)} %get-tuple-element.68.w_ref, f32[512,1280]{1,0:T(8,128)S(1)} %get-tuple-element.109.in_ref, bf16[3,128,1280]{2,1,0:T(8,128)(2,1)S(1)} %get-tuple-element.110.y_ref), custom_call_target="tpu_custom_call" | custom-call | flops 251658240 | bytes 5242880 | tf_op jit(solution)/shard_map/last_values/pallas_call | solution.py:394
  93.1 3.8 %collective-permute-start.26 = (f32[128,128]{1,0:T(8,128)S(1)}, f32[128,128]{1,0:T(8,128)S(1)}, u32[]{:S(2)}, u32[]{:S(2)}) collective-permute-start(f32[128,128]{1,0:T(8,128)S(1)} %add_add_fusion.a_ref), channel_id=1, source_target_pairs={{0,2},{1,3},{2,0},{3,1},{4,6},{5,7},{6,4},{7,5},{8,10},{9,11},{10,... | collective-permute-start | bytes 196616 | tf_op jit(solution)/shard_map/ppermute | solution.py:31
  99.3 2.4 %collective-permute-done.27.d_ref = f32[128,128]{1,0:T(8,128)S(1)} collective-permute-done((f32[128,128]{1,0:T(8,128)S(1)}, f32[128,128]{1,0:T(8,128)S(1)}, u32[]{:S(2)}, u32[]{:S(2)}) %collective-permute-start.27) | collective-permute-done | bytes 65568 | tf_op jit(solution)/shard_map/ppermute | solution.py:31
  (60 shorter events, 22.5 us)
Async XLA Ops:
  10.5 7.2 %collective-permute-start = (f32[4,6,8,1280]{3,2,1,0:T(8,128)S(1)}, f32[4,6,8,1280]{3,2,1,0:T(8,128)S(1)}, u32[]{:S(2)}, u32[]{:S(2)}) collective-permute-start(f32[4,6,8,1280]{3,2,1,0:T(8,128)S(1)} %get-tuple-element.64), channel_id=1, source_target_pairs={{0,4},{4,0},{8,12},{12,8},{16,20},{20,16},{24,28},{28,24},{32,36},... | collective-permute-start | bytes 2949128 | tf_op jit(solution)/shard_map/ppermute | solution.py:31
  17.9 4.5 %collective-permute-start.4 = (f32[2,64,1280]{2,1,0:T(8,128)S(1)}, f32[2,64,1280]{2,1,0:T(8,128)S(1)}, u32[]{:S(2)}, u32[]{:S(2)}) collective-permute-start(f32[2,64,1280]{2,1,0:T(8,128)S(1)} %get-tuple-element.76), channel_id=1, source_target_pairs={{0,4},{4,0},{8,12},{12,8},{16,20},{20,16},{24,28},{28,24},{32,36},... | collective-permute-start | bytes 1966088 | tf_op jit(solution)/shard_map/ppermute | solution.py:31
  18.0 4.5 %collective-permute-start.5 = (f32[128,1280]{1,0:T(8,128)S(1)}, f32[128,1280]{1,0:T(8,128)S(1)}, u32[]{:S(2)}, u32[]{:S(2)}) collective-permute-start(f32[128,1280]{1,0:T(8,128)S(1)} %get-tuple-element.78), channel_id=1, source_target_pairs={{0,4},{4,0},{8,12},{12,8},{16,20},{20,16},{24,28},{28,24},{32,36},... | collective-permute-start | bytes 1966088 | tf_op jit(solution)/shard_map/ppermute | solution.py:31
  18.5 11.8 %collective-permute-start.1 = (f32[6,8,1280]{2,1,0:T(8,128)S(1)}, f32[6,8,1280]{2,1,0:T(8,128)S(1)}, u32[]{:S(2)}, u32[]{:S(2)}) collective-permute-start(f32[6,8,1280]{2,1,0:T(8,128)S(1)} %get-tuple-element.72), channel_id=1, source_target_pairs={{0,8},{4,12},{8,0},{12,4},{16,24},{20,28},{24,16},{28,20},{32,40},... | collective-permute-start | bytes 737288 | tf_op jit(solution)/shard_map/ppermute | solution.py:31
  18.5 13.5 %collective-permute-start.2 = (f32[6,8,1280]{2,1,0:T(8,128)S(1)}, f32[6,8,1280]{2,1,0:T(8,128)S(1)}, u32[]{:S(2)}, u32[]{:S(2)}) collective-permute-start(f32[6,8,1280]{2,1,0:T(8,128)S(1)} %get-tuple-element.73), channel_id=1, source_target_pairs={{0,16},{4,20},{8,24},{12,28},{16,0},{20,4},{24,8},{28,12},{32,48},... | collective-permute-start | bytes 737288 | tf_op jit(solution)/shard_map/ppermute | solution.py:31
  20.7 13.3 %collective-permute-start.3 = (f32[6,8,1280]{2,1,0:T(8,128)S(1)}, f32[6,8,1280]{2,1,0:T(8,128)S(1)}, u32[]{:S(2)}, u32[]{:S(2)}) collective-permute-start(f32[6,8,1280]{2,1,0:T(8,128)S(1)} %get-tuple-element.74), channel_id=1, source_target_pairs={{0,24},{4,28},{8,16},{12,20},{16,8},{20,12},{24,0},{28,4},{32,56},... | collective-permute-start | bytes 737288 | tf_op jit(solution)/shard_map/ppermute | solution.py:31
  34.1 4.5 %collective-permute-start.6 = (f32[4,8,1280]{2,1,0:T(8,128)S(1)}, f32[4,8,1280]{2,1,0:T(8,128)S(1)}, u32[]{:S(2)}, u32[]{:S(2)}) collective-permute-start(f32[4,8,1280]{2,1,0:T(8,128)S(1)} %slice_add_fusion.6), channel_id=1, source_target_pairs={{0,32},{4,36},{8,40},{12,44},{16,48},{20,52},{24,56},{28,60},{32,0... | collective-permute-start | bytes 491528 | tf_op jit(solution)/shard_map/ppermute | solution.py:31
  38.6 9.5 %collective-permute-start.8 = (f32[8,1280]{1,0:T(8,128)S(1)}, f32[8,1280]{1,0:T(8,128)S(1)}, u32[]{:S(2)}, u32[]{:S(2)}) collective-permute-start(f32[8,1280]{1,0:T(8,128)S(1)} %get-tuple-element.130), channel_id=1, source_target_pairs={{0,128},{4,132},{8,136},{12,140},{16,144},{20,148},{24,152},{28,15... | collective-permute-start | bytes 122888 | tf_op jit(solution)/shard_map/ppermute | solution.py:31
  45.4 5.0 %collective-permute-start.9 = (f32[8,1280]{1,0:T(8,128)S(1)}, f32[8,1280]{1,0:T(8,128)S(1)}, u32[]{:S(2)}, u32[]{:S(2)}) collective-permute-start(f32[8,1280]{1,0:T(8,128)S(1)} %get-tuple-element.130), channel_id=1, source_target_pairs={{0,192},{4,196},{8,200},{12,204},{16,208},{20,212},{24,216},{28,22... | collective-permute-start | bytes 122888 | tf_op jit(solution)/shard_map/ppermute | solution.py:31
  45.4 12.7 %collective-permute-start.12 = (f32[64,1280]{1,0:T(8,128)S(1)}, f32[64,1280]{1,0:T(8,128)S(1)}, u32[]{:S(2)}, u32[]{:S(2)}) collective-permute-start(f32[64,1280]{1,0:T(8,128)S(1)} %get-tuple-element.86), channel_id=1, source_target_pairs={{0,16},{4,20},{8,24},{12,28},{16,0},{20,4},{24,8},{28,12},{32,48},... | collective-permute-start | bytes 983048 | tf_op jit(solution)/shard_map/ppermute | solution.py:31
  45.4 17.5 %collective-permute-start.13 = (f32[64,1280]{1,0:T(8,128)S(1)}, f32[64,1280]{1,0:T(8,128)S(1)}, u32[]{:S(2)}, u32[]{:S(2)}) collective-permute-start(f32[64,1280]{1,0:T(8,128)S(1)} %get-tuple-element.86), channel_id=1, source_target_pairs={{0,24},{4,28},{8,16},{12,20},{16,8},{20,12},{24,0},{28,4},{32,56},... | collective-permute-start | bytes 983048 | tf_op jit(solution)/shard_map/ppermute | solution.py:31
  46.4 11.6 %collective-permute-start.11 = (f32[64,1280]{1,0:T(8,128)S(1)}, f32[64,1280]{1,0:T(8,128)S(1)}, u32[]{:S(2)}, u32[]{:S(2)}) collective-permute-start(f32[64,1280]{1,0:T(8,128)S(1)} %get-tuple-element.85), channel_id=1, source_target_pairs={{0,8},{4,12},{8,0},{12,4},{16,24},{20,28},{24,16},{28,20},{32,40},... | collective-permute-start | bytes 983048 | tf_op jit(solution)/shard_map/ppermute | solution.py:31
  48.1 4.3 %collective-permute-start.7 = (f32[8,1280]{1,0:T(8,128)S(1)}, f32[8,1280]{1,0:T(8,128)S(1)}, u32[]{:S(2)}, u32[]{:S(2)}) collective-permute-start(f32[8,1280]{1,0:T(8,128)S(1)} %get-tuple-element.129), channel_id=1, source_target_pairs={{0,64},{4,68},{8,72},{12,76},{16,80},{20,84},{24,88},{28,92},{32,9... | collective-permute-start | bytes 122888 | tf_op jit(solution)/shard_map/ppermute | solution.py:31
  52.4 3.6 %collective-permute-start.10 = (f32[2,8,1280]{2,1,0:T(8,128)S(1)}, f32[2,8,1280]{2,1,0:T(8,128)S(1)}, u32[]{:S(2)}, u32[]{:S(2)}) collective-permute-start(f32[2,8,1280]{2,1,0:T(8,128)S(1)} %pad_maximum_fusion.2), channel_id=1, source_target_pairs={{0,32},{4,36},{8,40},{12,44},{16,48},{20,52},{24,56},{28,60},{32,0... | collective-permute-start | bytes 245768 | tf_op jit(solution)/shard_map/ppermute | solution.py:31
  63.1 4.8 %collective-permute-start.17 = (f32[2,64,1280]{2,1,0:T(8,128)S(1)}, f32[2,64,1280]{2,1,0:T(8,128)S(1)}, u32[]{:S(2)}, u32[]{:S(2)}) collective-permute-start(f32[2,64,1280]{2,1,0:T(8,128)S(1)} %pad_maximum_fusion), channel_id=1, source_target_pairs={{0,4},{4,0},{8,12},{12,8},{16,20},{20,16},{24,28},{28,24},{32,36},... | collective-permute-start | bytes 1966088 | tf_op jit(solution)/shard_map/ppermute | solution.py:31
  64.0 8.8 %collective-permute-start.14 = (f32[6,8,1280]{2,1,0:T(8,128)S(1)}, f32[6,8,1280]{2,1,0:T(8,128)S(1)}, u32[]{:S(2)}, u32[]{:S(2)}) collective-permute-start(f32[6,8,1280]{2,1,0:T(8,128)S(1)} %pad_maximum_fusion.1.refs_2_), channel_id=1, source_target_pairs={{0,8},{4,12},{8,0},{12,4},{16,24},{20,28},{24,16},{28,20},{32,40},... | collective-permute-start | bytes 737288 | tf_op jit(solution)/shard_map/ppermute | solution.py:31
  64.0 13.2 %collective-permute-start.15 = (f32[6,8,1280]{2,1,0:T(8,128)S(1)}, f32[6,8,1280]{2,1,0:T(8,128)S(1)}, u32[]{:S(2)}, u32[]{:S(2)}) collective-permute-start(f32[6,8,1280]{2,1,0:T(8,128)S(1)} %pad_maximum_fusion.1.refs_2_), channel_id=1, source_target_pairs={{0,16},{4,20},{8,24},{12,28},{16,0},{20,4},{24,8},{28,12},{32,48},... | collective-permute-start | bytes 737288 | tf_op jit(solution)/shard_map/ppermute | solution.py:31
  65.8 13.3 %collective-permute-start.16 = (f32[6,8,1280]{2,1,0:T(8,128)S(1)}, f32[6,8,1280]{2,1,0:T(8,128)S(1)}, u32[]{:S(2)}, u32[]{:S(2)}) collective-permute-start(f32[6,8,1280]{2,1,0:T(8,128)S(1)} %pad_maximum_fusion.1.refs_2_), channel_id=1, source_target_pairs={{0,24},{4,28},{8,16},{12,20},{16,8},{20,12},{24,0},{28,4},{32,56},... | collective-permute-start | bytes 737288 | tf_op jit(solution)/shard_map/ppermute | solution.py:31
  84.2 8.8 %collective-permute-start.22 = (f32[128,128]{1,0:T(8,128)S(1)}, f32[128,128]{1,0:T(8,128)S(1)}, u32[]{:S(2)}, u32[]{:S(2)}) collective-permute-start(f32[128,128]{1,0:T(8,128)S(1)} %get-tuple-element.106), channel_id=1, source_target_pairs={{0,1},{1,0},{2,3},{3,2},{4,5},{5,4},{6,7},{7,6},{8,9},{9,8},{10,11... | collective-permute-start | bytes 196616 | tf_op jit(solution)/shard_map/ppermute | solution.py:31
  85.8 7.2 %collective-permute-start.23 = (f32[128,128]{1,0:T(8,128)S(1)}, f32[128,128]{1,0:T(8,128)S(1)}, u32[]{:S(2)}, u32[]{:S(2)}) collective-permute-start(f32[128,128]{1,0:T(8,128)S(1)} %get-tuple-element.107), channel_id=1, source_target_pairs={{0,2},{1,3},{2,0},{3,1},{4,6},{5,7},{6,4},{7,5},{8,10},{9,11},{10,... | collective-permute-start | bytes 196616 | tf_op jit(solution)/shard_map/ppermute | solution.py:31
  88.4 4.6 %collective-permute-start.24 = (f32[128,128]{1,0:T(8,128)S(1)}, f32[128,128]{1,0:T(8,128)S(1)}, u32[]{:S(2)}, u32[]{:S(2)}) collective-permute-start(f32[128,128]{1,0:T(8,128)S(1)} %get-tuple-element.108), channel_id=1, source_target_pairs={{0,3},{1,2},{2,1},{3,0},{4,7},{5,6},{6,5},{7,4},{8,11},{9,10},{10,... | collective-permute-start | bytes 196616 | tf_op jit(solution)/shard_map/ppermute | solution.py:31
  93.0 5.3 %collective-permute-start.25 = (f32[128,128]{1,0:T(8,128)S(1)}, f32[128,128]{1,0:T(8,128)S(1)}, u32[]{:S(2)}, u32[]{:S(2)}) collective-permute-start(f32[128,128]{1,0:T(8,128)S(1)} %add_add_fusion.a_ref), channel_id=1, source_target_pairs={{0,1},{1,0},{2,3},{3,2},{4,5},{5,4},{6,7},{7,6},{8,9},{9,8},{10,11... | collective-permute-start | bytes 196616 | tf_op jit(solution)/shard_map/ppermute | solution.py:31
  93.1 6.2 %collective-permute-start.26 = (f32[128,128]{1,0:T(8,128)S(1)}, f32[128,128]{1,0:T(8,128)S(1)}, u32[]{:S(2)}, u32[]{:S(2)}) collective-permute-start(f32[128,128]{1,0:T(8,128)S(1)} %add_add_fusion.a_ref), channel_id=1, source_target_pairs={{0,2},{1,3},{2,0},{3,1},{4,6},{5,7},{6,4},{7,5},{8,10},{9,11},{10,... | collective-permute-start | bytes 196616 | tf_op jit(solution)/shard_map/ppermute | solution.py:31
  96.9 4.7 %collective-permute-start.27 = (f32[128,128]{1,0:T(8,128)S(1)}, f32[128,128]{1,0:T(8,128)S(1)}, u32[]{:S(2)}, u32[]{:S(2)}) collective-permute-start(f32[128,128]{1,0:T(8,128)S(1)} %add_add_fusion.a_ref), channel_id=1, source_target_pairs={{0,3},{1,2},{2,1},{3,0},{4,7},{5,6},{6,5},{7,4},{8,11},{9,10},{10,... | collective-permute-start | bytes 196616 | tf_op jit(solution)/shard_map/ppermute | solution.py:31
  (8 other events, 11.9 us)

commit v3 on v2

v3 whole, which is shorter than its diff:
```python
import functools

import jax
import jax.numpy as jnp
from jax import lax
from jax.experimental import pallas as pl
from jax.experimental.pallas import tpu as pltpu
from jax.sharding import PartitionSpec as P

HEAD_DIM = 64
CH = 64
TOK = 512
STATE = 128
COLS = 1280
HEADS = COLS // HEAD_DIM
BLK = 256
STEPS = COLS // BLK
SPANS = TOK // CH
USED = 10
TILE = 256
BF = jnp.bfloat16
F32 = jnp.float32
ROW, CORE, XMASK = 8, 1, 3
BLOCKS = tuple(slice(j * BLK, (j + 1) * BLK) for j in range(STEPS))

LOCAL = ((0, 0, 0), (0, 0, 1), (0, 0, 2), (1, 1, 0), (1, 1, 1), (1, 1, 2), (1, 0, 3))


def send(value, mask, axis="seq"):
    pairs = [(source, source ^ mask) for source in range(lax.axis_size(axis))]
    return lax.ppermute(value, axis, pairs)


def dot(a, b, over_a, over_b):
    return lax.dot_general(a, b, (((over_a,), (over_b,)), ((), ())), preferred_element_type=F32)


def coords():
    position = lax.axis_index("seq")
    return position, position & CORE, (position >> 1) & XMASK, (position >> 3) & CORE


def params(mib):
    return pltpu.CompilerParams(vmem_limit_bytes=mib * 1024 * 1024)


def cost():
    return pl.CostEstimate(flops=1024, bytes_accessed=1024, transcendentals=0)


def shape(*dims, kind=F32):
    return jax.ShapeDtypeStruct(dims, kind)


VMEM = pl.BlockSpec(memory_space=pltpu.VMEM)
SMEM = pl.BlockSpec(memory_space=pltpu.SMEM)
HBM = pl.BlockSpec(memory_space=pltpu.HBM)


def level_operand(z_ref, index, k, position, w_ref, v_ref, e_ref, block):
    upper = (position >> (k - 1)) & 1

    @pl.when(upper == 1)
    def _():
        for a in range(SPANS):
            rows = slice(a * CH, (a + 1) * CH)
            scaled = w_ref[k + 3, a : a + 1, block] * e_ref[rows, block].astype(F32)
            z_ref[index, rows, block] = scaled.astype(BF)

    @pl.when(upper == 0)
    def _():
        z_ref[index, :, block] = v_ref[:, block]


def near_kernel(
    code_hbm, gain_hbm, q_hbm, v_hbm, e_hbm, w_ref, q_ref, qt, v_ref, e_ref, z_ref, own_ref, oth_ref,
    code_ref, gain_ref, lw, res, sems
):
    position, core, x, z0 = coords()
    first = []
    for i, (far, near) in enumerate(((code_hbm, code_ref), (gain_hbm, gain_ref), (q_hbm, q_ref))):
        copy = pltpu.make_async_copy(far, near, sems.at[2 * STEPS + i])
        copy.start()
        first.append(copy)
    copies = []
    for j, block in enumerate(BLOCKS):
        for i, (far, near) in enumerate(((v_hbm, v_ref), (e_hbm, e_ref))):
            copy = pltpu.make_async_copy(far.at[:, block], near.at[:, block], sems.at[2 * j + i])
            copy.start()
            copies.append(copy)
    lw[...] = jnp.zeros_like(lw)
    for copy in first:
        copy.wait()
    for a in range(SPANS):
        lw[0:15, a : a + 1, 0:HEADS] = gain_ref[:, pl.ds(code_ref[a], 1), :]
    weights = lw[...].reshape(16 * SPANS, 128)[: USED * SPANS]
    high = weights.astype(BF)
    rest = weights - high.astype(F32)
    middle = rest.astype(BF)
    low = (rest - middle.astype(F32)).astype(BF)
    head = lax.broadcasted_iota(jnp.int32, (128, BLK), 0)
    for j, block in enumerate(BLOCKS):
        col = lax.broadcasted_iota(jnp.int32, (128, BLK), 1) + j * BLK
        spread = (head == col // HEAD_DIM).astype(BF)
        wide = dot(high, spread, 1, 0) + (dot(middle, spread, 1, 0) + dot(low, spread, 1, 0))
        w_ref[:, :, block] = wide.reshape(USED, SPANS, BLK)
    qt[...] = q_ref[...].T
    for j, block in enumerate(BLOCKS):
        copies[2 * j].wait()
        copies[2 * j + 1].wait()
        for index, k in enumerate((2, 3)):
            level_operand(z_ref, index, k, position, w_ref, v_ref, e_ref, block)
            res[...] = dot(qt[...], z_ref[index, :, block], 1, 0).reshape(2, STATE // 2, BLK)
            own_ref[index, :, block] = res[core]
            oth_ref[index, :, block] = res[core ^ 1]


def near_states(code, gain, q, v, e):
    half = STATE // 2
    return pl.pallas_call(
        near_kernel,
        in_specs=[HBM] * 5,
        out_specs=[VMEM] * 8,
        out_shape=[
            shape(USED, SPANS, COLS),
            shape(TOK, STATE, kind=BF),
            shape(STATE, TOK, kind=BF),
            shape(TOK, COLS, kind=BF),
            shape(TOK, COLS, kind=BF),
            shape(2, TOK, COLS, kind=BF),
            shape(2, half, COLS),
            shape(2, half, COLS),
        ],
        scratch_shapes=[
            pltpu.SMEM((SPANS,), jnp.int32),
            pltpu.VMEM((15, 16, HEADS), F32),
            pltpu.VMEM((16, SPANS, 128), F32),
            pltpu.VMEM((2, half, BLK), F32),
            pltpu.SemaphoreType.DMA((2 * STEPS + 3,)),
        ],
        compiler_params=params(20),
        cost_estimate=cost(),
        name="near_states",
    )(code, gain, q, v, e)


def far_kernel(qt, v_ref, e_ref, w_ref, z_ref, own_ref, oth_ref, res):
    position, core, x, z0 = coords()
    for block in BLOCKS:
        for index, k in enumerate((5, 6)):
            level_operand(z_ref, index, k, position, w_ref, v_ref, e_ref, block)
            res[...] = dot(qt[...], z_ref[index, :, block], 1, 0).reshape(8, 2, ROW, BLK)
            for xr in range(4):
                for zr in range(2):
                    own_ref[xr, 2 * zr + index, :, block] = res[(core << 2) | (xr ^ x), zr ^ z0]
                    oth_ref[xr, 2 * zr + index, :, block] = res[((core ^ 1) << 2) | (xr ^ x), zr ^ z0]
    own_ref[:, 4:6] = jnp.zeros((4, 2, ROW, COLS), F32)
    oth_ref[:, 4:6] = jnp.zeros((4, 2, ROW, COLS), F32)


def far_states(qt, v, e, w):
    return pl.pallas_call(
        far_kernel,
        in_specs=[VMEM] * 4,
        out_specs=[VMEM] * 3,
        out_shape=[
            shape(2, TOK, COLS, kind=BF),
            shape(4, 6, ROW, COLS),
            shape(4, 6, ROW, COLS),
        ],
        scratch_shapes=[pltpu.VMEM((8, 2, ROW, BLK), F32)],
        compiler_params=params(20),
        cost_estimate=cost(),
        name="far_states",
    )(qt, v, e, w)


def rest_kernel(qt, v_ref, e_ref, w_ref, own_in, oth_in, z_ref, own_ref, oth_ref, x_ref, res):
    position, core, x, z0 = coords()
    own_ref[:, 0:4] = own_in[:, 0:4]
    oth_ref[:, 0:4] = oth_in[:, 0:4]
    for block in BLOCKS:
        for index, k in enumerate((4, 1)):
            level_operand(z_ref, index, k, position, w_ref, v_ref, e_ref, block)
            out = dot(qt[...], z_ref[index, :, block], 1, 0)
            if k == 1:
                x_ref[:, block] = out
                continue
            res[...] = out.reshape(8, 2, ROW, BLK)
            for xr in range(4):
                own_ref[xr, 4:6, :, block] = res[(core << 2) | (xr ^ x)]
                oth_ref[xr, 4:6, :, block] = res[((core ^ 1) << 2) | (xr ^ x)]


def rest_states(qt, v, e, w, own, oth):
    return pl.pallas_call(
        rest_kernel,
        in_specs=[VMEM] * 6,
        out_specs=[VMEM] * 4,
        out_shape=[
            shape(2, TOK, COLS, kind=BF),
            shape(4, 6, ROW, COLS),
            shape(4, 6, ROW, COLS),
            shape(STATE, COLS),
        ],
        scratch_shapes=[pltpu.VMEM((8, 2, ROW, BLK), F32)],
        compiler_params=params(20),
        cost_estimate=cost(),
        name="rest_states",
    )(qt, v, e, w, own, oth)


def kept(level, flip):
    rows = lax.broadcasted_iota(jnp.int32, (TILE, TILE), 1 if flip else 0)
    keys = lax.broadcasted_iota(jnp.int32, (TILE, TILE), 0 if flip else 1)
    a, b = rows // CH, keys // CH
    if level == 0:
        return (a == b) & (keys <= rows)
    return ((a ^ b) >> (level - 1) == 1) & (a > b)


def add_outer(q_ref, w_ref, levels, position, y_ref, m_ref, d_ref, block):
    for index, k in enumerate(levels):

        @pl.when((position >> (k - 1)) & 1 == 1)
        def _():
            out = dot(q_ref[...], y_ref[index, :, block].astype(BF), 1, 0)
            for a in range(SPANS):
                rows = slice(a * CH, (a + 1) * CH)
                m_ref[rows, block] += w_ref[k + 3, a : a + 1, block] * out[rows, :]

    lower = None
    for index, k in enumerate(levels):
        part = (1 - ((position >> (k - 1)) & 1)).astype(F32) * y_ref[index, :, block]
        lower = part if lower is None else lower + part
    d_ref[:, block] += dot(q_ref[...], lower.astype(BF), 1, 0)


def local_kernel(q_ref, v_ref, e_ref, w_ref, zr_ref, y1_ref, m_ref, d_ref, dq_ref, score, flipped, grad, z, y):
    y[0] = y1_ref[...]
    position, core, x, z0 = coords()
    dq_ref[...] = jnp.zeros_like(dq_ref)
    grad[...] = jnp.zeros_like(grad)
    for index, (t, s, level) in enumerate(LOCAL):
        qt_rows = q_ref[t * TILE : (t + 1) * TILE, :]
        qs_rows = q_ref[s * TILE : (s + 1) * TILE, :]
        direct = dot(qt_rows, qs_rows, 1, 1)
        swapped = dot(qs_rows, qt_rows, 1, 1)
        if level < 3:
            direct = jnp.where(kept(level, False), direct, 0.0)
            swapped = jnp.where(kept(level, True), swapped, 0.0)
        score[index] = direct.astype(BF)
        flipped[index] = swapped.astype(BF)

    per = TILE // CH

    def one_block(j, carry):
        block = pl.ds(pl.multiple_of(j * BLK, BLK), BLK)
        mixed = [None, None]
        d_val = [None, None]
        for index, (t, s, level) in enumerate(LOCAL):
            vals = v_ref[s * TILE : (s + 1) * TILE, block]
            for a in range(per):
                rows = slice(t * TILE + a * CH, t * TILE + (a + 1) * CH)
                w_row = w_ref[level, t * per + a : t * per + a + 1, block]
                z[index, a * CH : (a + 1) * CH, :] = (w_row * e_ref[rows, block].astype(F32)).astype(BF)
            out = dot(score[index], vals, 1, 0)
            w_rows = jnp.concatenate(
                [
                    jnp.broadcast_to(w_ref[level, t * per + a : t * per + a + 1, block], (CH, BLK))
                    for a in range(per)
                ],
                axis=0,
            )
            out = w_rows * out
            back = dot(flipped[index], z[index], 1, 0)
            mixed[t] = out if mixed[t] is None else mixed[t] + out
            d_val[s] = back if d_val[s] is None else d_val[s] + back
            grad[index] += dot(z[index], vals, 1, 1)
        for i in range(2):
            m_ref[i * TILE : (i + 1) * TILE, block] = mixed[i]
            d_ref[i * TILE : (i + 1) * TILE, block] = d_val[i]
        add_outer(q_ref, w_ref, (1,), position, y, m_ref, d_ref, block)
        dq_ref[...] += dot(zr_ref[1, :, block], y[0, :, block].astype(BF), 1, 1)
        return carry

    lax.fori_loop(0, STEPS, one_block, 0)
    q = [q_ref[i * TILE : (i + 1) * TILE, :] for i in range(2)]
    cross = grad[6].astype(BF)
    extra = [dot(cross, q[1], 0, 0), dot(cross, q[0], 1, 0)]
    for i in range(2):
        total = jnp.zeros((TILE, TILE), F32)
        for level in range(3):
            total = total + jnp.where(kept(level, False), grad[3 * i + level], 0.0)
        total = total.astype(BF)
        part = dot(total, q[i], 1, 0) + dot(total, q[i], 0, 0)
        dq_ref[i * TILE : (i + 1) * TILE, :] += part + extra[i]


def local_part(q, v, e, w, zr, y1):
    return pl.pallas_call(
        local_kernel,
        in_specs=[VMEM] * 6,
        out_specs=[VMEM] * 3,
        out_shape=[shape(TOK, COLS), shape(TOK, COLS), shape(TOK, STATE)],
        scratch_shapes=[
            pltpu.VMEM((7, TILE, TILE), BF),
            pltpu.VMEM((7, TILE, TILE), BF),
            pltpu.VMEM((7, TILE, TILE), F32),
            pltpu.VMEM((7, TILE, BLK), BF),
            pltpu.VMEM((1, STATE, COLS), F32),
        ],
        compiler_params=params(20),
        cost_estimate=cost(),
        name="local_part",
    )(q, v, e, w, zr, y1)


def mid_kernel(q_ref, w_ref, m_in, d_in, dq_in, z_ref, y2_ref, y3_ref, y23o_ref, m_ref, d_ref, dq_ref, y):
    position, core, x, z0 = coords()
    half = STATE // 2
    own = pl.ds(pl.multiple_of(core * half, half), half)
    oth = pl.ds(pl.multiple_of((core ^ 1) * half, half), half)
    for index, ref in enumerate((y2_ref, y3_ref)):
        y[index, own, :] = ref[...]
        y[index, oth, :] = y23o_ref[index]
    grads = dq_in[...]
    for block in BLOCKS:
        m_ref[:, block] = m_in[:, block]
        d_ref[:, block] = d_in[:, block]
        add_outer(q_ref, w_ref, (2, 3), position, y, m_ref, d_ref, block)
        for index in range(2):
            grads = grads + dot(z_ref[index, :, block], y[index, :, block].astype(BF), 1, 1)
    dq_ref[...] = grads


def mid_part(q, w, m, d, dq, zn, y2, y3, y23o):
    return pl.pallas_call(
        mid_kernel,
        in_specs=[VMEM] * 9,
        out_specs=[VMEM] * 3,
        out_shape=[shape(TOK, COLS), shape(TOK, COLS), shape(TOK, STATE)],
        input_output_aliases={2: 0, 3: 1},
        scratch_shapes=[pltpu.VMEM((2, STATE, COLS), F32)],
        compiler_params=params(30),
        cost_estimate=cost(),
        name="mid_part",
    )(q, w, m, d, dq, zn, y2, y3, y23o)


def score_kernel(*refs):
    dq_in, zf_ref, zr_ref = refs[:3]
    pieces = refs[3:11]
    top_ref, low_ref, y = refs[11:]
    position, core, x, z0 = coords()
    for cr in range(2):
        for xr in range(4):
            piece = pieces[4 * cr + xr]
            place = ((cr ^ core) << 2) | (xr ^ x)
            rows = pl.ds(pl.multiple_of(place * 16, 16), 16)
            for index in range(2):
                pair = [piece[2 * z0 + index], piece[2 * (1 - z0) + index]]
                y[index, rows, :] = jnp.concatenate(pair, axis=0)
            y[2, rows, :] = piece[4:6].reshape(16, COLS)
    grads = dq_in[...]
    for block in BLOCKS:
        for index in range(3):
            z = zr_ref[0, :, block] if index == 2 else zf_ref[index, :, block]
            grads = grads + dot(z, y[index, :, block].astype(BF), 1, 1)
    top_ref[...] = grads[: TOK // 2]
    low_ref[...] = grads[TOK // 2 :]


def score_part(dq, zf, zr, pieces):
    part = shape(TOK // 2, STATE)
    return pl.pallas_call(
        score_kernel,
        in_specs=[VMEM] * 11,
        out_specs=[VMEM] * 3,
        out_shape=[part, part, shape(3, STATE, COLS)],
        compiler_params=params(20),
        cost_estimate=cost(),
        name="score_part",
    )(dq, zf, zr, *pieces)


def last_values_kernel(q_ref, d_in, y_ref, out_ref):
    position = lax.axis_index("seq")
    for block in BLOCKS:
        lower = None
        for index, k in enumerate((5, 6, 4)):
            part = (1 - ((position >> (k - 1)) & 1)).astype(F32) * y_ref[index, :, block]
            lower = part if lower is None else lower + part
        out_ref[:, block] = (d_in[:, block] + dot(q_ref[...], lower.astype(BF), 1, 0)).astype(BF)


def last_values(q, d, y):
    return pl.pallas_call(
        last_values_kernel,
        in_specs=[VMEM] * 3,
        out_specs=VMEM,
        out_shape=shape(TOK, COLS, kind=BF),
        compiler_params=params(20),
        cost_estimate=cost(),
        name="last_values",
    )(q, d, y)


def last_mixed_kernel(q_ref, w_ref, m_in, y_ref, out_ref):
    position = lax.axis_index("seq")
    for block in BLOCKS:
        outs = [dot(q_ref[...], y_ref[index, :, block].astype(BF), 1, 0) for index in range(3)]
        for a in range(SPANS):
            rows = slice(a * CH, (a + 1) * CH)
            total = m_in[rows, block]
            for index, k in enumerate((5, 6, 4)):
                upper = ((position >> (k - 1)) & 1).astype(F32)
                total = total + (upper * w_ref[k + 3, a : a + 1, block]) * outs[index][rows, :]
            out_ref[rows, block] = total.astype(BF)


def last_mixed(q, w, m, y):
    return pl.pallas_call(
        last_mixed_kernel,
        in_specs=[VMEM] * 4,
        out_specs=VMEM,
        out_shape=shape(TOK, COLS, kind=BF),
        compiler_params=params(20),
        cost_estimate=cost(),
        name="last_mixed",
    )(q, w, m, y)


def local(*args):
    tie = lax.optimization_barrier
    args = args[:3] + (args[3].transpose(1, 0, 2),) + args[4:]
    q_hbm, v_hbm, e_hbm, gain, code = [pltpu.with_memory_space_constraint(a, pltpu.HBM) for a in args]
    w, q, qt, v, e, zn, own_n, oth_n = near_states(code, gain, q_hbm, v_hbm, e_hbm)
    got_n = send(oth_n, 1)
    zf, own_f, oth_f = far_states(qt, v, e, w)
    near = [own_n[i] + got_n[i] for i in range(2)]
    near, own_f, oth_f = tie((near, own_f, oth_f))
    y2 = send(near[0], 2)
    y3 = send(near[1], 6)
    zr, own_f, oth_f, x1 = rest_states(qt, v, e, w, own_f, oth_f)
    got_f = send(oth_f, 1)
    y1 = send(x1, 1)

    chip = [own_f[j] + got_f[j] for j in range(4)]
    v2, chip, y1 = tie((v, chip, y1))
    slices = [send(chip[j], 2 * j) for j in (1, 2, 3)]
    m, d, dq = local_part(q, v2, e, w, zr, y1)
    slices, dq, near, y2, y3 = tie((slices, dq, near, y2, y3))
    y3b = send(near[1], 4)
    mine = [sum((s[i] for s in slices), chip[0][i]) for i in range(2)]
    other = sum((s[2:6] for s in slices), chip[0][2:6])

    low = send(other, 8)
    five = mine[0] + low[0]
    six = mine[1] + low[1]
    y5 = send(five, 16)
    y6 = send(six, 32) + send(six, 48)
    half = tie(jnp.stack([y5, y6]))
    rest = send(half, 8)
    quad = jnp.concatenate([half, rest, low[2:4]])
    quad, dq, y3b = tie((quad, dq, y3b))
    pieces = [quad] + [send(quad, 2 * j) for j in (1, 2, 3)]
    y3 = y3 + y3b
    y23o = send(jnp.stack([y2, y3]), 1)
    m, d, dq = mid_part(q, w, m, d, dq, zn, y2, y3, y23o)
    pieces[1], pieces[3], dq = tie((pieces[1], pieces[3], dq))
    swapped = [send(pieces[j], 1) for j in (0, 1, 3)]
    pieces[2], *swapped = tie((pieces[2], *swapped))
    swapped.insert(2, send(pieces[2], 1))
    pieces = pieces + swapped
    top, low, y = score_part(dq, zf, zr, pieces)
    got = [send(top, 1, "head"), send(low, 3, "head")]
    grad_values = last_values(q, d, y)
    got, grad_values = tie((got, grad_values))
    top = top + got[0]
    low = low + got[1]
    top, low, m = tie((top, low, m))
    got = [send(top, 3, "head"), send(low, 1, "head")]
    mixed = last_mixed(q, w, m, y)
    got, mixed = tie((got, mixed))
    grad_qk = jnp.concatenate([top + got[0], low + got[1]])
    return mixed, grad_qk, grad_values


def solution(mesh):
    placed = (P("seq", None), P("seq", "head"), P("seq", "head"), P(None, None, "head"), P("seq"))
    return jax.shard_map(
        local,
        mesh=mesh,
        in_specs=placed,
        out_specs=(P("seq", "head"), P("seq", None), P("seq", "head")),
        check_vma=False,
    )
```

time: 103 us -> 95.2 us (0.924)
  starting transfers between devices: 36.1 us -> 42 us
  waiting for transfers between devices: 30.7 us -> 25.2 us
  local copies, waits for them, and re-layouts: 5.14 us -> 0.01 us
  Pallas kernels: 29.3 us -> 24.7 us
    ppermute x28 -> x26, starting transfers between devices: 36.1 us -> 42 us  [send(): return lax.ppermute(value, axis, pairs)]
    ppermute x28 -> x26, waiting for transfers between devices: 30.7 us -> 25.2 us  [send(): return lax.ppermute(value, axis, pairs)]
    unnamed x9 -> x0, local copies, waits for them, and re-layouts: 5.13 us -> none
    pallas_call x1, Pallas kernels: 4.94 us -> 2.43 us  [mid_part(): pl.pallas_call(mid_kernel, in_specs=[VMEM] * 9, out_specs=[VMEM] * 3, out...]
    pallas_call x6, Pallas kernels: 16.6 us -> 14.1 us  [the longest x1 4.01 us: near_states(): pl.pallas_call(near_kernel, in_specs=[HBM] * 5, out_specs=[VMEM] * 8, out...]
  transfers between devices with their start and end apart: 28 -> 26, of which waited for: 16 -> 14; matrix products, arithmetic and copies ran while one was open for 0% -> 0% of each run, Pallas kernels for 22% -> 18%
where the time goes in v3:
time: 95.2 us; the launch traced here: 93.9 us
  starting transfers between devices  42 us (44%)
  waiting for transfers between devices  25.2 us (26%)
  Pallas kernels  24.7 us (26%)
  other arithmetic  1.13 us (1%)
    ppermute x26, starting transfers between devices, send(): return lax.ppermute(value, axis, pairs)  42 us
    ppermute x26, waiting for transfers between devices, send(): return lax.ppermute(value, axis, pairs)  25.2 us
    pallas_call x1, Pallas kernels, local_part(): pl.pallas_call(local_kernel, in_specs=[VMEM] * 6, out_specs=[VMEM] * 3, o...  8.14 us
    pallas_call x1, Pallas kernels, near_states(): pl.pallas_call(near_kernel, in_specs=[HBM] * 5, out_specs=[VMEM] * 8, out...  4.01 us
    pallas_call x1, Pallas kernels, rest_states(): pl.pallas_call(rest_kernel, in_specs=[VMEM] * 6, out_specs=[VMEM] * 4, ou...  2.57 us
    pallas_call x1, Pallas kernels, mid_part(): pl.pallas_call(mid_kernel, in_specs=[VMEM] * 9, out_specs=[VMEM] * 3, out...  2.43 us
    pallas_call x1, Pallas kernels, far_states(): pl.pallas_call(far_kernel, in_specs=[VMEM] * 4, out_specs=[VMEM] * 3, out...  2.43 us
    pallas_call x1, Pallas kernels, last_mixed(): pl.pallas_call(last_mixed_kernel, in_specs=[VMEM] * 4, out_specs=VMEM, ou...  2.23 us
  transfers between devices with their start and end apart: 26, of which 14 were waited for; matrix products, arithmetic and copies ran while one was open for 0% of the time, Pallas kernels for 18%

profile of v3, /device:TPU:1, one launch (start us, length us, event | category | flops | bytes accessed | tf_op | source)
XLA Modules:
  0.0 93.9 jit_solution(4947234185068892058)
XLA Ops:
  0.6 4.0 %near_states.1 = (f32[10,8,1280]{2,1,0:T(8,128)S(1)}, bf16[512,128]{1,0:T(8,128)(2,1)S(1)}, bf16[128,512]{1,0:T(8,128)(2,1)S(1)}, bf16[512,1280]{1,0:T(8,128)(2,...) custom-call(s32[8]{0:T(128)} %code_hbm.1, ...), custom_call_target="tpu_custom_call" | custom-call | flops 1024 | bytes 1024 | tf_op jit(solution)/shard_map/near_states/pallas_call | solution.py:120
  4.7 3.2 %collective-permute-start = (f32[2,64,1280]{2,1,0:T(8,128)S(1)}, f32[2,64,1280]{2,1,0:T(8,128)S(1)}, u32[]{:S(2)}, u32[]{:S(2)}) collective-permute-start(f32[2,64,1280]{2,1,0:T(8,128)S(1)} %get-tuple-element.68), channel_id=1, source_target_pairs={{0,4},{4,0},{8,12},{12,8},{16,20},{20,16},{24,28},{28,24},{32,36},... | collective-permute-start | bytes 1966088 | tf_op jit(solution)/shard_map/ppermute | solution.py:31
  7.9 2.4 %far_states.1 = (bf16[2,512,1280]{2,1,0:T(8,128)(2,1)S(1)}, f32[4,6,8,1280]{3,2,1,0:T(8,128)S(1)}, f32[4,6,8,1280]{3,2,1,0:T(8,128)S(1)}) custom-call(bf16[128,512]{1,0:T(8,128)(2,1)S(1)} %get-tuple-element.64.qt, bf16[512,1280]{1,0:T(8,128)(2,1)S(1)} %get-tuple-element.81.v_ref, bf16[512,1280]{1,0:T(8,128)(2,1)S(1)} %get-tuple-element.65.e_ref, ...), custom_call_target="tpu_custom_call" | custom-call | flops 1024 | bytes 1024 | tf_op jit(solution)/shard_map/far_states/pallas_call | solution.py:162
  10.4 2.6 %rest_states.1 = (bf16[2,512,1280]{2,1,0:T(8,128)(2,1)S(1)}, f32[4,6,8,1280]{3,2,1,0:T(8,128)S(1)}, f32[4,6,8,1280]{3,2,1,0:T(8,128)S(1)}, f32[128,1280]{1,0:T(8,128)S(1)}) custom-call(bf16[128,512]{1,0:T(8,128)(2,1)S(1)} %get-tuple-element.64.qt, bf16[512,1280]{1,0:T(8,128)(2,1)S(1)} %get-tuple-element.81.v_ref, ...), custom_call_target="tpu_custom_call" | custom-call | flops 1024 | bytes 1024 | tf_op jit(solution)/shard_map/rest_states/pallas_call | solution.py:196
  16.6 2.2 %collective-permute-start.4 = (f32[6,8,1280]{2,1,0:T(8,128)S(1)}, f32[6,8,1280]{2,1,0:T(8,128)S(1)}, u32[]{:S(2)}, u32[]{:S(2)}) collective-permute-start(f32[6,8,1280]{2,1,0:T(8,128)S(1)} %get-tuple-element.78), channel_id=1, source_target_pairs={{0,16},{4,20},{8,24},{12,28},{16,0},{20,4},{24,8},{28,12},{32,48},... | collective-permute-start | bytes 737288 | tf_op jit(solution)/shard_map/ppermute | solution.py:31
  18.8 1.6 %collective-permute-start.5 = (f32[6,8,1280]{2,1,0:T(8,128)S(1)}, f32[6,8,1280]{2,1,0:T(8,128)S(1)}, u32[]{:S(2)}, u32[]{:S(2)}) collective-permute-start(f32[6,8,1280]{2,1,0:T(8,128)S(1)} %get-tuple-element.79), channel_id=1, source_target_pairs={{0,24},{4,28},{8,16},{12,20},{16,8},{20,12},{24,0},{28,4},{32,56},... | collective-permute-start | bytes 737288 | tf_op jit(solution)/shard_map/ppermute | solution.py:31
  20.4 8.1 %local_part.1 = (f32[512,1280]{1,0:T(8,128)S(1)}, f32[512,1280]{1,0:T(8,128)S(1)}, f32[512,128]{1,0:T(8,128)S(1)}) custom-call(bf16[512,128]{1,0:T(8,128)(2,1)S(1)} %get-tuple-element.80.q_ref, bf16[512,1280]{1,0:T(8,128)(2,1)S(1)} %get-tuple-element.81.v_ref, bf16[512,1280]{1,0:T(8,128)(2,1)S(1)} %get-tuple-element.65.e_ref, ...), custom_call_target="tpu_custom_call" | custom-call | flops 1024 | bytes 1024 | tf_op jit(solution)/shard_map/local_part/pallas_call | solution.py:301
  28.6 5.6 %collective-permute-done.4 = f32[6,8,1280]{2,1,0:T(8,128)S(1)} collective-permute-done((f32[6,8,1280]{2,1,0:T(8,128)S(1)}, f32[6,8,1280]{2,1,0:T(8,128)S(1)}, u32[]{:S(2)}, u32[]{:S(2)}) %collective-permute-start.4) | collective-permute-done | bytes 245792 | tf_op jit(solution)/shard_map/ppermute | solution.py:31
  34.2 2.0 %collective-permute-start.8 = (f32[4,8,1280]{2,1,0:T(8,128)S(1)}, f32[4,8,1280]{2,1,0:T(8,128)S(1)}, u32[]{:S(2)}, u32[]{:S(2)}) collective-permute-start(f32[4,8,1280]{2,1,0:T(8,128)S(1)} %slice_add_fusion.6), channel_id=1, source_target_pairs={{0,32},{4,36},{8,40},{12,44},{16,48},{20,52},{24,56},{28,60},{32,0... | collective-permute-start | bytes 491528 | tf_op jit(solution)/shard_map/ppermute | solution.py:31
  36.2 3.2 %collective-permute-done.8 = f32[4,8,1280]{2,1,0:T(8,128)S(1)} collective-permute-done((f32[4,8,1280]{2,1,0:T(8,128)S(1)}, f32[4,8,1280]{2,1,0:T(8,128)S(1)}, u32[]{:S(2)}, u32[]{:S(2)}) %collective-permute-start.8) | collective-permute-done | bytes 163872 | tf_op jit(solution)/shard_map/ppermute | solution.py:31
  39.4 7.0 %collective-permute-start.10 = (f32[8,1280]{1,0:T(8,128)S(1)}, f32[8,1280]{1,0:T(8,128)S(1)}, u32[]{:S(2)}, u32[]{:S(2)}) collective-permute-start(f32[8,1280]{1,0:T(8,128)S(1)} %get-tuple-element.130), channel_id=1, source_target_pairs={{0,128},{4,132},{8,136},{12,140},{16,144},{20,148},{24,152},{28,15... | collective-permute-start | bytes 122888 | tf_op jit(solution)/shard_map/ppermute | solution.py:31
  48.5 2.9 %collective-permute-done.11 = f32[8,1280]{1,0:T(8,128)S(1)} collective-permute-done((f32[8,1280]{1,0:T(8,128)S(1)}, f32[8,1280]{1,0:T(8,128)S(1)}, u32[]{:S(2)}, u32[]{:S(2)}) %collective-permute-start.11) | collective-permute-done | bytes 40992 | tf_op jit(solution)/shard_map/ppermute | solution.py:31
  52.8 2.4 %collective-permute-done.12 = f32[2,8,1280]{2,1,0:T(8,128)S(1)} collective-permute-done((f32[2,8,1280]{2,1,0:T(8,128)S(1)}, f32[2,8,1280]{2,1,0:T(8,128)S(1)}, u32[]{:S(2)}, u32[]{:S(2)}) %collective-permute-start.12) | collective-permute-done | bytes 81952 | tf_op jit(solution)/shard_map/ppermute | solution.py:31
  55.4 4.4 %collective-permute-start.16 = (f32[2,64,1280]{2,1,0:T(8,128)S(1)}, f32[2,64,1280]{2,1,0:T(8,128)S(1)}, u32[]{:S(2)}, u32[]{:S(2)}) collective-permute-start(f32[2,64,1280]{2,1,0:T(8,128)S(1)} %pad_maximum_fusion), channel_id=1, source_target_pairs={{0,4},{4,0},{8,12},{12,8},{16,20},{20,16},{24,28},{28,24},{32,36},... | collective-permute-start | bytes 1966088 | tf_op jit(solution)/shard_map/ppermute | solution.py:31
  61.6 1.5 %collective-permute-start.17 = (f32[6,8,1280]{2,1,0:T(8,128)S(1)}, f32[6,8,1280]{2,1,0:T(8,128)S(1)}, u32[]{:S(2)}, u32[]{:S(2)}) collective-permute-start(f32[6,8,1280]{2,1,0:T(8,128)S(1)} %pad_maximum_fusion.2.refs_3_), channel_id=1, source_target_pairs={{0,16},{4,20},{8,24},{12,28},{16,0},{20,4},{24,8},{28,12},{32,48},... | collective-permute-start | bytes 737288 | tf_op jit(solution)/shard_map/ppermute | solution.py:31
  64.0 2.4 %mid_part.1 = (f32[512,1280]{1,0:T(8,128)S(1)}, f32[512,1280]{1,0:T(8,128)S(1)}, f32[512,128]{1,0:T(8,128)S(1)}) custom-call(bf16[512,128]{1,0:T(8,128)(2,1)S(1)} %get-tuple-element.80.q_ref, f32[10,8,1280]{2,1,0:T(8,128)S(1)} %get-tuple-element.66.w_ref, f32[512,1280]{1,0:T(8,128)S(1)} %get-tuple-element.93.m_in, ...), custom_call_target="tpu_custom_call", output_to_operand_aliasing={{0}: (2, {}), {1}: (3, {})} | custom-call | flops 1024 | bytes 1024 | tf_op jit(solution)/shard_map/mid_part/pallas_call | solution.py:338
  67.3 2.1 %collective-permute-done.15.refs_6_ = f32[6,8,1280]{2,1,0:T(8,128)S(1)} collective-permute-done((f32[6,8,1280]{2,1,0:T(8,128)S(1)}, f32[6,8,1280]{2,1,0:T(8,128)S(1)}, u32[]{:S(2)}, u32[]{:S(2)}) %collective-permute-start.15) | collective-permute-done | bytes 245792 | tf_op jit(solution)/shard_map/ppermute | solution.py:31
  69.5 6.0 %collective-permute-start.19 = (f32[6,8,1280]{2,1,0:T(8,128)S(1)}, f32[6,8,1280]{2,1,0:T(8,128)S(1)}, u32[]{:S(2)}, u32[]{:S(2)}) collective-permute-start(f32[6,8,1280]{2,1,0:T(8,128)S(1)} %collective-permute-done.14.refs_4_), channel_id=1, source_target_pairs={{0,4},{4,0},{8,12},{12,8},{16,20},{20,16},{24,28},{28,24},{32,36},... | collective-permute-start | bytes 737288 | tf_op jit(solution)/shard_map/ppermute | solution.py:31
  79.8 1.6 %collective-permute-start.22 = (f32[256,128]{1,0:T(8,128)S(1)}, f32[256,128]{1,0:T(8,128)S(1)}, u32[]{:S(2)}, u32[]{:S(2)}) collective-permute-start(f32[256,128]{1,0:T(8,128)S(1)} %get-tuple-element.109), channel_id=1, source_target_pairs={{0,1},{1,0},{2,3},{3,2},{4,5},{5,4},{6,7},{7,6},{8,9},{9,8},{10,11... | collective-permute-start | bytes 393224 | tf_op jit(solution)/shard_map/ppermute | solution.py:31
  81.4 1.9 %collective-permute-start.23 = (f32[256,128]{1,0:T(8,128)S(1)}, f32[256,128]{1,0:T(8,128)S(1)}, u32[]{:S(2)}, u32[]{:S(2)}) collective-permute-start(f32[256,128]{1,0:T(8,128)S(1)} %get-tuple-element.110), channel_id=1, source_target_pairs={{0,3},{1,2},{2,1},{3,0},{4,7},{5,6},{6,5},{7,4},{8,11},{9,10},{10,... | collective-permute-start | bytes 393224 | tf_op jit(solution)/shard_map/ppermute | solution.py:31
  83.3 1.6 %last_values.1 = bf16[512,1280]{1,0:T(8,128)(2,1)} custom-call(bf16[512,128]{1,0:T(8,128)(2,1)S(1)} %get-tuple-element.80.q_ref, f32[512,1280]{1,0:T(8,128)S(1)} %get-tuple-element.111.d_in, f32[3,128,1280]{2,1,0:T(8,128)S(1)} %get-tuple-element.112.y_ref), custom_call_target="tpu_custom_call" | custom-call | flops 1024 | bytes 1024 | tf_op jit(solution)/shard_map/last_values/pallas_call | solution.py:398
  84.9 2.1 %collective-permute-done.23 = f32[256,128]{1,0:T(8,128)S(1)} collective-permute-done((f32[256,128]{1,0:T(8,128)S(1)}, f32[256,128]{1,0:T(8,128)S(1)}, u32[]{:S(2)}, u32[]{:S(2)}) %collective-permute-start.23) | collective-permute-done | bytes 131104 | tf_op jit(solution)/shard_map/ppermute | solution.py:31
  87.0 2.0 %collective-permute-start.24 = (f32[256,128]{1,0:T(8,128)S(1)}, f32[256,128]{1,0:T(8,128)S(1)}, u32[]{:S(2)}, u32[]{:S(2)}) collective-permute-start(f32[256,128]{1,0:T(8,128)S(1)} %add.126), channel_id=1, source_target_pairs={{0,3},{1,2},{2,1},{3,0},{4,7},{5,6},{6,5},{7,4},{8,11},{9,10},{10,... | collective-permute-start | bytes 393224 | tf_op jit(solution)/shard_map/ppermute | solution.py:31
  89.0 2.2 %last_mixed.1 = bf16[512,1280]{1,0:T(8,128)(2,1)} custom-call(bf16[512,128]{1,0:T(8,128)(2,1)S(1)} %get-tuple-element.80.q_ref, f32[10,8,1280]{2,1,0:T(8,128)S(1)} %get-tuple-element.66.w_ref, f32[512,1280]{1,0:T(8,128)S(1)} %get-tuple-element.118.m_in, f32[3,128,1280]{2,1,0:T(8,128)S(1)} %get-tuple-element.112.y_ref), custom_call_target="tpu_custom_call" | custom-call | flops 1024 | bytes 1024 | tf_op jit(solution)/shard_map/last_mixed/pallas_call | solution.py:423
  (51 shorter events, 18.0 us)
Async XLA Ops:
  4.7 5.7 %collective-permute-start = (f32[2,64,1280]{2,1,0:T(8,128)S(1)}, f32[2,64,1280]{2,1,0:T(8,128)S(1)}, u32[]{:S(2)}, u32[]{:S(2)}) collective-permute-start(f32[2,64,1280]{2,1,0:T(8,128)S(1)} %get-tuple-element.68), channel_id=1, source_target_pairs={{0,4},{4,0},{8,12},{12,8},{16,20},{20,16},{24,28},{28,24},{32,36},... | collective-permute-start | bytes 1966088 | tf_op jit(solution)/shard_map/ppermute | solution.py:31
  13.0 2.7 %collective-permute-start.1 = (f32[4,6,8,1280]{3,2,1,0:T(8,128)S(1)}, f32[4,6,8,1280]{3,2,1,0:T(8,128)S(1)}, u32[]{:S(2)}, u32[]{:S(2)}) collective-permute-start(f32[4,6,8,1280]{3,2,1,0:T(8,128)S(1)} %get-tuple-element.74), channel_id=1, source_target_pairs={{0,4},{4,0},{8,12},{12,8},{16,20},{20,16},{24,28},{28,24},{32,36},... | collective-permute-start | bytes 2949128 | tf_op jit(solution)/shard_map/ppermute | solution.py:31
  13.1 3.5 %collective-permute-start.2 = (f32[128,1280]{1,0:T(8,128)S(1)}, f32[128,1280]{1,0:T(8,128)S(1)}, u32[]{:S(2)}, u32[]{:S(2)}) collective-permute-start(f32[128,1280]{1,0:T(8,128)S(1)} %get-tuple-element.75), channel_id=1, source_target_pairs={{0,4},{4,0},{8,12},{12,8},{16,20},{20,16},{24,28},{28,24},{32,36},... | collective-permute-start | bytes 1966088 | tf_op jit(solution)/shard_map/ppermute | solution.py:31
  13.6 15.0 %collective-permute-start.6 = (f32[64,1280]{1,0:T(8,128)S(1)}, f32[64,1280]{1,0:T(8,128)S(1)}, u32[]{:S(2)}, u32[]{:S(2)}) collective-permute-start(f32[64,1280]{1,0:T(8,128)S(1)} %get-tuple-element.85), channel_id=1, source_target_pairs={{0,8},{4,12},{8,0},{12,4},{16,24},{20,28},{24,16},{28,20},{32,40},... | collective-permute-start | bytes 983048 | tf_op jit(solution)/shard_map/ppermute | solution.py:31
  13.6 15.0 %collective-permute-start.7 = (f32[64,1280]{1,0:T(8,128)S(1)}, f32[64,1280]{1,0:T(8,128)S(1)}, u32[]{:S(2)}, u32[]{:S(2)}) collective-permute-start(f32[64,1280]{1,0:T(8,128)S(1)} %get-tuple-element.91), channel_id=1, source_target_pairs={{0,24},{4,28},{8,16},{12,20},{16,8},{20,12},{24,0},{28,4},{32,56},... | collective-permute-start | bytes 983048 | tf_op jit(solution)/shard_map/ppermute | solution.py:31
  16.6 12.0 %collective-permute-start.3 = (f32[6,8,1280]{2,1,0:T(8,128)S(1)}, f32[6,8,1280]{2,1,0:T(8,128)S(1)}, u32[]{:S(2)}, u32[]{:S(2)}) collective-permute-start(f32[6,8,1280]{2,1,0:T(8,128)S(1)} %get-tuple-element.77), channel_id=1, source_target_pairs={{0,8},{4,12},{8,0},{12,4},{16,24},{20,28},{24,16},{28,20},{32,40},... | collective-permute-start | bytes 737288 | tf_op jit(solution)/shard_map/ppermute | solution.py:31
  16.6 17.6 %collective-permute-start.4 = (f32[6,8,1280]{2,1,0:T(8,128)S(1)}, f32[6,8,1280]{2,1,0:T(8,128)S(1)}, u32[]{:S(2)}, u32[]{:S(2)}) collective-permute-start(f32[6,8,1280]{2,1,0:T(8,128)S(1)} %get-tuple-element.78), channel_id=1, source_target_pairs={{0,16},{4,20},{8,24},{12,28},{16,0},{20,4},{24,8},{28,12},{32,48},... | collective-permute-start | bytes 737288 | tf_op jit(solution)/shard_map/ppermute | solution.py:31
  18.8 15.4 %collective-permute-start.5 = (f32[6,8,1280]{2,1,0:T(8,128)S(1)}, f32[6,8,1280]{2,1,0:T(8,128)S(1)}, u32[]{:S(2)}, u32[]{:S(2)}) collective-permute-start(f32[6,8,1280]{2,1,0:T(8,128)S(1)} %get-tuple-element.79), channel_id=1, source_target_pairs={{0,24},{4,28},{8,16},{12,20},{16,8},{20,12},{24,0},{28,4},{32,56},... | collective-permute-start | bytes 737288 | tf_op jit(solution)/shard_map/ppermute | solution.py:31
  34.2 5.2 %collective-permute-start.8 = (f32[4,8,1280]{2,1,0:T(8,128)S(1)}, f32[4,8,1280]{2,1,0:T(8,128)S(1)}, u32[]{:S(2)}, u32[]{:S(2)}) collective-permute-start(f32[4,8,1280]{2,1,0:T(8,128)S(1)} %slice_add_fusion.6), channel_id=1, source_target_pairs={{0,32},{4,36},{8,40},{12,44},{16,48},{20,52},{24,56},{28,60},{32,0... | collective-permute-start | bytes 491528 | tf_op jit(solution)/shard_map/ppermute | solution.py:31
  39.4 9.1 %collective-permute-start.10 = (f32[8,1280]{1,0:T(8,128)S(1)}, f32[8,1280]{1,0:T(8,128)S(1)}, u32[]{:S(2)}, u32[]{:S(2)}) collective-permute-start(f32[8,1280]{1,0:T(8,128)S(1)} %get-tuple-element.130), channel_id=1, source_target_pairs={{0,128},{4,132},{8,136},{12,140},{16,144},{20,148},{24,152},{28,15... | collective-permute-start | bytes 122888 | tf_op jit(solution)/shard_map/ppermute | solution.py:31
  46.4 5.1 %collective-permute-start.11 = (f32[8,1280]{1,0:T(8,128)S(1)}, f32[8,1280]{1,0:T(8,128)S(1)}, u32[]{:S(2)}, u32[]{:S(2)}) collective-permute-start(f32[8,1280]{1,0:T(8,128)S(1)} %get-tuple-element.130), channel_id=1, source_target_pairs={{0,192},{4,196},{8,200},{12,204},{16,208},{20,212},{24,216},{28,22... | collective-permute-start | bytes 122888 | tf_op jit(solution)/shard_map/ppermute | solution.py:31
  46.4 8.9 %collective-permute-start.13 = (f32[64,1280]{1,0:T(8,128)S(1)}, f32[64,1280]{1,0:T(8,128)S(1)}, u32[]{:S(2)}, u32[]{:S(2)}) collective-permute-start(f32[64,1280]{1,0:T(8,128)S(1)} %get-tuple-element.91), channel_id=1, source_target_pairs={{0,16},{4,20},{8,24},{12,28},{16,0},{20,4},{24,8},{28,12},{32,48},... | collective-permute-start | bytes 983048 | tf_op jit(solution)/shard_map/ppermute | solution.py:31
  47.2 4.2 %collective-permute-start.9 = (f32[8,1280]{1,0:T(8,128)S(1)}, f32[8,1280]{1,0:T(8,128)S(1)}, u32[]{:S(2)}, u32[]{:S(2)}) collective-permute-start(f32[8,1280]{1,0:T(8,128)S(1)} %get-tuple-element.129), channel_id=1, source_target_pairs={{0,64},{4,68},{8,72},{12,76},{16,80},{20,84},{24,88},{28,92},{32,9... | collective-permute-start | bytes 122888 | tf_op jit(solution)/shard_map/ppermute | solution.py:31
  51.5 3.8 %collective-permute-start.12 = (f32[2,8,1280]{2,1,0:T(8,128)S(1)}, f32[2,8,1280]{2,1,0:T(8,128)S(1)}, u32[]{:S(2)}, u32[]{:S(2)}) collective-permute-start(f32[2,8,1280]{2,1,0:T(8,128)S(1)} %pad_maximum_fusion.3), channel_id=1, source_target_pairs={{0,32},{4,36},{8,40},{12,44},{16,48},{20,52},{24,56},{28,60},{32,0... | collective-permute-start | bytes 245768 | tf_op jit(solution)/shard_map/ppermute | solution.py:31
  55.4 8.6 %collective-permute-start.16 = (f32[2,64,1280]{2,1,0:T(8,128)S(1)}, f32[2,64,1280]{2,1,0:T(8,128)S(1)}, u32[]{:S(2)}, u32[]{:S(2)}) collective-permute-start(f32[2,64,1280]{2,1,0:T(8,128)S(1)} %pad_maximum_fusion), channel_id=1, source_target_pairs={{0,4},{4,0},{8,12},{12,8},{16,20},{20,16},{24,28},{28,24},{32,36},... | collective-permute-start | bytes 1966088 | tf_op jit(solution)/shard_map/ppermute | solution.py:31
  59.8 7.5 %collective-permute-start.14 = (f32[6,8,1280]{2,1,0:T(8,128)S(1)}, f32[6,8,1280]{2,1,0:T(8,128)S(1)}, u32[]{:S(2)}, u32[]{:S(2)}) collective-permute-start(f32[6,8,1280]{2,1,0:T(8,128)S(1)} %pad_maximum_fusion.2.refs_3_), channel_id=1, source_target_pairs={{0,8},{4,12},{8,0},{12,4},{16,24},{20,28},{24,16},{28,20},{32,40},... | collective-permute-start | bytes 737288 | tf_op jit(solution)/shard_map/ppermute | solution.py:31
  60.6 8.9 %collective-permute-start.15 = (f32[6,8,1280]{2,1,0:T(8,128)S(1)}, f32[6,8,1280]{2,1,0:T(8,128)S(1)}, u32[]{:S(2)}, u32[]{:S(2)}) collective-permute-start(f32[6,8,1280]{2,1,0:T(8,128)S(1)} %pad_maximum_fusion.2.refs_3_), channel_id=1, source_target_pairs={{0,24},{4,28},{8,16},{12,20},{16,8},{20,12},{24,0},{28,4},{32,56},... | collective-permute-start | bytes 737288 | tf_op jit(solution)/shard_map/ppermute | solution.py:31
  61.6 13.8 %collective-permute-start.17 = (f32[6,8,1280]{2,1,0:T(8,128)S(1)}, f32[6,8,1280]{2,1,0:T(8,128)S(1)}, u32[]{:S(2)}, u32[]{:S(2)}) collective-permute-start(f32[6,8,1280]{2,1,0:T(8,128)S(1)} %pad_maximum_fusion.2.refs_3_), channel_id=1, source_target_pairs={{0,16},{4,20},{8,24},{12,28},{16,0},{20,4},{24,8},{28,12},{32,48},... | collective-permute-start | bytes 737288 | tf_op jit(solution)/shard_map/ppermute | solution.py:31
  63.1 12.3 %collective-permute-start.18 = (f32[6,8,1280]{2,1,0:T(8,128)S(1)}, f32[6,8,1280]{2,1,0:T(8,128)S(1)}, u32[]{:S(2)}, u32[]{:S(2)}) collective-permute-start(f32[6,8,1280]{2,1,0:T(8,128)S(1)} %pad_maximum_fusion.2.refs_3_), channel_id=1, source_target_pairs={{0,4},{4,0},{8,12},{12,8},{16,20},{20,16},{24,28},{28,24},{32,36},... | collective-permute-start | bytes 737288 | tf_op jit(solution)/shard_map/ppermute | solution.py:31
  69.5 7.1 %collective-permute-start.19 = (f32[6,8,1280]{2,1,0:T(8,128)S(1)}, f32[6,8,1280]{2,1,0:T(8,128)S(1)}, u32[]{:S(2)}, u32[]{:S(2)}) collective-permute-start(f32[6,8,1280]{2,1,0:T(8,128)S(1)} %collective-permute-done.14.refs_4_), channel_id=1, source_target_pairs={{0,4},{4,0},{8,12},{12,8},{16,20},{20,16},{24,28},{28,24},{32,36},... | collective-permute-start | bytes 737288 | tf_op jit(solution)/shard_map/ppermute | solution.py:31
  79.8 5.1 %collective-permute-start.22 = (f32[256,128]{1,0:T(8,128)S(1)}, f32[256,128]{1,0:T(8,128)S(1)}, u32[]{:S(2)}, u32[]{:S(2)}) collective-permute-start(f32[256,128]{1,0:T(8,128)S(1)} %get-tuple-element.109), channel_id=1, source_target_pairs={{0,1},{1,0},{2,3},{3,2},{4,5},{5,4},{6,7},{7,6},{8,9},{9,8},{10,11... | collective-permute-start | bytes 393224 | tf_op jit(solution)/shard_map/ppermute | solution.py:31
  81.4 5.6 %collective-permute-start.23 = (f32[256,128]{1,0:T(8,128)S(1)}, f32[256,128]{1,0:T(8,128)S(1)}, u32[]{:S(2)}, u32[]{:S(2)}) collective-permute-start(f32[256,128]{1,0:T(8,128)S(1)} %get-tuple-element.110), channel_id=1, source_target_pairs={{0,3},{1,2},{2,1},{3,0},{4,7},{5,6},{6,5},{7,4},{8,11},{9,10},{10,... | collective-permute-start | bytes 393224 | tf_op jit(solution)/shard_map/ppermute | solution.py:31
  87.0 5.1 %collective-permute-start.24 = (f32[256,128]{1,0:T(8,128)S(1)}, f32[256,128]{1,0:T(8,128)S(1)}, u32[]{:S(2)}, u32[]{:S(2)}) collective-permute-start(f32[256,128]{1,0:T(8,128)S(1)} %add.126), channel_id=1, source_target_pairs={{0,3},{1,2},{2,1},{3,0},{4,7},{5,6},{6,5},{7,4},{8,11},{9,10},{10,... | collective-permute-start | bytes 393224 | tf_op jit(solution)/shard_map/ppermute | solution.py:31
  89.0 4.1 %collective-permute-start.25 = (f32[256,128]{1,0:T(8,128)S(1)}, f32[256,128]{1,0:T(8,128)S(1)}, u32[]{:S(2)}, u32[]{:S(2)}) collective-permute-start(f32[256,128]{1,0:T(8,128)S(1)} %add.127), channel_id=1, source_target_pairs={{0,1},{1,0},{2,3},{3,2},{4,5},{5,4},{6,7},{7,6},{8,9},{9,8},{10,11... | collective-permute-start | bytes 393224 | tf_op jit(solution)/shard_map/ppermute | solution.py:31
  (2 other events, 3.0 us)

commit v4 on v3

v4 whole, which is shorter than its diff:
```python
import functools

import jax
import jax.numpy as jnp
from jax import lax
from jax.experimental import pallas as pl
from jax.experimental.pallas import tpu as pltpu
from jax.sharding import PartitionSpec as P

HEAD_DIM = 64
CH = 64
TOK = 512
STATE = 128
COLS = 1280
HEADS = COLS // HEAD_DIM
BLK = 256
STEPS = COLS // BLK
SPANS = TOK // CH
USED = 10
TILE = 256
FIRST = 3
BF = jnp.bfloat16
F32 = jnp.float32
ROW, CORE, XMASK = 8, 1, 3
BLOCKS = tuple(slice(j * BLK, (j + 1) * BLK) for j in range(STEPS))

LOCAL = ((0, 0, 0), (0, 0, 1), (0, 0, 2), (1, 1, 0), (1, 1, 1), (1, 1, 2), (1, 0, 3))


def send(value, even, odd=None):
    odd = even if odd is None else odd
    pairs = [(source, source ^ (odd if source & CORE else even)) for source in range(lax.axis_size("seq"))]
    return lax.ppermute(value, "seq", pairs)


def send_head(value, even, odd):
    heads = lax.axis_size("head")
    pairs = []
    for source in range(lax.axis_size("seq")):
        for group in range(heads):
            target = group ^ (odd if source & CORE else even)
            pairs.append((source * heads + group, source * heads + target))
    return lax.ppermute(value, ("seq", "head"), pairs)


def neighbour(slot, core):
    return (slot * (1 + 2 * core)) & XMASK


def dot(a, b, over_a, over_b):
    return lax.dot_general(a, b, (((over_a,), (over_b,)), ((), ())), preferred_element_type=F32)


def coords():
    position = lax.axis_index("seq")
    return position, position & CORE, (position >> 1) & XMASK, (position >> 3) & CORE


def params(mib):
    return pltpu.CompilerParams(vmem_limit_bytes=mib * 1024 * 1024)


def cost():
    return pl.CostEstimate(flops=1024, bytes_accessed=1024, transcendentals=0)


def shape(*dims, kind=F32):
    return jax.ShapeDtypeStruct(dims, kind)


VMEM = pl.BlockSpec(memory_space=pltpu.VMEM)
SMEM = pl.BlockSpec(memory_space=pltpu.SMEM)
HBM = pl.BlockSpec(memory_space=pltpu.HBM)


def level_operand(z_ref, index, k, position, w_ref, v_ref, e_ref, block):
    upper = (position >> (k - 1)) & 1

    @pl.when(upper == 1)
    def _():
        for a in range(SPANS):
            rows = slice(a * CH, (a + 1) * CH)
            scaled = w_ref[k + 3, a : a + 1, block] * e_ref[rows, block].astype(F32)
            z_ref[index, rows, block] = scaled.astype(BF)

    @pl.when(upper == 0)
    def _():
        z_ref[index, :, block] = v_ref[:, block]


def far_kernel(
    code_hbm, gain_hbm, q_hbm, v_hbm, e_hbm, w_ref, q_ref, qt, v_ref, e_ref, z_ref, own_ref, oth_ref,
    code_ref, gain_ref, lw, res, sems
):
    position, core, x, z0 = coords()
    first = []
    for i, (far, near) in enumerate(((code_hbm, code_ref), (gain_hbm, gain_ref), (q_hbm, q_ref))):
        copy = pltpu.make_async_copy(far, near, sems.at[2 * STEPS + i])
        copy.start()
        first.append(copy)
    copies = []
    for j, block in enumerate(BLOCKS):
        for i, (far, near) in enumerate(((v_hbm, v_ref), (e_hbm, e_ref))):
            copy = pltpu.make_async_copy(far.at[:, block], near.at[:, block], sems.at[2 * j + i])
            copy.start()
            copies.append(copy)
    lw[...] = jnp.zeros_like(lw)
    for copy in first:
        copy.wait()
    for a in range(SPANS):
        lw[0:15, a : a + 1, 0:HEADS] = gain_ref[:, pl.ds(code_ref[a], 1), :]
    weights = lw[...].reshape(16 * SPANS, 128)[: USED * SPANS]
    high = weights.astype(BF)
    rest = weights - high.astype(F32)
    middle = rest.astype(BF)
    low = (rest - middle.astype(F32)).astype(BF)
    head = lax.broadcasted_iota(jnp.int32, (128, BLK), 0)
    for j, block in enumerate(BLOCKS):
        col = lax.broadcasted_iota(jnp.int32, (128, BLK), 1) + j * BLK
        spread = (head == col // HEAD_DIM).astype(BF)
        wide = dot(high, spread, 1, 0) + (dot(middle, spread, 1, 0) + dot(low, spread, 1, 0))
        w_ref[:, :, block] = wide.reshape(USED, SPANS, BLK)
    qt[...] = q_ref[...].T
    for j, block in enumerate(BLOCKS):
        copies[2 * j].wait()
        copies[2 * j + 1].wait()
        for index, k in enumerate((6, 4, 5)):
            level_operand(z_ref, index, k, position, w_ref, v_ref, e_ref, block)
            res[...] = dot(qt[...], z_ref[index, :, block], 1, 0).reshape(8, 2, ROW, BLK)
            for xr in range(4):
                for zr in range(2):
                    half = zr ^ z0 if k == 6 else zr
                    own_place = (core << 2) | (neighbour(xr, core) ^ x)
                    oth_place = ((core ^ 1) << 2) | (neighbour(xr, core ^ 1) ^ x)
                    own_ref[xr, 2 * index + zr, :, block] = res[own_place, half]
                    oth_ref[xr, 2 * index + zr, :, block] = res[oth_place, half]


def far_states(code, gain, q, v, e):
    return pl.pallas_call(
        far_kernel,
        in_specs=[HBM] * 5,
        out_specs=[VMEM] * 8,
        out_shape=[
            shape(USED, SPANS, COLS),
            shape(TOK, STATE, kind=BF),
            shape(STATE, TOK, kind=BF),
            shape(TOK, COLS, kind=BF),
            shape(TOK, COLS, kind=BF),
            shape(3, TOK, COLS, kind=BF),
            shape(4, 6, ROW, COLS),
            shape(4, 6, ROW, COLS),
        ],
        scratch_shapes=[
            pltpu.SMEM((SPANS,), jnp.int32),
            pltpu.VMEM((15, 16, HEADS), F32),
            pltpu.VMEM((16, SPANS, 128), F32),
            pltpu.VMEM((8, 2, ROW, BLK), F32),
            pltpu.SemaphoreType.DMA((2 * STEPS + 3,)),
        ],
        compiler_params=params(20),
        cost_estimate=cost(),
        name="far_states",
    )(code, gain, q, v, e)


def near_kernel(qt, v_ref, e_ref, w_ref, z_ref, x_ref, own_ref, oth_ref, res):
    position, core, x, z0 = coords()
    for index, k in enumerate((2, 3, 1)):
        for block in BLOCKS:
            level_operand(z_ref, index, k, position, w_ref, v_ref, e_ref, block)
            out = dot(qt[...], z_ref[index, :, block], 1, 0)
            if k == 1:
                x_ref[:, block] = out
            else:
                res[...] = out.reshape(2, STATE // 2, BLK)
                own_ref[index, :, block] = res[core]
                oth_ref[index, :, block] = res[core ^ 1]


def near_states(qt, v, e, w):
    half = STATE // 2
    return pl.pallas_call(
        near_kernel,
        in_specs=[VMEM] * 4,
        out_specs=[VMEM] * 4,
        out_shape=[
            shape(3, TOK, COLS, kind=BF),
            shape(STATE, COLS),
            shape(2, half, COLS),
            shape(2, half, COLS),
        ],
        scratch_shapes=[pltpu.VMEM((2, half, BLK), F32)],
        compiler_params=params(20),
        cost_estimate=cost(),
        name="near_states",
    )(qt, v, e, w)


def kept(level, flip):
    rows = lax.broadcasted_iota(jnp.int32, (TILE, TILE), 1 if flip else 0)
    keys = lax.broadcasted_iota(jnp.int32, (TILE, TILE), 0 if flip else 1)
    a, b = rows // CH, keys // CH
    if level == 0:
        return (a == b) & (keys <= rows)
    return ((a ^ b) >> (level - 1) == 1) & (a > b)


def add_outer(q_ref, w_ref, levels, position, y_ref, m_ref, d_ref, block):
    for index, k in enumerate(levels):

        @pl.when((position >> (k - 1)) & 1 == 1)
        def _():
            out = dot(q_ref[...], y_ref[index, :, block].astype(BF), 1, 0)
            for a in range(SPANS):
                rows = slice(a * CH, (a + 1) * CH)
                m_ref[rows, block] += w_ref[k + 3, a : a + 1, block] * out[rows, :]

    lower = None
    for index, k in enumerate(levels):
        part = (1 - ((position >> (k - 1)) & 1)).astype(F32) * y_ref[index, :, block]
        lower = part if lower is None else lower + part
    d_ref[:, block] += dot(q_ref[...], lower.astype(BF), 1, 0)


def local_blocks(first, count, q_ref, v_ref, e_ref, w_ref, score, flipped, m_ref, d_ref, dq_ref, grad, z):
    grad[...] = jnp.zeros_like(grad)
    per = TILE // CH

    def one_block(j, carry):
        block = pl.ds(pl.multiple_of((first + j) * BLK, BLK), BLK)
        out_block = pl.ds(pl.multiple_of(j * BLK, BLK), BLK)
        mixed = [None, None]
        d_val = [None, None]
        for index, (t, s, level) in enumerate(LOCAL):
            vals = v_ref[s * TILE : (s + 1) * TILE, block]
            for a in range(per):
                rows = slice(t * TILE + a * CH, t * TILE + (a + 1) * CH)
                w_row = w_ref[level, t * per + a : t * per + a + 1, block]
                z[index, a * CH : (a + 1) * CH, :] = (w_row * e_ref[rows, block].astype(F32)).astype(BF)
            out = dot(score[index], vals, 1, 0)
            w_rows = jnp.concatenate(
                [
                    jnp.broadcast_to(w_ref[level, t * per + a : t * per + a + 1, block], (CH, BLK))
                    for a in range(per)
                ],
                axis=0,
            )
            out = w_rows * out
            back = dot(flipped[index], z[index], 1, 0)
            mixed[t] = out if mixed[t] is None else mixed[t] + out
            d_val[s] = back if d_val[s] is None else d_val[s] + back
            grad[index] += dot(z[index], vals, 1, 1)
        for i in range(2):
            m_ref[i * TILE : (i + 1) * TILE, out_block] = mixed[i]
            d_ref[i * TILE : (i + 1) * TILE, out_block] = d_val[i]
        return carry

    lax.fori_loop(0, count, one_block, 0)
    q = [q_ref[i * TILE : (i + 1) * TILE, :] for i in range(2)]
    cross = grad[6].astype(BF)
    extra = [dot(cross, q[1], 0, 0), dot(cross, q[0], 1, 0)]
    for i in range(2):
        total = jnp.zeros((TILE, TILE), F32)
        for level in range(3):
            total = total + jnp.where(kept(level, False), grad[3 * i + level], 0.0)
        total = total.astype(BF)
        part = dot(total, q[i], 1, 0) + dot(total, q[i], 0, 0)
        dq_ref[i * TILE : (i + 1) * TILE, :] = part + extra[i]


def first_local_kernel(q_ref, v_ref, e_ref, w_ref, m_ref, d_ref, dq_ref, score, flipped, grad, z):
    for index, (t, s, level) in enumerate(LOCAL):
        qt_rows = q_ref[t * TILE : (t + 1) * TILE, :]
        qs_rows = q_ref[s * TILE : (s + 1) * TILE, :]
        direct = dot(qt_rows, qs_rows, 1, 1)
        swapped = dot(qs_rows, qt_rows, 1, 1)
        if level < 3:
            direct = jnp.where(kept(level, False), direct, 0.0)
            swapped = jnp.where(kept(level, True), swapped, 0.0)
        score[index] = direct.astype(BF)
        flipped[index] = swapped.astype(BF)
    local_blocks(0, FIRST, q_ref, v_ref, e_ref, w_ref, score, flipped, m_ref, d_ref, dq_ref, grad, z)


def other_local_kernel(q_ref, v_ref, e_ref, w_ref, score, flipped, m_ref, d_ref, dq_ref, grad, z):
    local_blocks(FIRST, STEPS - FIRST, q_ref, v_ref, e_ref, w_ref, score, flipped, m_ref, d_ref, dq_ref, grad, z)


def local_part(q, v, e, w, scores):
    wide = (STEPS - FIRST if scores else FIRST) * BLK
    kernel, name = (other_local_kernel, "other_local") if scores else (first_local_kernel, "first_local")
    table = shape(7, TILE, TILE, kind=BF)
    return pl.pallas_call(
        kernel,
        in_specs=[VMEM] * (4 + len(scores)),
        out_specs=[VMEM] * (5 - len(scores)),
        out_shape=[shape(TOK, wide), shape(TOK, wide), shape(TOK, STATE)] + [table] * (2 - len(scores)),
        scratch_shapes=[pltpu.VMEM((7, TILE, TILE), F32), pltpu.VMEM((7, TILE, BLK), BF)],
        compiler_params=params(20),
        cost_estimate=pl.CostEstimate(flops=1 << 33, bytes_accessed=1 << 25, transcendentals=0),
        name=name,
    )(q, v, e, w, *scores)


def mid_kernel(
    q_ref, w_ref, ma, da, dqa, mb, db, dqb, z_ref, y1_ref, y2_ref, y3_ref, y23o_ref, m_ref, d_ref, dq_ref, y
):
    position, core, x, z0 = coords()
    half = STATE // 2
    own = pl.ds(pl.multiple_of(core * half, half), half)
    oth = pl.ds(pl.multiple_of((core ^ 1) * half, half), half)
    for index, ref in enumerate((y2_ref, y3_ref)):
        y[index, own, :] = ref[...]
        y[index, oth, :] = y23o_ref[index]
    y[2] = y1_ref[...]
    grads = dqa[...] + dqb[...]
    m_ref[:, : FIRST * BLK] = ma[...]
    d_ref[:, : FIRST * BLK] = da[...]
    m_ref[:, FIRST * BLK :] = mb[...]
    d_ref[:, FIRST * BLK :] = db[...]
    for block in BLOCKS:
        add_outer(q_ref, w_ref, (2, 3, 1), position, y, m_ref, d_ref, block)
        for index in range(3):
            grads = grads + dot(z_ref[index, :, block], y[index, :, block].astype(BF), 1, 1)
    dq_ref[...] = grads


def mid_part(q, w, first, other, zn, y1, y2, y3, y23o):
    return pl.pallas_call(
        mid_kernel,
        in_specs=[VMEM] * 13,
        out_specs=[VMEM] * 3,
        out_shape=[shape(TOK, COLS), shape(TOK, COLS), shape(TOK, STATE)],
        scratch_shapes=[pltpu.VMEM((3, STATE, COLS), F32)],
        compiler_params=params(30),
        cost_estimate=cost(),
        name="mid_part",
    )(q, w, *first, *other, zn, y1, y2, y3, y23o)


def score_kernel(*refs):
    dq_in, zf_ref = refs[:2]
    pieces = refs[2:10]
    top_ref, low_ref, y = refs[10:]
    position, core, x, z0 = coords()
    for cr in range(2):
        for xr in range(4):
            piece = pieces[4 * cr + xr]
            place = ((cr ^ core) << 2) | (neighbour(xr, cr ^ core) ^ x)
            rows = pl.ds(pl.multiple_of(place * 16, 16), 16)
            y[0, rows, :] = jnp.concatenate([piece[z0], piece[1 - z0]], axis=0)
            y[1, rows, :] = piece[2:4].reshape(16, COLS)
            y[2, rows, :] = piece[4:6].reshape(16, COLS)
    grads = dq_in[...]
    for block in BLOCKS:
        for index in range(3):
            grads = grads + dot(zf_ref[index, :, block], y[index, :, block].astype(BF), 1, 1)
    top_ref[...] = grads[: TOK // 2]
    low_ref[...] = grads[TOK // 2 :]


def score_part(dq, zf, pieces):
    part = shape(TOK // 2, STATE)
    return pl.pallas_call(
        score_kernel,
        in_specs=[VMEM] * 10,
        out_specs=[VMEM] * 3,
        out_shape=[part, part, shape(3, STATE, COLS)],
        compiler_params=params(20),
        cost_estimate=cost(),
        name="score_part",
    )(dq, zf, *pieces)


def last_values_kernel(q_ref, d_in, y_ref, out_ref):
    position = lax.axis_index("seq")
    for block in BLOCKS:
        lower = None
        for index, k in enumerate((6, 4, 5)):
            part = (1 - ((position >> (k - 1)) & 1)).astype(F32) * y_ref[index, :, block]
            lower = part if lower is None else lower + part
        out_ref[:, block] = (d_in[:, block] + dot(q_ref[...], lower.astype(BF), 1, 0)).astype(BF)


def last_values(q, d, y):
    return pl.pallas_call(
        last_values_kernel,
        in_specs=[VMEM] * 3,
        out_specs=VMEM,
        out_shape=shape(TOK, COLS, kind=BF),
        compiler_params=params(20),
        cost_estimate=cost(),
        name="last_values",
    )(q, d, y)


def last_mixed_kernel(q_ref, w_ref, m_in, y_ref, out_ref):
    position = lax.axis_index("seq")
    for block in BLOCKS:
        outs = [dot(q_ref[...], y_ref[index, :, block].astype(BF), 1, 0) for index in range(3)]
        for a in range(SPANS):
            rows = slice(a * CH, (a + 1) * CH)
            total = m_in[rows, block]
            for index, k in enumerate((6, 4, 5)):
                upper = ((position >> (k - 1)) & 1).astype(F32)
                total = total + (upper * w_ref[k + 3, a : a + 1, block]) * outs[index][rows, :]
            out_ref[rows, block] = total.astype(BF)


def last_mixed(q, w, m, y):
    return pl.pallas_call(
        last_mixed_kernel,
        in_specs=[VMEM] * 4,
        out_specs=VMEM,
        out_shape=shape(TOK, COLS, kind=BF),
        compiler_params=params(20),
        cost_estimate=cost(),
        name="last_mixed",
    )(q, w, m, y)


def local(*args):
    tie = lax.optimization_barrier
    args = args[:3] + (args[3].transpose(1, 0, 2),) + args[4:]
    q_hbm, v_hbm, e_hbm, gain, code = [pltpu.with_memory_space_constraint(a, pltpu.HBM) for a in args]
    w, q, qt, v, e, zf, own_f, oth_f = far_states(code, gain, q_hbm, v_hbm, e_hbm)
    got_f = send(oth_f, 1)
    zn, x1, own_n, oth_n = near_states(qt, v, e, w)

    chip = [own_f[j] + got_f[j] for j in range(4)]
    chip, x1, oth_n = tie((chip, x1, oth_n))
    slices = [send(chip[j], 2 * j, 2 * (4 - j)) for j in (1, 2, 3)]
    got_n = send(oth_n, 1)
    y1 = send(x1, 1)
    near = [own_n[i] + got_n[i] for i in range(2)]
    slices, near, y1 = tie((slices, near, y1))
    mine = sum((s[0] for s in slices), chip[0][0])
    cross = sum((s[1:4] for s in slices), chip[0][1:4])
    pair = sum((s[4:6] for s in slices), chip[0][4:6])

    low = send(cross, 8)
    five = send(pair, 16)
    y2 = send(near[0], 2)
    y3 = [send(near[1], 6), send(near[1], 4)]
    six = mine + low[0]
    six, five, v2 = tie((six, five, v))
    y6 = [send(six, 32, 48), send(six, 48, 32)]
    *first, score, flipped = local_part(q, v2, e, w, ())
    half = jnp.concatenate([(y6[0] + y6[1])[None], five])
    half, score, v3 = tie((half, score, v2))
    rest = send(half, 8)
    other = local_part(q, v3, e, w, (score, flipped))
    rest, other = tie((rest, other))
    quad = jnp.concatenate([half[0:1], rest[0:1], low[1:3], half[1:3] + rest[1:3]])
    quad, other, y2, y3 = tie((quad, other, y2, y3))
    y3 = y3[0] + y3[1]
    y23o = send(jnp.stack([y2, y3]), 1)
    pieces = [quad] + [send(quad, 2 * j, 2 * (4 - j)) for j in (1, 2, 3)]
    m, d, dq = mid_part(q, w, first, other, zn, y1, y2, y3, y23o)
    for j in (1, 3, 2):
        pieces[j], dq = tie((pieces[j], dq))
    pieces = pieces + [send(p, 1) for p in pieces]
    top, low, y = score_part(dq, zf, pieces)
    got = [send_head(top, 1, 3), send_head(low, 3, 1)]
    grad_values = last_values(q, d, y)
    got, grad_values = tie((got, grad_values))
    top = top + got[0]
    low = low + got[1]
    top, low, m = tie((top, low, m))
    got = [send_head(top, 3, 1), send_head(low, 1, 3)]
    mixed = last_mixed(q, w, m, y)
    got, mixed = tie((got, mixed))
    grad_qk = jnp.concatenate([top + got[0], low + got[1]])
    return mixed, grad_qk, grad_values


def solution(mesh):
    placed = (P("seq", None), P("seq", "head"), P("seq", "head"), P(None, None, "head"), P("seq"))
    return jax.shard_map(
        local,
        mesh=mesh,
        in_specs=placed,
        out_specs=(P("seq", "head"), P("seq", None), P("seq", "head")),
        check_vma=False,
    )
```

time: 95.2 us -> 89.4 us (0.939)
  starting transfers between devices: 42 us -> 34.6 us
  waiting for transfers between devices: 25.2 us -> 27.4 us
    ppermute x26, starting transfers between devices: 42 us -> 34.6 us  [the longest x22 30 us: send(): return lax.ppermute(value, 'seq', pairs)]
    ppermute x26, waiting for transfers between devices: 25.2 us -> 27.4 us  [the longest x22 23 us: send(): return lax.ppermute(value, 'seq', pairs)]
  transfers between devices with their start and end apart: 26 -> 26, of which waited for: 14 -> 12; matrix products, arithmetic and copies ran while one was open for 0% -> 0% of each run, Pallas kernels for 18% -> 20%
where the time goes in v4:
time: 89.4 us; the launch traced here: 88.2 us
  starting transfers between devices  34.6 us (39%)
  waiting for transfers between devices  27.4 us (31%)
  Pallas kernels  24.1 us (27%)
  other arithmetic  1.15 us (1%)
    ppermute x22, starting transfers between devices, send(): return lax.ppermute(value, 'seq', pairs)  30 us
    ppermute x22, waiting for transfers between devices, send(): return lax.ppermute(value, 'seq', pairs)  23 us
    pallas_call x2, Pallas kernels, local_part(): pl.pallas_call(kernel, in_specs=[VMEM] * (4 + len(scores)), out_specs=[VM...  6.24 us
    pallas_call x1, Pallas kernels, far_states(): pl.pallas_call(far_kernel, in_specs=[HBM] * 5, out_specs=[VMEM] * 8, out_...  5.15 us
    ppermute x4, starting transfers between devices, send_head(): return lax.ppermute(value, ('seq', 'head'), pairs)  4.57 us
    ppermute x4, waiting for transfers between devices, send_head(): return lax.ppermute(value, ('seq', 'head'), pairs)  4.38 us
    pallas_call x1, Pallas kernels, near_states(): pl.pallas_call(near_kernel, in_specs=[VMEM] * 4, out_specs=[VMEM] * 4, ou...  3.81 us
    pallas_call x1, Pallas kernels, mid_part(): pl.pallas_call(mid_kernel, in_specs=[VMEM] * 13, out_specs=[VMEM] * 3, ou...  3.78 us
  transfers between devices with their start and end apart: 26, of which 12 were waited for; matrix products, arithmetic and copies ran while one was open for 0% of the time, Pallas kernels for 20%

profile of v4, /device:TPU:1, one launch (start us, length us, event | category | flops | bytes accessed | tf_op | source)
XLA Modules:
  0.0 88.2 jit_solution(3418919598223963518)
XLA Ops:
  0.6 5.1 %far_states.1 = (f32[10,8,1280]{2,1,0:T(8,128)S(1)}, bf16[512,128]{1,0:T(8,128)(2,1)S(1)}, bf16[128,512]{1,0:T(8,128)(2,1)S(1)}, bf16[512,1280]{1,0:T(8,128)(2,1...) custom-call(s32[8]{0:T(128)} %code_hbm.1, ...), custom_call_target="tpu_custom_call" | custom-call | flops 1024 | bytes 1024 | tf_op jit(solution)/shard_map/far_states/pallas_call | solution.py:140
  5.8 3.3 %collective-permute-start = (f32[4,6,8,1280]{3,2,1,0:T(8,128)S(1)}, f32[4,6,8,1280]{3,2,1,0:T(8,128)S(1)}, u32[]{:S(2)}, u32[]{:S(2)}) collective-permute-start(f32[4,6,8,1280]{3,2,1,0:T(8,128)S(1)} %get-tuple-element.74), channel_id=1, source_target_pairs={{0,4},{4,0},{8,12},{12,8},{16,20},{20,16},{24,28},{28,24},{32,36},... | collective-permute-start | bytes 2949128 | tf_op jit(solution)/shard_map/ppermute | solution.py:33
  9.1 3.8 %near_states.1 = (bf16[3,512,1280]{2,1,0:T(8,128)(2,1)S(1)}, f32[128,1280]{1,0:T(8,128)S(1)}, f32[2,64,1280]{2,1,0:T(8,128)S(1)}, f32[2,64,1280]{2,1,0:T(8,128)S(1)}) custom-call(bf16[128,512]{1,0:T(8,128)(2,1)S(1)} %get-tuple-element.75.qt, bf16[512,1280]{1,0:T(8,128)(2,1)S(1)} %get-tuple-element.97.v_ref, bf16[512,1280]{1,0:T(8,128)(2,1)S(1)} %get-tuple-element.77.e_ref, ...), custom_call_target="tpu_custom_call" | custom-call | flops 1024 | bytes 1024 | tf_op jit(solution)/shard_map/near_states/pallas_call | solution.py:183
  15.0 1.9 %collective-permute-start.3 = (f32[6,8,1280]{2,1,0:T(8,128)S(1)}, f32[6,8,1280]{2,1,0:T(8,128)S(1)}, u32[]{:S(2)}, u32[]{:S(2)}) collective-permute-start(f32[6,8,1280]{2,1,0:T(8,128)S(1)} %get-tuple-element.84), channel_id=1, source_target_pairs={{0,24},{4,12},{8,16},{12,4},{16,8},{20,28},{24,0},{28,20},{32,56},... | collective-permute-start | bytes 737288 | tf_op jit(solution)/shard_map/ppermute | solution.py:33
  17.0 7.6 %collective-permute-done.1 = f32[6,8,1280]{2,1,0:T(8,128)S(1)} collective-permute-done((f32[6,8,1280]{2,1,0:T(8,128)S(1)}, f32[6,8,1280]{2,1,0:T(8,128)S(1)}, u32[]{:S(2)}, u32[]{:S(2)}) %collective-permute-start.1) | collective-permute-done | bytes 245792 | tf_op jit(solution)/shard_map/ppermute | solution.py:33
  24.6 2.9 %collective-permute-done.3 = f32[6,8,1280]{2,1,0:T(8,128)S(1)} collective-permute-done((f32[6,8,1280]{2,1,0:T(8,128)S(1)}, f32[6,8,1280]{2,1,0:T(8,128)S(1)}, u32[]{:S(2)}, u32[]{:S(2)}) %collective-permute-start.3) | collective-permute-done | bytes 245792 | tf_op jit(solution)/shard_map/ppermute | solution.py:33
  27.7 2.8 %collective-permute-start.12 = (f32[64,1280]{1,0:T(8,128)S(1)}, f32[64,1280]{1,0:T(8,128)S(1)}, u32[]{:S(2)}, u32[]{:S(2)}) collective-permute-start(f32[64,1280]{1,0:T(8,128)S(1)} %get-tuple-element.108), channel_id=1, source_target_pairs={{0,24},{4,28},{8,16},{12,20},{16,8},{20,12},{24,0},{28,4},{32,56},... | collective-permute-start | bytes 983048 | tf_op jit(solution)/shard_map/ppermute | solution.py:33
  30.7 3.1 %collective-permute-start.7 = (f32[2,8,1280]{2,1,0:T(8,128)S(1)}, f32[2,8,1280]{2,1,0:T(8,128)S(1)}, u32[]{:S(2)}, u32[]{:S(2)}) collective-permute-start(f32[2,8,1280]{2,1,0:T(8,128)S(1)} %slice_add_fusion.8), channel_id=1, source_target_pairs={{0,64},{4,68},{8,72},{12,76},{16,80},{20,84},{24,88},{28,92},{32,9... | collective-permute-start | bytes 245768 | tf_op jit(solution)/shard_map/ppermute | solution.py:33
  34.3 3.3 %collective-permute-done.7 = f32[2,8,1280]{2,1,0:T(8,128)S(1)} collective-permute-done((f32[2,8,1280]{2,1,0:T(8,128)S(1)}, f32[2,8,1280]{2,1,0:T(8,128)S(1)}, u32[]{:S(2)}, u32[]{:S(2)}) %collective-permute-start.7) | collective-permute-done | bytes 81952 | tf_op jit(solution)/shard_map/ppermute | solution.py:33
  37.6 2.8 %collective-permute-start.8 = (f32[8,1280]{1,0:T(8,128)S(1)}, f32[8,1280]{1,0:T(8,128)S(1)}, u32[]{:S(2)}, u32[]{:S(2)}) collective-permute-start(f32[8,1280]{1,0:T(8,128)S(1)} %fusion.6), channel_id=1, source_target_pairs={{0,128},{4,196},{8,136},{12,204},{16,144},{20,212},{24,152},{28,22... | collective-permute-start | bytes 122888 | tf_op jit(solution)/shard_map/ppermute | solution.py:33
  40.4 1.6 %collective-permute-start.9 = (f32[8,1280]{1,0:T(8,128)S(1)}, f32[8,1280]{1,0:T(8,128)S(1)}, u32[]{:S(2)}, u32[]{:S(2)}) collective-permute-start(f32[8,1280]{1,0:T(8,128)S(1)} %fusion.6), channel_id=1, source_target_pairs={{0,192},{4,132},{8,200},{12,140},{16,208},{20,148},{24,216},{28,15... | collective-permute-start | bytes 122888 | tf_op jit(solution)/shard_map/ppermute | solution.py:33
  41.9 3.8 %first_local.1 = (f32[512,768]{1,0:T(8,128)S(1)}, f32[512,768]{1,0:T(8,128)S(1)}, f32[512,128]{1,0:T(8,128)S(1)}, bf16[7,256,256]{2,1,0:T(8,128)(2,1)S(1)}, bf16[7,256,256]{2,1,0:T(8,128)(2,1)S(1)}) custom-call(bf16[512,128]{1,0:T(8,128)(2,1)S(1)} %get-tuple-element.93.q_ref, bf16[512,1280]{1,0:T(8,128)(2,1)S(1)} %get-tuple-element.97.v_ref, ...), custom_call_target="tpu_custom_call" | custom-call | flops 8589934592 | bytes 33554432 | tf_op jit(solution)/shard_map/first_local/pallas_call | solution.py:294
  47.2 1.6 %collective-permute-start.10 = (f32[3,8,1280]{2,1,0:T(8,128)S(1)}, f32[3,8,1280]{2,1,0:T(8,128)S(1)}, u32[]{:S(2)}, u32[]{:S(2)}) collective-permute-start(f32[3,8,1280]{2,1,0:T(8,128)S(1)} %pad_maximum_fusion.3), channel_id=1, source_target_pairs={{0,32},{4,36},{8,40},{12,44},{16,48},{20,52},{24,56},{28,60},{32,0... | collective-permute-start | bytes 368648 | tf_op jit(solution)/shard_map/ppermute | solution.py:33
  48.8 2.4 %other_local.1 = (f32[512,512]{1,0:T(8,128)S(1)}, f32[512,512]{1,0:T(8,128)S(1)}, f32[512,128]{1,0:T(8,128)S(1)}) custom-call(bf16[512,128]{1,0:T(8,128)(2,1)S(1)} %get-tuple-element.93.q_ref, bf16[512,1280]{1,0:T(8,128)(2,1)S(1)} %get-tuple-element.97.v_ref, bf16[512,1280]{1,0:T(8,128)(2,1)S(1)} %get-tuple-element.77.e_ref, ...), custom_call_target="tpu_custom_call" | custom-call | flops 8589934592 | bytes 33554432 | tf_op jit(solution)/shard_map/other_local/pallas_call | solution.py:294
  51.5 4.6 %collective-permute-start.17 = (f32[2,64,1280]{2,1,0:T(8,128)S(1)}, f32[2,64,1280]{2,1,0:T(8,128)S(1)}, u32[]{:S(2)}, u32[]{:S(2)}) collective-permute-start(f32[2,64,1280]{2,1,0:T(8,128)S(1)} %pad_maximum_fusion), channel_id=1, source_target_pairs={{0,4},{4,0},{8,12},{12,8},{16,20},{20,16},{24,28},{28,24},{32,36},... | collective-permute-start | bytes 1966088 | tf_op jit(solution)/shard_map/ppermute | solution.py:33
  56.0 1.7 %collective-permute-start.16 = (f32[6,8,1280]{2,1,0:T(8,128)S(1)}, f32[6,8,1280]{2,1,0:T(8,128)S(1)}, u32[]{:S(2)}, u32[]{:S(2)}) collective-permute-start(f32[6,8,1280]{2,1,0:T(8,128)S(1)} %pad_maximum_fusion.2.refs_2_), channel_id=1, source_target_pairs={{0,8},{4,28},{8,0},{12,20},{16,24},{20,12},{24,16},{28,4},{32,40},... | collective-permute-start | bytes 737288 | tf_op jit(solution)/shard_map/ppermute | solution.py:33
  59.0 1.5 %collective-permute-start.14 = (f32[6,8,1280]{2,1,0:T(8,128)S(1)}, f32[6,8,1280]{2,1,0:T(8,128)S(1)}, u32[]{:S(2)}, u32[]{:S(2)}) collective-permute-start(f32[6,8,1280]{2,1,0:T(8,128)S(1)} %pad_maximum_fusion.2.refs_2_), channel_id=1, source_target_pairs={{0,16},{4,20},{8,24},{12,28},{16,0},{20,4},{24,8},{28,12},{32,48},... | collective-permute-start | bytes 737288 | tf_op jit(solution)/shard_map/ppermute | solution.py:33
  61.2 3.8 %mid_part.1 = (f32[512,1280]{1,0:T(8,128)S(1)}, f32[512,1280]{1,0:T(8,128)S(1)}, f32[512,128]{1,0:T(8,128)S(1)}) custom-call(bf16[512,128]{1,0:T(8,128)(2,1)S(1)} %get-tuple-element.93.q_ref, f32[10,8,1280]{2,1,0:T(8,128)S(1)} %get-tuple-element.78.w_ref, f32[512,768]{1,0:T(8,128)S(1)} %get-tuple-element.110.ma, f32[512,768]{1,0:T(8,128)S(1)} %get-tuple-element.111.da, ...), custom_call_target="tpu_custom_call" | custom-call | flops 1024 | bytes 1024 | tf_op jit(solution)/shard_map/mid_part/pallas_call | solution.py:330
  65.7 5.3 %collective-permute-done.14.refs_4_ = f32[6,8,1280]{2,1,0:T(8,128)S(1)} collective-permute-done((f32[6,8,1280]{2,1,0:T(8,128)S(1)}, f32[6,8,1280]{2,1,0:T(8,128)S(1)}, u32[]{:S(2)}, u32[]{:S(2)}) %collective-permute-start.14) | collective-permute-done | bytes 245792 | tf_op jit(solution)/shard_map/ppermute | solution.py:33
  74.6 2.8 %collective-permute-start.22 = (f32[256,128]{1,0:T(8,128)S(1)}, f32[256,128]{1,0:T(8,128)S(1)}, u32[]{:S(2)}, u32[]{:S(2)}) collective-permute-start(f32[256,128]{1,0:T(8,128)S(1)} %get-tuple-element.129), channel_id=1, source_target_pairs={{0,1},{1,0},{2,3},{3,2},{4,7},{5,6},{6,5},{7,4},{8,9},{9,8},{10,11... | collective-permute-start | bytes 393224 | tf_op jit(solution)/shard_map/ppermute | solution.py:43
  77.4 1.6 %last_values.1 = bf16[512,1280]{1,0:T(8,128)(2,1)} custom-call(bf16[512,128]{1,0:T(8,128)(2,1)S(1)} %get-tuple-element.93.q_ref, f32[512,1280]{1,0:T(8,128)S(1)} %get-tuple-element.131.d_in, f32[3,128,1280]{2,1,0:T(8,128)S(1)} %get-tuple-element.132.y_ref), custom_call_target="tpu_custom_call" | custom-call | flops 1024 | bytes 1024 | tf_op jit(solution)/shard_map/last_values/pallas_call | solution.py:387
  79.8 1.8 %collective-permute-done.23 = f32[256,128]{1,0:T(8,128)S(1)} collective-permute-done((f32[256,128]{1,0:T(8,128)S(1)}, f32[256,128]{1,0:T(8,128)S(1)}, u32[]{:S(2)}, u32[]{:S(2)}) %collective-permute-start.23) | collective-permute-done | bytes 131104 | tf_op jit(solution)/shard_map/ppermute | solution.py:43
  83.3 2.2 %last_mixed.1 = bf16[512,1280]{1,0:T(8,128)(2,1)} custom-call(bf16[512,128]{1,0:T(8,128)(2,1)S(1)} %get-tuple-element.93.q_ref, f32[10,8,1280]{2,1,0:T(8,128)S(1)} %get-tuple-element.78.w_ref, f32[512,1280]{1,0:T(8,128)S(1)} %get-tuple-element.138.m_in, f32[3,128,1280]{2,1,0:T(8,128)S(1)} %get-tuple-element.132.y_ref), custom_call_target="tpu_custom_call" | custom-call | flops 1024 | bytes 1024 | tf_op jit(solution)/shard_map/last_mixed/pallas_call | solution.py:412
  85.5 1.9 %collective-permute-done.25 = f32[256,128]{1,0:T(8,128)S(1)} collective-permute-done((f32[256,128]{1,0:T(8,128)S(1)}, f32[256,128]{1,0:T(8,128)S(1)}, u32[]{:S(2)}, u32[]{:S(2)}) %collective-permute-start.25) | collective-permute-done | bytes 131104 | tf_op jit(solution)/shard_map/ppermute | solution.py:43
  (58 shorter events, 14.1 us)
Async XLA Ops:
  5.8 7.1 %collective-permute-start = (f32[4,6,8,1280]{3,2,1,0:T(8,128)S(1)}, f32[4,6,8,1280]{3,2,1,0:T(8,128)S(1)}, u32[]{:S(2)}, u32[]{:S(2)}) collective-permute-start(f32[4,6,8,1280]{3,2,1,0:T(8,128)S(1)} %get-tuple-element.74), channel_id=1, source_target_pairs={{0,4},{4,0},{8,12},{12,8},{16,20},{20,16},{24,28},{28,24},{32,36},... | collective-permute-start | bytes 2949128 | tf_op jit(solution)/shard_map/ppermute | solution.py:33
  13.0 3.9 %collective-permute-start.4 = (f32[2,64,1280]{2,1,0:T(8,128)S(1)}, f32[2,64,1280]{2,1,0:T(8,128)S(1)}, u32[]{:S(2)}, u32[]{:S(2)}) collective-permute-start(f32[2,64,1280]{2,1,0:T(8,128)S(1)} %get-tuple-element.86), channel_id=1, source_target_pairs={{0,4},{4,0},{8,12},{12,8},{16,20},{20,16},{24,28},{28,24},{32,36},... | collective-permute-start | bytes 1966088 | tf_op jit(solution)/shard_map/ppermute | solution.py:33
  13.1 14.3 %collective-permute-start.5 = (f32[128,1280]{1,0:T(8,128)S(1)}, f32[128,1280]{1,0:T(8,128)S(1)}, u32[]{:S(2)}, u32[]{:S(2)}) collective-permute-start(f32[128,1280]{1,0:T(8,128)S(1)} %get-tuple-element.87), channel_id=1, source_target_pairs={{0,4},{4,0},{8,12},{12,8},{16,20},{20,16},{24,28},{28,24},{32,36},... | collective-permute-start | bytes 1966088 | tf_op jit(solution)/shard_map/ppermute | solution.py:33
  13.6 10.9 %collective-permute-start.1 = (f32[6,8,1280]{2,1,0:T(8,128)S(1)}, f32[6,8,1280]{2,1,0:T(8,128)S(1)}, u32[]{:S(2)}, u32[]{:S(2)}) collective-permute-start(f32[6,8,1280]{2,1,0:T(8,128)S(1)} %get-tuple-element.82), channel_id=1, source_target_pairs={{0,8},{4,28},{8,0},{12,20},{16,24},{20,12},{24,16},{28,4},{32,40},... | collective-permute-start | bytes 737288 | tf_op jit(solution)/shard_map/ppermute | solution.py:33
  14.6 10.0 %collective-permute-start.2 = (f32[6,8,1280]{2,1,0:T(8,128)S(1)}, f32[6,8,1280]{2,1,0:T(8,128)S(1)}, u32[]{:S(2)}, u32[]{:S(2)}) collective-permute-start(f32[6,8,1280]{2,1,0:T(8,128)S(1)} %get-tuple-element.83), channel_id=1, source_target_pairs={{0,16},{4,20},{8,24},{12,28},{16,0},{20,4},{24,8},{28,12},{32,48},... | collective-permute-start | bytes 737288 | tf_op jit(solution)/shard_map/ppermute | solution.py:33
  15.0 12.5 %collective-permute-start.3 = (f32[6,8,1280]{2,1,0:T(8,128)S(1)}, f32[6,8,1280]{2,1,0:T(8,128)S(1)}, u32[]{:S(2)}, u32[]{:S(2)}) collective-permute-start(f32[6,8,1280]{2,1,0:T(8,128)S(1)} %get-tuple-element.84), channel_id=1, source_target_pairs={{0,24},{4,12},{8,16},{12,4},{16,8},{20,28},{24,0},{28,20},{32,56},... | collective-permute-start | bytes 737288 | tf_op jit(solution)/shard_map/ppermute | solution.py:33
  27.5 6.7 %collective-permute-start.6 = (f32[3,8,1280]{2,1,0:T(8,128)S(1)}, f32[3,8,1280]{2,1,0:T(8,128)S(1)}, u32[]{:S(2)}, u32[]{:S(2)}) collective-permute-start(f32[3,8,1280]{2,1,0:T(8,128)S(1)} %slice_add_fusion.6), channel_id=1, source_target_pairs={{0,32},{4,36},{8,40},{12,44},{16,48},{20,52},{24,56},{28,60},{32,0... | collective-permute-start | bytes 368648 | tf_op jit(solution)/shard_map/ppermute | solution.py:33
  27.7 23.7 %collective-permute-start.12 = (f32[64,1280]{1,0:T(8,128)S(1)}, f32[64,1280]{1,0:T(8,128)S(1)}, u32[]{:S(2)}, u32[]{:S(2)}) collective-permute-start(f32[64,1280]{1,0:T(8,128)S(1)} %get-tuple-element.108), channel_id=1, source_target_pairs={{0,24},{4,28},{8,16},{12,20},{16,8},{20,12},{24,0},{28,4},{32,56},... | collective-permute-start | bytes 983048 | tf_op jit(solution)/shard_map/ppermute | solution.py:33
  30.5 20.9 %collective-permute-start.13 = (f32[64,1280]{1,0:T(8,128)S(1)}, f32[64,1280]{1,0:T(8,128)S(1)}, u32[]{:S(2)}, u32[]{:S(2)}) collective-permute-start(f32[64,1280]{1,0:T(8,128)S(1)} %get-tuple-element.108), channel_id=1, source_target_pairs={{0,16},{4,20},{8,24},{12,28},{16,0},{20,4},{24,8},{28,12},{32,48},... | collective-permute-start | bytes 983048 | tf_op jit(solution)/shard_map/ppermute | solution.py:33
  30.7 6.8 %collective-permute-start.7 = (f32[2,8,1280]{2,1,0:T(8,128)S(1)}, f32[2,8,1280]{2,1,0:T(8,128)S(1)}, u32[]{:S(2)}, u32[]{:S(2)}) collective-permute-start(f32[2,8,1280]{2,1,0:T(8,128)S(1)} %slice_add_fusion.8), channel_id=1, source_target_pairs={{0,64},{4,68},{8,72},{12,76},{16,80},{20,84},{24,88},{28,92},{32,9... | collective-permute-start | bytes 245768 | tf_op jit(solution)/shard_map/ppermute | solution.py:33
  33.8 17.5 %collective-permute-start.11 = (f32[64,1280]{1,0:T(8,128)S(1)}, f32[64,1280]{1,0:T(8,128)S(1)}, u32[]{:S(2)}, u32[]{:S(2)}) collective-permute-start(f32[64,1280]{1,0:T(8,128)S(1)} %get-tuple-element.107), channel_id=1, source_target_pairs={{0,8},{4,12},{8,0},{12,4},{16,24},{20,28},{24,16},{28,20},{32,40},... | collective-permute-start | bytes 983048 | tf_op jit(solution)/shard_map/ppermute | solution.py:33
  37.6 8.2 %collective-permute-start.8 = (f32[8,1280]{1,0:T(8,128)S(1)}, f32[8,1280]{1,0:T(8,128)S(1)}, u32[]{:S(2)}, u32[]{:S(2)}) collective-permute-start(f32[8,1280]{1,0:T(8,128)S(1)} %fusion.6), channel_id=1, source_target_pairs={{0,128},{4,196},{8,136},{12,204},{16,144},{20,212},{24,152},{28,22... | collective-permute-start | bytes 122888 | tf_op jit(solution)/shard_map/ppermute | solution.py:33
  40.4 6.9 %collective-permute-start.9 = (f32[8,1280]{1,0:T(8,128)S(1)}, f32[8,1280]{1,0:T(8,128)S(1)}, u32[]{:S(2)}, u32[]{:S(2)}) collective-permute-start(f32[8,1280]{1,0:T(8,128)S(1)} %fusion.6), channel_id=1, source_target_pairs={{0,192},{4,132},{8,200},{12,140},{16,208},{20,148},{24,216},{28,15... | collective-permute-start | bytes 122888 | tf_op jit(solution)/shard_map/ppermute | solution.py:33
  47.2 4.0 %collective-permute-start.10 = (f32[3,8,1280]{2,1,0:T(8,128)S(1)}, f32[3,8,1280]{2,1,0:T(8,128)S(1)}, u32[]{:S(2)}, u32[]{:S(2)}) collective-permute-start(f32[3,8,1280]{2,1,0:T(8,128)S(1)} %pad_maximum_fusion.3), channel_id=1, source_target_pairs={{0,32},{4,36},{8,40},{12,44},{16,48},{20,52},{24,56},{28,60},{32,0... | collective-permute-start | bytes 368648 | tf_op jit(solution)/shard_map/ppermute | solution.py:33
  51.5 9.7 %collective-permute-start.17 = (f32[2,64,1280]{2,1,0:T(8,128)S(1)}, f32[2,64,1280]{2,1,0:T(8,128)S(1)}, u32[]{:S(2)}, u32[]{:S(2)}) collective-permute-start(f32[2,64,1280]{2,1,0:T(8,128)S(1)} %pad_maximum_fusion), channel_id=1, source_target_pairs={{0,4},{4,0},{8,12},{12,8},{16,20},{20,16},{24,28},{28,24},{32,36},... | collective-permute-start | bytes 1966088 | tf_op jit(solution)/shard_map/ppermute | solution.py:33
  56.0 8.9 %collective-permute-start.16 = (f32[6,8,1280]{2,1,0:T(8,128)S(1)}, f32[6,8,1280]{2,1,0:T(8,128)S(1)}, u32[]{:S(2)}, u32[]{:S(2)}) collective-permute-start(f32[6,8,1280]{2,1,0:T(8,128)S(1)} %pad_maximum_fusion.2.refs_2_), channel_id=1, source_target_pairs={{0,8},{4,28},{8,0},{12,20},{16,24},{20,12},{24,16},{28,4},{32,40},... | collective-permute-start | bytes 737288 | tf_op jit(solution)/shard_map/ppermute | solution.py:33
  57.8 8.0 %collective-permute-start.15 = (f32[6,8,1280]{2,1,0:T(8,128)S(1)}, f32[6,8,1280]{2,1,0:T(8,128)S(1)}, u32[]{:S(2)}, u32[]{:S(2)}) collective-permute-start(f32[6,8,1280]{2,1,0:T(8,128)S(1)} %pad_maximum_fusion.2.refs_2_), channel_id=1, source_target_pairs={{0,24},{4,12},{8,16},{12,4},{16,8},{20,28},{24,0},{28,20},{32,56},... | collective-permute-start | bytes 737288 | tf_op jit(solution)/shard_map/ppermute | solution.py:33
  59.0 12.1 %collective-permute-start.14 = (f32[6,8,1280]{2,1,0:T(8,128)S(1)}, f32[6,8,1280]{2,1,0:T(8,128)S(1)}, u32[]{:S(2)}, u32[]{:S(2)}) collective-permute-start(f32[6,8,1280]{2,1,0:T(8,128)S(1)} %pad_maximum_fusion.2.refs_2_), channel_id=1, source_target_pairs={{0,16},{4,20},{8,24},{12,28},{16,0},{20,4},{24,8},{28,12},{32,48},... | collective-permute-start | bytes 737288 | tf_op jit(solution)/shard_map/ppermute | solution.py:33
  60.4 11.1 %collective-permute-start.18 = (f32[6,8,1280]{2,1,0:T(8,128)S(1)}, f32[6,8,1280]{2,1,0:T(8,128)S(1)}, u32[]{:S(2)}, u32[]{:S(2)}) collective-permute-start(f32[6,8,1280]{2,1,0:T(8,128)S(1)} %pad_maximum_fusion.2.refs_2_), channel_id=1, source_target_pairs={{0,4},{4,0},{8,12},{12,8},{16,20},{20,16},{24,28},{28,24},{32,36},... | collective-permute-start | bytes 737288 | tf_op jit(solution)/shard_map/ppermute | solution.py:33
  71.1 1.9 %collective-permute-start.21 = (f32[6,8,1280]{2,1,0:T(8,128)S(1)}, f32[6,8,1280]{2,1,0:T(8,128)S(1)}, u32[]{:S(2)}, u32[]{:S(2)}) collective-permute-start(f32[6,8,1280]{2,1,0:T(8,128)S(1)} %collective-permute-done.15.refs_5_), channel_id=1, source_target_pairs={{0,4},{4,0},{8,12},{12,8},{16,20},{20,16},{24,28},{28,24},{32,36},... | collective-permute-start | bytes 737288 | tf_op jit(solution)/shard_map/ppermute | solution.py:33
  74.6 5.2 %collective-permute-start.22 = (f32[256,128]{1,0:T(8,128)S(1)}, f32[256,128]{1,0:T(8,128)S(1)}, u32[]{:S(2)}, u32[]{:S(2)}) collective-permute-start(f32[256,128]{1,0:T(8,128)S(1)} %get-tuple-element.129), channel_id=1, source_target_pairs={{0,1},{1,0},{2,3},{3,2},{4,7},{5,6},{6,5},{7,4},{8,9},{9,8},{10,11... | collective-permute-start | bytes 393224 | tf_op jit(solution)/shard_map/ppermute | solution.py:43
  77.4 4.1 %collective-permute-start.23 = (f32[256,128]{1,0:T(8,128)S(1)}, f32[256,128]{1,0:T(8,128)S(1)}, u32[]{:S(2)}, u32[]{:S(2)}) collective-permute-start(f32[256,128]{1,0:T(8,128)S(1)} %get-tuple-element.130), channel_id=1, source_target_pairs={{0,3},{1,2},{2,1},{3,0},{4,5},{5,4},{6,7},{7,6},{8,11},{9,10},{10,... | collective-permute-start | bytes 393224 | tf_op jit(solution)/shard_map/ppermute | solution.py:43
  81.6 4.0 %collective-permute-start.24 = (f32[256,128]{1,0:T(8,128)S(1)}, f32[256,128]{1,0:T(8,128)S(1)}, u32[]{:S(2)}, u32[]{:S(2)}) collective-permute-start(f32[256,128]{1,0:T(8,128)S(1)} %add.119), channel_id=1, source_target_pairs={{0,3},{1,2},{2,1},{3,0},{4,5},{5,4},{6,7},{7,6},{8,11},{9,10},{10,... | collective-permute-start | bytes 393224 | tf_op jit(solution)/shard_map/ppermute | solution.py:43
  81.9 5.5 %collective-permute-start.25 = (f32[256,128]{1,0:T(8,128)S(1)}, f32[256,128]{1,0:T(8,128)S(1)}, u32[]{:S(2)}, u32[]{:S(2)}) collective-permute-start(f32[256,128]{1,0:T(8,128)S(1)} %add.120), channel_id=1, source_target_pairs={{0,1},{1,0},{2,3},{3,2},{4,7},{5,6},{6,5},{7,4},{8,9},{9,8},{10,11... | collective-permute-start | bytes 393224 | tf_op jit(solution)/shard_map/ppermute | solution.py:43
  (4 other events, 17.2 us)

commit v5 on v4

--- a/solution.py
+++ b/solution.py
@@ -223,8 +223,7 @@
     d_ref[:, block] += dot(q_ref[...], lower.astype(BF), 1, 0)
 
 
-def local_blocks(first, count, q_ref, v_ref, e_ref, w_ref, score, flipped, m_ref, d_ref, dq_ref, grad, z):
-    grad[...] = jnp.zeros_like(grad)
+def local_blocks(first, count, v_ref, e_ref, w_ref, score, flipped, m_ref, d_ref, before, grad, z):
     per = TILE // CH
 
     def one_block(j, carry):
@@ -250,13 +249,36 @@
             back = dot(flipped[index], z[index], 1, 0)
             mixed[t] = out if mixed[t] is None else mixed[t] + out
             d_val[s] = back if d_val[s] is None else d_val[s] + back
-            grad[index] += dot(z[index], vals, 1, 1)
+            grad[index] = before[index] + dot(z[index], vals, 1, 1)
         for i in range(2):
             m_ref[i * TILE : (i + 1) * TILE, out_block] = mixed[i]
             d_ref[i * TILE : (i + 1) * TILE, out_block] = d_val[i]
         return carry
 
     lax.fori_loop(0, count, one_block, 0)
+
+
+def first_local_kernel(q_ref, v_ref, e_ref, w_ref, m_ref, d_ref, score, flipped, grad, z):
+    grad[...] = jnp.zeros_like(grad)
+    for index, (t, s, level) in enumerate(LOCAL):
+        qt_rows = q_ref[t * TILE : (t + 1) * TILE, :]
+        qs_rows = q_ref[s * TILE : (s + 1) * TILE, :]
+        direct = dot(qt_rows, qs_rows, 1, 1)
+        swapped = dot(qs_rows, qt_rows, 1, 1)
+        if level < 3:
+            direct = jnp.where(kept(level, False), direct, 0.0)
+            swapped = jnp.where(kept(level, True), swapped, 0.0)
+        score[index] = direct.astype(BF)
+        flipped[index] = swapped.astype(BF)
+    local_blocks(0, FIRST, v_ref, e_ref, w_ref, score, flipped, m_ref, d_ref, grad, grad, z)
+
+
+def next_local_kernel(q_ref, v_ref, e_ref, w_ref, score, flipped, before, m_ref, d_ref, grad, z):
+    local_blocks(FIRST, 1, v_ref, e_ref, w_ref, score, flipped, m_ref, d_ref, before, grad, z)
+
+
+def end_local_kernel(q_ref, v_ref, e_ref, w_ref, score, flipped, before, m_ref, d_ref, dq_ref, grad, z):
+    local_blocks(FIRST + 1, 1, v_ref, e_ref, w_ref, score, flipped, m_ref, d_ref, before, grad, z)
     q = [q_ref[i * TILE : (i + 1) * TILE, :] for i in range(2)]
     cross = grad[6].astype(BF)
     extra = [dot(cross, q[1], 0, 0), dot(cross, q[0], 1, 0)]
@@ -269,42 +291,29 @@
         dq_ref[i * TILE : (i + 1) * TILE, :] = part + extra[i]
 
 
-def first_local_kernel(q_ref, v_ref, e_ref, w_ref, m_ref, d_ref, dq_ref, score, flipped, grad, z):
-    for index, (t, s, level) in enumerate(LOCAL):
-        qt_rows = q_ref[t * TILE : (t + 1) * TILE, :]
-        qs_rows = q_ref[s * TILE : (s + 1) * TILE, :]
-        direct = dot(qt_rows, qs_rows, 1, 1)
-        swapped = dot(qs_rows, qt_rows, 1, 1)
-        if level < 3:
-            direct = jnp.where(kept(level, False), direct, 0.0)
-            swapped = jnp.where(kept(level, True), swapped, 0.0)
-        score[index] = direct.astype(BF)
-        flipped[index] = swapped.astype(BF)
-    local_blocks(0, FIRST, q_ref, v_ref, e_ref, w_ref, score, flipped, m_ref, d_ref, dq_ref, grad, z)
-
-
-def other_local_kernel(q_ref, v_ref, e_ref, w_ref, score, flipped, m_ref, d_ref, dq_ref, grad, z):
-    local_blocks(FIRST, STEPS - FIRST, q_ref, v_ref, e_ref, w_ref, score, flipped, m_ref, d_ref, dq_ref, grad, z)
-
-
-def local_part(q, v, e, w, scores):
-    wide = (STEPS - FIRST if scores else FIRST) * BLK
-    kernel, name = (other_local_kernel, "other_local") if scores else (first_local_kernel, "first_local")
+def local_part(stage, q, v, e, w, tables):
+    kernel = (first_local_kernel, next_local_kernel, end_local_kernel)[stage]
+    wide = BLK if stage else FIRST * BLK
     table = shape(7, TILE, TILE, kind=BF)
+    grad = shape(7, TILE, TILE)
+    outs = ([table, table, grad], [grad], [shape(TOK, STATE)])[stage]
+    scratch = [pltpu.VMEM((7, TILE, BLK), BF)]
+    if stage == 2:
+        scratch = [pltpu.VMEM((7, TILE, TILE), F32)] + scratch
     return pl.pallas_call(
         kernel,
-        in_specs=[VMEM] * (4 + len(scores)),
-        out_specs=[VMEM] * (5 - len(scores)),
-        out_shape=[shape(TOK, wide), shape(TOK, wide), shape(TOK, STATE)] + [table] * (2 - len(scores)),
-        scratch_shapes=[pltpu.VMEM((7, TILE, TILE), F32), pltpu.VMEM((7, TILE, BLK), BF)],
+        in_specs=[VMEM] * (4 + len(tables)),
+        out_specs=[VMEM] * (2 + len(outs)),
+        out_shape=[shape(TOK, wide), shape(TOK, wide)] + outs,
+        scratch_shapes=scratch,
         compiler_params=params(20),
         cost_estimate=pl.CostEstimate(flops=1 << 33, bytes_accessed=1 << 25, transcendentals=0),
-        name=name,
-    )(q, v, e, w, *scores)
+        name=("first_local", "next_local", "end_local")[stage],
+    )(q, v, e, w, *tables)
 
 
 def mid_kernel(
-    q_ref, w_ref, ma, da, dqa, mb, db, dqb, z_ref, y1_ref, y2_ref, y3_ref, y23o_ref, m_ref, d_ref, dq_ref, y
+    q_ref, w_ref, ma, da, mb, db, mc, dc, dq_in, z_ref, y1_ref, y2_ref, y3_ref, y23o_ref, m_ref, d_ref, dq_ref, y
 ):
     position, core, x, z0 = coords()
     half = STATE // 2
@@ -314,11 +323,13 @@
         y[index, own, :] = ref[...]
         y[index, oth, :] = y23o_ref[index]
     y[2] = y1_ref[...]
-    grads = dqa[...] + dqb[...]
+    grads = dq_in[...]
     m_ref[:, : FIRST * BLK] = ma[...]
     d_ref[:, : FIRST * BLK] = da[...]
-    m_ref[:, FIRST * BLK :] = mb[...]
-    d_ref[:, FIRST * BLK :] = db[...]
+    m_ref[:, BLOCKS[FIRST]] = mb[...]
+    d_ref[:, BLOCKS[FIRST]] = db[...]
+    m_ref[:, BLOCKS[FIRST + 1]] = mc[...]
+    d_ref[:, BLOCKS[FIRST + 1]] = dc[...]
     for block in BLOCKS:
         add_outer(q_ref, w_ref, (2, 3, 1), position, y, m_ref, d_ref, block)
         for index in range(3):
@@ -326,17 +337,17 @@
     dq_ref[...] = grads
 
 
-def mid_part(q, w, first, other, zn, y1, y2, y3, y23o):
+def mid_part(q, w, own, zn, y1, y2, y3, y23o):
     return pl.pallas_call(
         mid_kernel,
-        in_specs=[VMEM] * 13,
+        in_specs=[VMEM] * 14,
         out_specs=[VMEM] * 3,
         out_shape=[shape(TOK, COLS), shape(TOK, COLS), shape(TOK, STATE)],
         scratch_shapes=[pltpu.VMEM((3, STATE, COLS), F32)],
         compiler_params=params(30),
         cost_estimate=cost(),
         name="mid_part",
-    )(q, w, *first, *other, zn, y1, y2, y3, y23o)
+    )(q, w, *own, zn, y1, y2, y3, y23o)
 
 
 def score_kernel(*refs):
@@ -429,12 +440,13 @@
     zn, x1, own_n, oth_n = near_states(qt, v, e, w)
 
     chip = [own_f[j] + got_f[j] for j in range(4)]
-    chip, x1, oth_n = tie((chip, x1, oth_n))
+    chip, x1, oth_n, v1 = tie((chip, x1, oth_n, v))
     slices = [send(chip[j], 2 * j, 2 * (4 - j)) for j in (1, 2, 3)]
     got_n = send(oth_n, 1)
     y1 = send(x1, 1)
     near = [own_n[i] + got_n[i] for i in range(2)]
-    slices, near, y1 = tie((slices, near, y1))
+    ma, da, score, flipped, grad = local_part(0, q, v1, e, w, ())
+    slices, near, y1, grad = tie((slices, near, y1, grad))
     mine = sum((s[0] for s in slices), chip[0][0])
     cross = sum((s[1:4] for s in slices), chip[0][1:4])
     pair = sum((s[4:6] for s in slices), chip[0][4:6])
@@ -443,21 +455,22 @@
     five = send(pair, 16)
     y2 = send(near[0], 2)
     y3 = [send(near[1], 6), send(near[1], 4)]
+    low, five = tie((low, five))
     six = mine + low[0]
-    six, five, v2 = tie((six, five, v))
+    six, v2 = tie((six, v1))
     y6 = [send(six, 32, 48), send(six, 48, 32)]
-    *first, score, flipped = local_part(q, v2, e, w, ())
+    mb, db, grad = local_part(1, q, v2, e, w, (score, flipped, grad))
     half = jnp.concatenate([(y6[0] + y6[1])[None], five])
-    half, score, v3 = tie((half, score, v2))
+    half, grad, v3 = tie((half, grad, v2))
     rest = send(half, 8)
-    other = local_part(q, v3, e, w, (score, flipped))
-    rest, other = tie((rest, other))
+    mc, dc, dq = local_part(2, q, v3, e, w, (score, flipped, grad))
+    rest, dq = tie((rest, dq))
     quad = jnp.concatenate([half[0:1], rest[0:1], low[1:3], half[1:3] + rest[1:3]])
-    quad, other, y2, y3 = tie((quad, other, y2, y3))
+    quad, dq, y2, y3 = tie((quad, dq, y2, y3))
     y3 = y3[0] + y3[1]
     y23o = send(jnp.stack([y2, y3]), 1)
     pieces = [quad] + [send(quad, 2 * j, 2 * (4 - j)) for j in (1, 2, 3)]
-    m, d, dq = mid_part(q, w, first, other, zn, y1, y2, y3, y23o)
+    m, d, dq = mid_part(q, w, (ma, da, mb, db, mc, dc, dq), zn, y1, y2, y3, y23o)
     for j in (1, 3, 2):
         pieces[j], dq = tie((pieces[j], dq))
     pieces = pieces + [send(p, 1) for p in pieces]

time: 89.4 us -> 86.8 us (0.971)
  waiting for transfers between devices: 27.4 us -> 25.9 us
    ppermute x22, waiting for transfers between devices: 23 us -> 21.5 us  [send(): return lax.ppermute(value, 'seq', pairs)]
    pallas_call x3 -> x4, Pallas kernels: 10 us -> 9.38 us  [the longest x3 5.61 us: local_part(): pl.pallas_call(kernel, in_specs=[VMEM] * (4 + len(tables)), out_specs=[VM...]
where the time goes in v5:
time: 86.8 us; the launch traced here: 86 us
  starting transfers between devices  34.6 us (40%)
  waiting for transfers between devices  25.9 us (30%)
  Pallas kernels  23.5 us (27%)
  other arithmetic  1.15 us (1%)
  between operations  0.88 us (1%)
    ppermute x22, starting transfers between devices, send(): return lax.ppermute(value, 'seq', pairs)  30 us
    ppermute x22, waiting for transfers between devices, send(): return lax.ppermute(value, 'seq', pairs)  21.5 us
    pallas_call x3, Pallas kernels, local_part(): pl.pallas_call(kernel, in_specs=[VMEM] * (4 + len(tables)), out_specs=[VM...  5.61 us
    pallas_call x1, Pallas kernels, far_states(): pl.pallas_call(far_kernel, in_specs=[HBM] * 5, out_specs=[VMEM] * 8, out_...  5.15 us
    ppermute x4, starting transfers between devices, send_head(): return lax.ppermute(value, ('seq', 'head'), pairs)  4.56 us
    ppermute x4, waiting for transfers between devices, send_head(): return lax.ppermute(value, ('seq', 'head'), pairs)  4.39 us
    pallas_call x1, Pallas kernels, near_states(): pl.pallas_call(near_kernel, in_specs=[VMEM] * 4, out_specs=[VMEM] * 4, ou...  3.81 us
    pallas_call x1, Pallas kernels, mid_part(): pl.pallas_call(mid_kernel, in_specs=[VMEM] * 14, out_specs=[VMEM] * 3, ou...  3.77 us
  transfers between devices with their start and end apart: 26, of which 12 were waited for; matrix products, arithmetic and copies ran while one was open for 0% of the time, Pallas kernels for 20%

profile of v5, /device:TPU:1, one launch (start us, length us, event | category | flops | bytes accessed | tf_op | source)
XLA Modules:
  0.0 86.0 jit_solution(12653753048081493078)
XLA Ops:
  0.6 5.1 %far_states.1 = (f32[10,8,1280]{2,1,0:T(8,128)S(1)}, bf16[512,128]{1,0:T(8,128)(2,1)S(1)}, bf16[128,512]{1,0:T(8,128)(2,1)S(1)}, bf16[512,1280]{1,0:T(8,128)(2,1...) custom-call(s32[8]{0:T(128)} %code_hbm.1, ...), custom_call_target="tpu_custom_call" | custom-call | flops 1024 | bytes 1024 | tf_op jit(solution)/shard_map/far_states/pallas_call | solution.py:140
  5.8 3.3 %collective-permute-start = (f32[4,6,8,1280]{3,2,1,0:T(8,128)S(1)}, f32[4,6,8,1280]{3,2,1,0:T(8,128)S(1)}, u32[]{:S(2)}, u32[]{:S(2)}) collective-permute-start(f32[4,6,8,1280]{3,2,1,0:T(8,128)S(1)} %get-tuple-element.76), channel_id=1, source_target_pairs={{0,4},{4,0},{8,12},{12,8},{16,20},{20,16},{24,28},{28,24},{32,36},... | collective-permute-start | bytes 2949128 | tf_op jit(solution)/shard_map/ppermute | solution.py:33
  9.1 3.8 %near_states.1 = (bf16[3,512,1280]{2,1,0:T(8,128)(2,1)S(1)}, f32[128,1280]{1,0:T(8,128)S(1)}, f32[2,64,1280]{2,1,0:T(8,128)S(1)}, f32[2,64,1280]{2,1,0:T(8,128)S(1)}) custom-call(bf16[128,512]{1,0:T(8,128)(2,1)S(1)} %get-tuple-element.77.qt, bf16[512,1280]{1,0:T(8,128)(2,1)S(1)} %get-tuple-element.105.v_ref, bf16[512,1280]{1,0:T(8,128)(2,1)S(1)} %get-tuple-element.79.e_ref, ...), custom_call_target="tpu_custom_call" | custom-call | flops 1024 | bytes 1024 | tf_op jit(solution)/shard_map/near_states/pallas_call | solution.py:183
  15.0 1.9 %collective-permute-start.3 = (f32[6,8,1280]{2,1,0:T(8,128)S(1)}, f32[6,8,1280]{2,1,0:T(8,128)S(1)}, u32[]{:S(2)}, u32[]{:S(2)}) collective-permute-start(f32[6,8,1280]{2,1,0:T(8,128)S(1)} %get-tuple-element.86), channel_id=1, source_target_pairs={{0,24},{4,12},{8,16},{12,4},{16,8},{20,28},{24,0},{28,20},{32,56},... | collective-permute-start | bytes 737288 | tf_op jit(solution)/shard_map/ppermute | solution.py:33
  16.9 3.4 %first_local.1 = (f32[512,768]{1,0:T(8,128)S(1)}, f32[512,768]{1,0:T(8,128)S(1)}, bf16[7,256,256]{2,1,0:T(8,128)(2,1)S(1)}, bf16[7,256,256]{2,1,0:T(8,128)(2,1)S(1)}, f32[7,256,256]{2,1,0:T(8,128)S(1)}) custom-call(bf16[512,128]{1,0:T(8,128)(2,1)S(1)} %get-tuple-element.90.q_ref, bf16[512,1280]{1,0:T(8,128)(2,1)S(1)} %get-tuple-element.105.v_ref, ...), custom_call_target="tpu_custom_call" | custom-call | flops 8589934592 | bytes 33554432 | tf_op jit(solution)/shard_map/first_local/pallas_call | solution.py:303
  20.4 4.2 %collective-permute-done.1 = f32[6,8,1280]{2,1,0:T(8,128)S(1)} collective-permute-done((f32[6,8,1280]{2,1,0:T(8,128)S(1)}, f32[6,8,1280]{2,1,0:T(8,128)S(1)}, u32[]{:S(2)}, u32[]{:S(2)}) %collective-permute-start.1) | collective-permute-done | bytes 245792 | tf_op jit(solution)/shard_map/ppermute | solution.py:33
  24.6 2.9 %collective-permute-done.3 = f32[6,8,1280]{2,1,0:T(8,128)S(1)} collective-permute-done((f32[6,8,1280]{2,1,0:T(8,128)S(1)}, f32[6,8,1280]{2,1,0:T(8,128)S(1)}, u32[]{:S(2)}, u32[]{:S(2)}) %collective-permute-start.3) | collective-permute-done | bytes 245792 | tf_op jit(solution)/shard_map/ppermute | solution.py:33
  27.7 3.2 %collective-permute-start.7 = (f32[2,8,1280]{2,1,0:T(8,128)S(1)}, f32[2,8,1280]{2,1,0:T(8,128)S(1)}, u32[]{:S(2)}, u32[]{:S(2)}) collective-permute-start(f32[2,8,1280]{2,1,0:T(8,128)S(1)} %slice_add_fusion.8), channel_id=1, source_target_pairs={{0,64},{4,68},{8,72},{12,76},{16,80},{20,84},{24,88},{28,92},{32,9... | collective-permute-start | bytes 245768 | tf_op jit(solution)/shard_map/ppermute | solution.py:33
  30.8 2.7 %collective-permute-start.12 = (f32[64,1280]{1,0:T(8,128)S(1)}, f32[64,1280]{1,0:T(8,128)S(1)}, u32[]{:S(2)}, u32[]{:S(2)}) collective-permute-start(f32[64,1280]{1,0:T(8,128)S(1)} %get-tuple-element.111), channel_id=1, source_target_pairs={{0,24},{4,28},{8,16},{12,20},{16,8},{20,12},{24,0},{28,4},{32,56},... | collective-permute-start | bytes 983048 | tf_op jit(solution)/shard_map/ppermute | solution.py:33
  34.2 3.4 %collective-permute-start.8 = (f32[8,1280]{1,0:T(8,128)S(1)}, f32[8,1280]{1,0:T(8,128)S(1)}, u32[]{:S(2)}, u32[]{:S(2)}) collective-permute-start(f32[8,1280]{1,0:T(8,128)S(1)} %add_bitcast_fusion.1), channel_id=1, source_target_pairs={{0,128},{4,196},{8,136},{12,204},{16,144},{20,212},{24,152},{28,22... | collective-permute-start | bytes 122888 | tf_op jit(solution)/shard_map/ppermute | solution.py:33
  37.6 1.7 %collective-permute-start.9 = (f32[8,1280]{1,0:T(8,128)S(1)}, f32[8,1280]{1,0:T(8,128)S(1)}, u32[]{:S(2)}, u32[]{:S(2)}) collective-permute-start(f32[8,1280]{1,0:T(8,128)S(1)} %add_bitcast_fusion.1), channel_id=1, source_target_pairs={{0,192},{4,132},{8,200},{12,140},{16,208},{20,148},{24,216},{28,15... | collective-permute-start | bytes 122888 | tf_op jit(solution)/shard_map/ppermute | solution.py:33
  40.2 4.6 %collective-permute-done.9 = f32[8,1280]{1,0:T(8,128)S(1)} collective-permute-done((f32[8,1280]{1,0:T(8,128)S(1)}, f32[8,1280]{1,0:T(8,128)S(1)}, u32[]{:S(2)}, u32[]{:S(2)}) %collective-permute-start.9) | collective-permute-done | bytes 40992 | tf_op jit(solution)/shard_map/ppermute | solution.py:33
  47.2 1.8 %collective-permute-done.10 = f32[3,8,1280]{2,1,0:T(8,128)S(1)} collective-permute-done((f32[3,8,1280]{2,1,0:T(8,128)S(1)}, f32[3,8,1280]{2,1,0:T(8,128)S(1)}, u32[]{:S(2)}, u32[]{:S(2)}) %collective-permute-start.10) | collective-permute-done | bytes 122912 | tf_op jit(solution)/shard_map/ppermute | solution.py:33
  49.2 5.5 %collective-permute-start.17 = (f32[2,64,1280]{2,1,0:T(8,128)S(1)}, f32[2,64,1280]{2,1,0:T(8,128)S(1)}, u32[]{:S(2)}, u32[]{:S(2)}) collective-permute-start(f32[2,64,1280]{2,1,0:T(8,128)S(1)} %pad_maximum_fusion), channel_id=1, source_target_pairs={{0,4},{4,0},{8,12},{12,8},{16,20},{20,16},{24,28},{28,24},{32,36},... | collective-permute-start | bytes 1966088 | tf_op jit(solution)/shard_map/ppermute | solution.py:33
  55.6 2.9 %collective-permute-start.14 = (f32[6,8,1280]{2,1,0:T(8,128)S(1)}, f32[6,8,1280]{2,1,0:T(8,128)S(1)}, u32[]{:S(2)}, u32[]{:S(2)}) collective-permute-start(f32[6,8,1280]{2,1,0:T(8,128)S(1)} %pad_maximum_fusion.2.refs_2_), channel_id=1, source_target_pairs={{0,16},{4,20},{8,24},{12,28},{16,0},{20,4},{24,8},{28,12},{32,48},... | collective-permute-start | bytes 737288 | tf_op jit(solution)/shard_map/ppermute | solution.py:33
  58.8 3.8 %mid_part.1 = (f32[512,1280]{1,0:T(8,128)S(1)}, f32[512,1280]{1,0:T(8,128)S(1)}, f32[512,128]{1,0:T(8,128)S(1)}) custom-call(bf16[512,128]{1,0:T(8,128)(2,1)S(1)} %get-tuple-element.90.q_ref, f32[10,8,1280]{2,1,0:T(8,128)S(1)} %get-tuple-element.80.w_ref, f32[512,768]{1,0:T(8,128)S(1)} %get-tuple-element.113.ma, f32[512,768]{1,0:T(8,128)S(1)} %get-tuple-element.114.da, ...), custom_call_target="tpu_custom_call" | custom-call | flops 1024 | bytes 1024 | tf_op jit(solution)/shard_map/mid_part/pallas_call | solution.py:341
  63.6 5.2 %collective-permute-done.14.refs_4_ = f32[6,8,1280]{2,1,0:T(8,128)S(1)} collective-permute-done((f32[6,8,1280]{2,1,0:T(8,128)S(1)}, f32[6,8,1280]{2,1,0:T(8,128)S(1)}, u32[]{:S(2)}, u32[]{:S(2)}) %collective-permute-start.14) | collective-permute-done | bytes 245792 | tf_op jit(solution)/shard_map/ppermute | solution.py:33
  71.1 1.3 %score_part.1 = (f32[256,128]{1,0:T(8,128)S(1)}, f32[256,128]{1,0:T(8,128)S(1)}, f32[3,128,1280]{2,1,0:T(8,128)S(1)}) custom-call(f32[512,128]{1,0:T(8,128)S(1)} %get-tuple-element.128.refs_0_, bf16[3,512,1280]{2,1,0:T(8,128)(2,1)S(1)} %get-tuple-element.129.refs_1_, f32[6,8,1280]{2,1,0:T(8,128)S(1)} %pad_maximum_fusion.2.refs_2_, ...), custom_call_target="tpu_custom_call" | custom-call | flops 1024 | bytes 1024 | tf_op jit(solution)/shard_map/score_part/pallas_call | solution.py:376
  72.4 2.8 %collective-permute-start.22 = (f32[256,128]{1,0:T(8,128)S(1)}, f32[256,128]{1,0:T(8,128)S(1)}, u32[]{:S(2)}, u32[]{:S(2)}) collective-permute-start(f32[256,128]{1,0:T(8,128)S(1)} %get-tuple-element.133), channel_id=1, source_target_pairs={{0,1},{1,0},{2,3},{3,2},{4,7},{5,6},{6,5},{7,4},{8,9},{9,8},{10,11... | collective-permute-start | bytes 393224 | tf_op jit(solution)/shard_map/ppermute | solution.py:43
  75.2 1.6 %last_values.1 = bf16[512,1280]{1,0:T(8,128)(2,1)} custom-call(bf16[512,128]{1,0:T(8,128)(2,1)S(1)} %get-tuple-element.90.q_ref, f32[512,1280]{1,0:T(8,128)S(1)} %get-tuple-element.135.d_in, f32[3,128,1280]{2,1,0:T(8,128)S(1)} %get-tuple-element.136.y_ref), custom_call_target="tpu_custom_call" | custom-call | flops 1024 | bytes 1024 | tf_op jit(solution)/shard_map/last_values/pallas_call | solution.py:398
  77.6 1.8 %collective-permute-done.23 = f32[256,128]{1,0:T(8,128)S(1)} collective-permute-done((f32[256,128]{1,0:T(8,128)S(1)}, f32[256,128]{1,0:T(8,128)S(1)}, u32[]{:S(2)}, u32[]{:S(2)}) %collective-permute-start.23) | collective-permute-done | bytes 131104 | tf_op jit(solution)/shard_map/ppermute | solution.py:43
  79.7 1.4 %collective-permute-start.25 = (f32[256,128]{1,0:T(8,128)S(1)}, f32[256,128]{1,0:T(8,128)S(1)}, u32[]{:S(2)}, u32[]{:S(2)}) collective-permute-start(f32[256,128]{1,0:T(8,128)S(1)} %add.120), channel_id=1, source_target_pairs={{0,1},{1,0},{2,3},{3,2},{4,7},{5,6},{6,5},{7,4},{8,9},{9,8},{10,11... | collective-permute-start | bytes 393224 | tf_op jit(solution)/shard_map/ppermute | solution.py:43
  81.1 2.2 %last_mixed.1 = bf16[512,1280]{1,0:T(8,128)(2,1)} custom-call(bf16[512,128]{1,0:T(8,128)(2,1)S(1)} %get-tuple-element.90.q_ref, f32[10,8,1280]{2,1,0:T(8,128)S(1)} %get-tuple-element.80.w_ref, f32[512,1280]{1,0:T(8,128)S(1)} %get-tuple-element.142.m_in, f32[3,128,1280]{2,1,0:T(8,128)S(1)} %get-tuple-element.136.y_ref), custom_call_target="tpu_custom_call" | custom-call | flops 1024 | bytes 1024 | tf_op jit(solution)/shard_map/last_mixed/pallas_call | solution.py:423
  83.3 1.9 %collective-permute-done.25 = f32[256,128]{1,0:T(8,128)S(1)} collective-permute-done((f32[256,128]{1,0:T(8,128)S(1)}, f32[256,128]{1,0:T(8,128)S(1)}, u32[]{:S(2)}, u32[]{:S(2)}) %collective-permute-start.25) | collective-permute-done | bytes 131104 | tf_op jit(solution)/shard_map/ppermute | solution.py:43
  (59 shorter events, 12.7 us)
Async XLA Ops:
  5.8 7.1 %collective-permute-start = (f32[4,6,8,1280]{3,2,1,0:T(8,128)S(1)}, f32[4,6,8,1280]{3,2,1,0:T(8,128)S(1)}, u32[]{:S(2)}, u32[]{:S(2)}) collective-permute-start(f32[4,6,8,1280]{3,2,1,0:T(8,128)S(1)} %get-tuple-element.76), channel_id=1, source_target_pairs={{0,4},{4,0},{8,12},{12,8},{16,20},{20,16},{24,28},{28,24},{32,36},... | collective-permute-start | bytes 2949128 | tf_op jit(solution)/shard_map/ppermute | solution.py:33
  13.0 7.3 %collective-permute-start.4 = (f32[2,64,1280]{2,1,0:T(8,128)S(1)}, f32[2,64,1280]{2,1,0:T(8,128)S(1)}, u32[]{:S(2)}, u32[]{:S(2)}) collective-permute-start(f32[2,64,1280]{2,1,0:T(8,128)S(1)} %get-tuple-element.88), channel_id=1, source_target_pairs={{0,4},{4,0},{8,12},{12,8},{16,20},{20,16},{24,28},{28,24},{32,36},... | collective-permute-start | bytes 1966088 | tf_op jit(solution)/shard_map/ppermute | solution.py:33
  13.1 14.3 %collective-permute-start.5 = (f32[128,1280]{1,0:T(8,128)S(1)}, f32[128,1280]{1,0:T(8,128)S(1)}, u32[]{:S(2)}, u32[]{:S(2)}) collective-permute-start(f32[128,1280]{1,0:T(8,128)S(1)} %get-tuple-element.89), channel_id=1, source_target_pairs={{0,4},{4,0},{8,12},{12,8},{16,20},{20,16},{24,28},{28,24},{32,36},... | collective-permute-start | bytes 1966088 | tf_op jit(solution)/shard_map/ppermute | solution.py:33
  13.6 10.9 %collective-permute-start.1 = (f32[6,8,1280]{2,1,0:T(8,128)S(1)}, f32[6,8,1280]{2,1,0:T(8,128)S(1)}, u32[]{:S(2)}, u32[]{:S(2)}) collective-permute-start(f32[6,8,1280]{2,1,0:T(8,128)S(1)} %get-tuple-element.84), channel_id=1, source_target_pairs={{0,8},{4,28},{8,0},{12,20},{16,24},{20,12},{24,16},{28,4},{32,40},... | collective-permute-start | bytes 737288 | tf_op jit(solution)/shard_map/ppermute | solution.py:33
  14.6 10.0 %collective-permute-start.2 = (f32[6,8,1280]{2,1,0:T(8,128)S(1)}, f32[6,8,1280]{2,1,0:T(8,128)S(1)}, u32[]{:S(2)}, u32[]{:S(2)}) collective-permute-start(f32[6,8,1280]{2,1,0:T(8,128)S(1)} %get-tuple-element.85), channel_id=1, source_target_pairs={{0,16},{4,20},{8,24},{12,28},{16,0},{20,4},{24,8},{28,12},{32,48},... | collective-permute-start | bytes 737288 | tf_op jit(solution)/shard_map/ppermute | solution.py:33
  15.0 12.5 %collective-permute-start.3 = (f32[6,8,1280]{2,1,0:T(8,128)S(1)}, f32[6,8,1280]{2,1,0:T(8,128)S(1)}, u32[]{:S(2)}, u32[]{:S(2)}) collective-permute-start(f32[6,8,1280]{2,1,0:T(8,128)S(1)} %get-tuple-element.86), channel_id=1, source_target_pairs={{0,24},{4,12},{8,16},{12,4},{16,8},{20,28},{24,0},{28,20},{32,56},... | collective-permute-start | bytes 737288 | tf_op jit(solution)/shard_map/ppermute | solution.py:33
  27.5 6.6 %collective-permute-start.6 = (f32[3,8,1280]{2,1,0:T(8,128)S(1)}, f32[3,8,1280]{2,1,0:T(8,128)S(1)}, u32[]{:S(2)}, u32[]{:S(2)}) collective-permute-start(f32[3,8,1280]{2,1,0:T(8,128)S(1)} %slice_add_fusion.6), channel_id=1, source_target_pairs={{0,32},{4,36},{8,40},{12,44},{16,48},{20,52},{24,56},{28,60},{32,0... | collective-permute-start | bytes 368648 | tf_op jit(solution)/shard_map/ppermute | solution.py:33
  27.7 6.5 %collective-permute-start.7 = (f32[2,8,1280]{2,1,0:T(8,128)S(1)}, f32[2,8,1280]{2,1,0:T(8,128)S(1)}, u32[]{:S(2)}, u32[]{:S(2)}) collective-permute-start(f32[2,8,1280]{2,1,0:T(8,128)S(1)} %slice_add_fusion.8), channel_id=1, source_target_pairs={{0,64},{4,68},{8,72},{12,76},{16,80},{20,84},{24,88},{28,92},{32,9... | collective-permute-start | bytes 245768 | tf_op jit(solution)/shard_map/ppermute | solution.py:33
  30.8 18.2 %collective-permute-start.12 = (f32[64,1280]{1,0:T(8,128)S(1)}, f32[64,1280]{1,0:T(8,128)S(1)}, u32[]{:S(2)}, u32[]{:S(2)}) collective-permute-start(f32[64,1280]{1,0:T(8,128)S(1)} %get-tuple-element.111), channel_id=1, source_target_pairs={{0,24},{4,28},{8,16},{12,20},{16,8},{20,12},{24,0},{28,4},{32,56},... | collective-permute-start | bytes 983048 | tf_op jit(solution)/shard_map/ppermute | solution.py:33
  33.6 15.5 %collective-permute-start.13 = (f32[64,1280]{1,0:T(8,128)S(1)}, f32[64,1280]{1,0:T(8,128)S(1)}, u32[]{:S(2)}, u32[]{:S(2)}) collective-permute-start(f32[64,1280]{1,0:T(8,128)S(1)} %get-tuple-element.111), channel_id=1, source_target_pairs={{0,16},{4,20},{8,24},{12,28},{16,0},{20,4},{24,8},{28,12},{32,48},... | collective-permute-start | bytes 983048 | tf_op jit(solution)/shard_map/ppermute | solution.py:33
  33.8 15.3 %collective-permute-start.11 = (f32[64,1280]{1,0:T(8,128)S(1)}, f32[64,1280]{1,0:T(8,128)S(1)}, u32[]{:S(2)}, u32[]{:S(2)}) collective-permute-start(f32[64,1280]{1,0:T(8,128)S(1)} %get-tuple-element.110), channel_id=1, source_target_pairs={{0,8},{4,12},{8,0},{12,4},{16,24},{20,28},{24,16},{28,20},{32,40},... | collective-permute-start | bytes 983048 | tf_op jit(solution)/shard_map/ppermute | solution.py:33
  34.2 6.0 %collective-permute-start.8 = (f32[8,1280]{1,0:T(8,128)S(1)}, f32[8,1280]{1,0:T(8,128)S(1)}, u32[]{:S(2)}, u32[]{:S(2)}) collective-permute-start(f32[8,1280]{1,0:T(8,128)S(1)} %add_bitcast_fusion.1), channel_id=1, source_target_pairs={{0,128},{4,196},{8,136},{12,204},{16,144},{20,212},{24,152},{28,22... | collective-permute-start | bytes 122888 | tf_op jit(solution)/shard_map/ppermute | solution.py:33
  37.6 7.3 %collective-permute-start.9 = (f32[8,1280]{1,0:T(8,128)S(1)}, f32[8,1280]{1,0:T(8,128)S(1)}, u32[]{:S(2)}, u32[]{:S(2)}) collective-permute-start(f32[8,1280]{1,0:T(8,128)S(1)} %add_bitcast_fusion.1), channel_id=1, source_target_pairs={{0,192},{4,132},{8,200},{12,140},{16,208},{20,148},{24,216},{28,15... | collective-permute-start | bytes 122888 | tf_op jit(solution)/shard_map/ppermute | solution.py:33
  44.9 4.1 %collective-permute-start.10 = (f32[3,8,1280]{2,1,0:T(8,128)S(1)}, f32[3,8,1280]{2,1,0:T(8,128)S(1)}, u32[]{:S(2)}, u32[]{:S(2)}) collective-permute-start(f32[3,8,1280]{2,1,0:T(8,128)S(1)} %pad_maximum_fusion.3), channel_id=1, source_target_pairs={{0,32},{4,36},{8,40},{12,44},{16,48},{20,52},{24,56},{28,60},{32,0... | collective-permute-start | bytes 368648 | tf_op jit(solution)/shard_map/ppermute | solution.py:33
  49.2 9.6 %collective-permute-start.17 = (f32[2,64,1280]{2,1,0:T(8,128)S(1)}, f32[2,64,1280]{2,1,0:T(8,128)S(1)}, u32[]{:S(2)}, u32[]{:S(2)}) collective-permute-start(f32[2,64,1280]{2,1,0:T(8,128)S(1)} %pad_maximum_fusion), channel_id=1, source_target_pairs={{0,4},{4,0},{8,12},{12,8},{16,20},{20,16},{24,28},{28,24},{32,36},... | collective-permute-start | bytes 1966088 | tf_op jit(solution)/shard_map/ppermute | solution.py:33
  54.6 8.9 %collective-permute-start.16 = (f32[6,8,1280]{2,1,0:T(8,128)S(1)}, f32[6,8,1280]{2,1,0:T(8,128)S(1)}, u32[]{:S(2)}, u32[]{:S(2)}) collective-permute-start(f32[6,8,1280]{2,1,0:T(8,128)S(1)} %pad_maximum_fusion.2.refs_2_), channel_id=1, source_target_pairs={{0,8},{4,28},{8,0},{12,20},{16,24},{20,12},{24,16},{28,4},{32,40},... | collective-permute-start | bytes 737288 | tf_op jit(solution)/shard_map/ppermute | solution.py:33
  55.6 8.0 %collective-permute-start.15 = (f32[6,8,1280]{2,1,0:T(8,128)S(1)}, f32[6,8,1280]{2,1,0:T(8,128)S(1)}, u32[]{:S(2)}, u32[]{:S(2)}) collective-permute-start(f32[6,8,1280]{2,1,0:T(8,128)S(1)} %pad_maximum_fusion.2.refs_2_), channel_id=1, source_target_pairs={{0,24},{4,12},{8,16},{12,4},{16,8},{20,28},{24,0},{28,20},{32,56},... | collective-permute-start | bytes 737288 | tf_op jit(solution)/shard_map/ppermute | solution.py:33
  55.6 13.2 %collective-permute-start.14 = (f32[6,8,1280]{2,1,0:T(8,128)S(1)}, f32[6,8,1280]{2,1,0:T(8,128)S(1)}, u32[]{:S(2)}, u32[]{:S(2)}) collective-permute-start(f32[6,8,1280]{2,1,0:T(8,128)S(1)} %pad_maximum_fusion.2.refs_2_), channel_id=1, source_target_pairs={{0,16},{4,20},{8,24},{12,28},{16,0},{20,4},{24,8},{28,12},{32,48},... | collective-permute-start | bytes 737288 | tf_op jit(solution)/shard_map/ppermute | solution.py:33
  58.5 10.9 %collective-permute-start.18 = (f32[6,8,1280]{2,1,0:T(8,128)S(1)}, f32[6,8,1280]{2,1,0:T(8,128)S(1)}, u32[]{:S(2)}, u32[]{:S(2)}) collective-permute-start(f32[6,8,1280]{2,1,0:T(8,128)S(1)} %pad_maximum_fusion.2.refs_2_), channel_id=1, source_target_pairs={{0,4},{4,0},{8,12},{12,8},{16,20},{20,16},{24,28},{28,24},{32,36},... | collective-permute-start | bytes 737288 | tf_op jit(solution)/shard_map/ppermute | solution.py:33
  68.8 1.9 %collective-permute-start.21 = (f32[6,8,1280]{2,1,0:T(8,128)S(1)}, f32[6,8,1280]{2,1,0:T(8,128)S(1)}, u32[]{:S(2)}, u32[]{:S(2)}) collective-permute-start(f32[6,8,1280]{2,1,0:T(8,128)S(1)} %collective-permute-done.15.refs_5_), channel_id=1, source_target_pairs={{0,4},{4,0},{8,12},{12,8},{16,20},{20,16},{24,28},{28,24},{32,36},... | collective-permute-start | bytes 737288 | tf_op jit(solution)/shard_map/ppermute | solution.py:33
  72.4 5.2 %collective-permute-start.22 = (f32[256,128]{1,0:T(8,128)S(1)}, f32[256,128]{1,0:T(8,128)S(1)}, u32[]{:S(2)}, u32[]{:S(2)}) collective-permute-start(f32[256,128]{1,0:T(8,128)S(1)} %get-tuple-element.133), channel_id=1, source_target_pairs={{0,1},{1,0},{2,3},{3,2},{4,7},{5,6},{6,5},{7,4},{8,9},{9,8},{10,11... | collective-permute-start | bytes 393224 | tf_op jit(solution)/shard_map/ppermute | solution.py:43
  75.2 4.1 %collective-permute-start.23 = (f32[256,128]{1,0:T(8,128)S(1)}, f32[256,128]{1,0:T(8,128)S(1)}, u32[]{:S(2)}, u32[]{:S(2)}) collective-permute-start(f32[256,128]{1,0:T(8,128)S(1)} %get-tuple-element.134), channel_id=1, source_target_pairs={{0,3},{1,2},{2,1},{3,0},{4,5},{5,4},{6,7},{7,6},{8,11},{9,10},{10,... | collective-permute-start | bytes 393224 | tf_op jit(solution)/shard_map/ppermute | solution.py:43
  79.4 4.0 %collective-permute-start.24 = (f32[256,128]{1,0:T(8,128)S(1)}, f32[256,128]{1,0:T(8,128)S(1)}, u32[]{:S(2)}, u32[]{:S(2)}) collective-permute-start(f32[256,128]{1,0:T(8,128)S(1)} %add.119), channel_id=1, source_target_pairs={{0,3},{1,2},{2,1},{3,0},{4,5},{5,4},{6,7},{7,6},{8,11},{9,10},{10,... | collective-permute-start | bytes 393224 | tf_op jit(solution)/shard_map/ppermute | solution.py:43
  79.7 5.5 %collective-permute-start.25 = (f32[256,128]{1,0:T(8,128)S(1)}, f32[256,128]{1,0:T(8,128)S(1)}, u32[]{:S(2)}, u32[]{:S(2)}) collective-permute-start(f32[256,128]{1,0:T(8,128)S(1)} %add.120), channel_id=1, source_target_pairs={{0,1},{1,0},{2,3},{3,2},{4,7},{5,6},{6,5},{7,4},{8,9},{9,8},{10,11... | collective-permute-start | bytes 393224 | tf_op jit(solution)/shard_map/ppermute | solution.py:43
  (4 other events, 13.4 us)

commit v6 on v5

--- a/solution.py
+++ b/solution.py
@@ -164,18 +164,14 @@
     )(code, gain, q, v, e)
 
 
-def near_kernel(qt, v_ref, e_ref, w_ref, z_ref, x_ref, own_ref, oth_ref, res):
+def near_kernel(qt, v_ref, e_ref, w_ref, z_ref, own_ref, oth_ref, res):
     position, core, x, z0 = coords()
-    for index, k in enumerate((2, 3, 1)):
+    for index, k in enumerate((2, 3)):
         for block in BLOCKS:
             level_operand(z_ref, index, k, position, w_ref, v_ref, e_ref, block)
-            out = dot(qt[...], z_ref[index, :, block], 1, 0)
-            if k == 1:
-                x_ref[:, block] = out
-            else:
-                res[...] = out.reshape(2, STATE // 2, BLK)
-                own_ref[index, :, block] = res[core]
-                oth_ref[index, :, block] = res[core ^ 1]
+            res[...] = dot(qt[...], z_ref[index, :, block], 1, 0).reshape(2, STATE // 2, BLK)
+            own_ref[index, :, block] = res[core]
+            oth_ref[index, :, block] = res[core ^ 1]
 
 
 def near_states(qt, v, e, w):
@@ -183,10 +179,9 @@
     return pl.pallas_call(
         near_kernel,
         in_specs=[VMEM] * 4,
-        out_specs=[VMEM] * 4,
+        out_specs=[VMEM] * 3,
         out_shape=[
-            shape(3, TOK, COLS, kind=BF),
-            shape(STATE, COLS),
+            shape(2, TOK, COLS, kind=BF),
             shape(2, half, COLS),
             shape(2, half, COLS),
         ],
@@ -258,7 +253,13 @@
     lax.fori_loop(0, count, one_block, 0)
 
 
-def first_local_kernel(q_ref, v_ref, e_ref, w_ref, m_ref, d_ref, score, flipped, grad, z):
+def first_local_kernel(
+    q_ref, v_ref, e_ref, w_ref, qt, m_ref, d_ref, score, flipped, grad, z1_ref, x1_ref, z
+):
+    position = lax.axis_index("seq")
+    for block in BLOCKS:
+        level_operand(z1_ref, 0, 1, position, w_ref, v_ref, e_ref, block)
+        x1_ref[:, block] = dot(qt[...], z1_ref[0, :, block], 1, 0)
     grad[...] = jnp.zeros_like(grad)
     for index, (t, s, level) in enumerate(LOCAL):
         qt_rows = q_ref[t * TILE : (t + 1) * TILE, :]
@@ -296,7 +297,8 @@
     wide = BLK if stage else FIRST * BLK
     table = shape(7, TILE, TILE, kind=BF)
     grad = shape(7, TILE, TILE)
-    outs = ([table, table, grad], [grad], [shape(TOK, STATE)])[stage]
+    level_one = [shape(1, TOK, COLS, kind=BF), shape(STATE, COLS)]
+    outs = ([table, table, grad] + level_one, [grad], [shape(TOK, STATE)])[stage]
     scratch = [pltpu.VMEM((7, TILE, BLK), BF)]
     if stage == 2:
         scratch = [pltpu.VMEM((7, TILE, TILE), F32)] + scratch
@@ -313,7 +315,7 @@
 
 
 def mid_kernel(
-    q_ref, w_ref, ma, da, mb, db, mc, dc, dq_in, z_ref, y1_ref, y2_ref, y3_ref, y23o_ref, m_ref, d_ref, dq_ref, y
+    q_ref, w_ref, ma, da, mb, db, mc, dc, dq_in, z_ref, z1_ref, y1_ref, y2_ref, y3_ref, y23o_ref, m_ref, d_ref, dq_ref, y
 ):
     position, core, x, z0 = coords()
     half = STATE // 2
@@ -333,21 +335,22 @@
     for block in BLOCKS:
         add_outer(q_ref, w_ref, (2, 3, 1), position, y, m_ref, d_ref, block)
         for index in range(3):
-            grads = grads + dot(z_ref[index, :, block], y[index, :, block].astype(BF), 1, 1)
+            z = z1_ref[0, :, block] if index == 2 else z_ref[index, :, block]
+            grads = grads + dot(z, y[index, :, block].astype(BF), 1, 1)
     dq_ref[...] = grads
 
 
-def mid_part(q, w, own, zn, y1, y2, y3, y23o):
+def mid_part(q, w, own, zn, z1, y1, y2, y3, y23o):
     return pl.pallas_call(
         mid_kernel,
-        in_specs=[VMEM] * 14,
+        in_specs=[VMEM] * 15,
         out_specs=[VMEM] * 3,
         out_shape=[shape(TOK, COLS), shape(TOK, COLS), shape(TOK, STATE)],
         scratch_shapes=[pltpu.VMEM((3, STATE, COLS), F32)],
         compiler_params=params(30),
         cost_estimate=cost(),
         name="mid_part",
-    )(q, w, *own, zn, y1, y2, y3, y23o)
+    )(q, w, *own, zn, z1, y1, y2, y3, y23o)
 
 
 def score_kernel(*refs):
@@ -437,16 +440,15 @@
     q_hbm, v_hbm, e_hbm, gain, code = [pltpu.with_memory_space_constraint(a, pltpu.HBM) for a in args]
     w, q, qt, v, e, zf, own_f, oth_f = far_states(code, gain, q_hbm, v_hbm, e_hbm)
     got_f = send(oth_f, 1)
-    zn, x1, own_n, oth_n = near_states(qt, v, e, w)
+    zn, own_n, oth_n = near_states(qt, v, e, w)
 
     chip = [own_f[j] + got_f[j] for j in range(4)]
-    chip, x1, oth_n, v1 = tie((chip, x1, oth_n, v))
+    chip, oth_n, v1 = tie((chip, oth_n, v))
     slices = [send(chip[j], 2 * j, 2 * (4 - j)) for j in (1, 2, 3)]
     got_n = send(oth_n, 1)
-    y1 = send(x1, 1)
     near = [own_n[i] + got_n[i] for i in range(2)]
-    ma, da, score, flipped, grad = local_part(0, q, v1, e, w, ())
-    slices, near, y1, grad = tie((slices, near, y1, grad))
+    ma, da, score, flipped, grad, z1, x1 = local_part(0, q, v1, e, w, (qt,))
+    slices, near, grad = tie((slices, near, grad))
     mine = sum((s[0] for s in slices), chip[0][0])
     cross = sum((s[1:4] for s in slices), chip[0][1:4])
     pair = sum((s[4:6] for s in slices), chip[0][4:6])
@@ -466,11 +468,12 @@
     mc, dc, dq = local_part(2, q, v3, e, w, (score, flipped, grad))
     rest, dq = tie((rest, dq))
     quad = jnp.concatenate([half[0:1], rest[0:1], low[1:3], half[1:3] + rest[1:3]])
-    quad, dq, y2, y3 = tie((quad, dq, y2, y3))
+    quad, dq, x1, y2, y3 = tie((quad, dq, x1, y2, y3))
+    y1 = send(x1, 1)
     y3 = y3[0] + y3[1]
     y23o = send(jnp.stack([y2, y3]), 1)
     pieces = [quad] + [send(quad, 2 * j, 2 * (4 - j)) for j in (1, 2, 3)]
-    m, d, dq = mid_part(q, w, (ma, da, mb, db, mc, dc, dq), zn, y1, y2, y3, y23o)
+    m, d, dq = mid_part(q, w, (ma, da, mb, db, mc, dc, dq), zn, z1, y1, y2, y3, y23o)
     for j in (1, 3, 2):
         pieces[j], dq = tie((pieces[j], dq))
     pieces = pieces + [send(p, 1) for p in pieces]

time: 86.8 us -> 86.3 us (level)
    pallas_call x2, Pallas kernels: 7.58 us -> 6.33 us  [the longest x1 3.74 us: mid_part(): pl.pallas_call(mid_kernel, in_specs=[VMEM] * 15, out_specs=[VMEM] * 3, ou...]
    pallas_call x3, Pallas kernels: 5.61 us -> 6.75 us  [local_part(): pl.pallas_call(kernel, in_specs=[VMEM] * (4 + len(tables)), out_specs=[VM...]
  transfers between devices with their start and end apart: 26 -> 26, of which waited for: 12 -> 14; matrix products, arithmetic and copies ran while one was open for 0% -> 0% of each run, Pallas kernels for 20% -> 20%
where the time goes in v6:
time: 86.3 us; the launch traced here: 86.2 us
  starting transfers between devices  34.3 us (40%)
  waiting for transfers between devices  26.5 us (31%)
  Pallas kernels  23.3 us (27%)
  other arithmetic  1.15 us (1%)
  between operations  0.89 us (1%)
    ppermute x22, starting transfers between devices, send(): return lax.ppermute(value, 'seq', pairs)  29.9 us
    ppermute x22, waiting for transfers between devices, send(): return lax.ppermute(value, 'seq', pairs)  21.7 us
    pallas_call x3, Pallas kernels, local_part(): pl.pallas_call(kernel, in_specs=[VMEM] * (4 + len(tables)), out_specs=[VM...  6.75 us
    pallas_call x1, Pallas kernels, far_states(): pl.pallas_call(far_kernel, in_specs=[HBM] * 5, out_specs=[VMEM] * 8, out_...  5.15 us
    ppermute x4, waiting for transfers between devices, send_head(): return lax.ppermute(value, ('seq', 'head'), pairs)  4.8 us
    ppermute x4, starting transfers between devices, send_head(): return lax.ppermute(value, ('seq', 'head'), pairs)  4.34 us
    pallas_call x1, Pallas kernels, mid_part(): pl.pallas_call(mid_kernel, in_specs=[VMEM] * 15, out_specs=[VMEM] * 3, ou...  3.74 us
    pallas_call x1, Pallas kernels, near_states(): pl.pallas_call(near_kernel, in_specs=[VMEM] * 4, out_specs=[VMEM] * 3, ou...  2.59 us
  transfers between devices with their start and end apart: 26, of which 14 were waited for; matrix products, arithmetic and copies ran while one was open for 0% of the time, Pallas kernels for 20%

profile of v6, /device:TPU:1, one launch (start us, length us, event | category | flops | bytes accessed | tf_op | source)
XLA Modules:
  0.0 86.2 jit_solution(7226339532107974943)
XLA Ops:
  0.6 5.1 %far_states.1 = (f32[10,8,1280]{2,1,0:T(8,128)S(1)}, bf16[512,128]{1,0:T(8,128)(2,1)S(1)}, bf16[128,512]{1,0:T(8,128)(2,1)S(1)}, bf16[512,1280]{1,0:T(8,128)(2,1...) custom-call(s32[8]{0:T(128)} %code_hbm.1, ...), custom_call_target="tpu_custom_call" | custom-call | flops 1024 | bytes 1024 | tf_op jit(solution)/shard_map/far_states/pallas_call | solution.py:140
  5.8 3.3 %collective-permute-start = (f32[4,6,8,1280]{3,2,1,0:T(8,128)S(1)}, f32[4,6,8,1280]{3,2,1,0:T(8,128)S(1)}, u32[]{:S(2)}, u32[]{:S(2)}) collective-permute-start(f32[4,6,8,1280]{3,2,1,0:T(8,128)S(1)} %get-tuple-element.76), channel_id=1, source_target_pairs={{0,4},{4,0},{8,12},{12,8},{16,20},{20,16},{24,28},{28,24},{32,36},... | collective-permute-start | bytes 2949128 | tf_op jit(solution)/shard_map/ppermute | solution.py:33
  9.1 2.6 %near_states.1 = (bf16[2,512,1280]{2,1,0:T(8,128)(2,1)S(1)}, f32[2,64,1280]{2,1,0:T(8,128)S(1)}, f32[2,64,1280]{2,1,0:T(8,128)S(1)}) custom-call(bf16[128,512]{1,0:T(8,128)(2,1)S(1)} %get-tuple-element.77.qt, bf16[512,1280]{1,0:T(8,128)(2,1)S(1)} %get-tuple-element.103.v_ref, bf16[512,1280]{1,0:T(8,128)(2,1)S(1)} %get-tuple-element.79.e_ref, ...), custom_call_target="tpu_custom_call" | custom-call | flops 1024 | bytes 1024 | tf_op jit(solution)/shard_map/near_states/pallas_call | solution.py:179
  13.4 1.9 %collective-permute-start.3 = (f32[6,8,1280]{2,1,0:T(8,128)S(1)}, f32[6,8,1280]{2,1,0:T(8,128)S(1)}, u32[]{:S(2)}, u32[]{:S(2)}) collective-permute-start(f32[6,8,1280]{2,1,0:T(8,128)S(1)} %get-tuple-element.85), channel_id=1, source_target_pairs={{0,24},{4,12},{8,16},{12,4},{16,8},{20,28},{24,0},{28,20},{32,56},... | collective-permute-start | bytes 737288 | tf_op jit(solution)/shard_map/ppermute | solution.py:33
  15.3 4.6 %first_local.1 = (f32[512,768]{1,0:T(8,128)S(1)}, f32[512,768]{1,0:T(8,128)S(1)}, bf16[7,256,256]{2,1,0:T(8,128)(2,1)S(1)}, bf16[7,256,256]{2,1,0:T(8,128)(2,1)S...) custom-call(bf16[512,128]{1,0:T(8,128)(2,1)S(1)} %get-tuple-element.88.q_ref, ...), custom_call_target="tpu_custom_call" | custom-call | flops 8589934592 | bytes 33554432 | tf_op jit(solution)/shard_map/first_local/pallas_call | solution.py:305
  20.3 2.2 %collective-permute-done.2 = f32[6,8,1280]{2,1,0:T(8,128)S(1)} collective-permute-done((f32[6,8,1280]{2,1,0:T(8,128)S(1)}, f32[6,8,1280]{2,1,0:T(8,128)S(1)}, u32[]{:S(2)}, u32[]{:S(2)}) %collective-permute-start.2) | collective-permute-done | bytes 245792 | tf_op jit(solution)/shard_map/ppermute | solution.py:33
  22.4 3.7 %collective-permute-done.3 = f32[6,8,1280]{2,1,0:T(8,128)S(1)} collective-permute-done((f32[6,8,1280]{2,1,0:T(8,128)S(1)}, f32[6,8,1280]{2,1,0:T(8,128)S(1)}, u32[]{:S(2)}, u32[]{:S(2)}) %collective-permute-start.3) | collective-permute-done | bytes 245792 | tf_op jit(solution)/shard_map/ppermute | solution.py:33
  26.3 3.2 %collective-permute-start.6 = (f32[2,8,1280]{2,1,0:T(8,128)S(1)}, f32[2,8,1280]{2,1,0:T(8,128)S(1)}, u32[]{:S(2)}, u32[]{:S(2)}) collective-permute-start(f32[2,8,1280]{2,1,0:T(8,128)S(1)} %slice_add_fusion.8), channel_id=1, source_target_pairs={{0,64},{4,68},{8,72},{12,76},{16,80},{20,84},{24,88},{28,92},{32,9... | collective-permute-start | bytes 245768 | tf_op jit(solution)/shard_map/ppermute | solution.py:33
  29.5 2.7 %collective-permute-start.11 = (f32[64,1280]{1,0:T(8,128)S(1)}, f32[64,1280]{1,0:T(8,128)S(1)}, u32[]{:S(2)}, u32[]{:S(2)}) collective-permute-start(f32[64,1280]{1,0:T(8,128)S(1)} %get-tuple-element.110), channel_id=1, source_target_pairs={{0,24},{4,28},{8,16},{12,20},{16,8},{20,12},{24,0},{28,4},{32,56},... | collective-permute-start | bytes 983048 | tf_op jit(solution)/shard_map/ppermute | solution.py:33
  32.8 3.4 %collective-permute-start.7 = (f32[8,1280]{1,0:T(8,128)S(1)}, f32[8,1280]{1,0:T(8,128)S(1)}, u32[]{:S(2)}, u32[]{:S(2)}) collective-permute-start(f32[8,1280]{1,0:T(8,128)S(1)} %add_bitcast_fusion.1), channel_id=1, source_target_pairs={{0,128},{4,196},{8,136},{12,204},{16,144},{20,212},{24,152},{28,22... | collective-permute-start | bytes 122888 | tf_op jit(solution)/shard_map/ppermute | solution.py:33
  36.3 1.7 %collective-permute-start.8 = (f32[8,1280]{1,0:T(8,128)S(1)}, f32[8,1280]{1,0:T(8,128)S(1)}, u32[]{:S(2)}, u32[]{:S(2)}) collective-permute-start(f32[8,1280]{1,0:T(8,128)S(1)} %add_bitcast_fusion.1), channel_id=1, source_target_pairs={{0,192},{4,132},{8,200},{12,140},{16,208},{20,148},{24,216},{28,15... | collective-permute-start | bytes 122888 | tf_op jit(solution)/shard_map/ppermute | solution.py:33
  38.9 4.9 %collective-permute-done.8 = f32[8,1280]{1,0:T(8,128)S(1)} collective-permute-done((f32[8,1280]{1,0:T(8,128)S(1)}, f32[8,1280]{1,0:T(8,128)S(1)}, u32[]{:S(2)}, u32[]{:S(2)}) %collective-permute-start.8) | collective-permute-done | bytes 40992 | tf_op jit(solution)/shard_map/ppermute | solution.py:33
  46.0 2.0 %collective-permute-done.9 = f32[3,8,1280]{2,1,0:T(8,128)S(1)} collective-permute-done((f32[3,8,1280]{2,1,0:T(8,128)S(1)}, f32[3,8,1280]{2,1,0:T(8,128)S(1)}, u32[]{:S(2)}, u32[]{:S(2)}) %collective-permute-start.9) | collective-permute-done | bytes 122912 | tf_op jit(solution)/shard_map/ppermute | solution.py:33
  48.2 5.1 %collective-permute-start.17 = (f32[2,64,1280]{2,1,0:T(8,128)S(1)}, f32[2,64,1280]{2,1,0:T(8,128)S(1)}, u32[]{:S(2)}, u32[]{:S(2)}) collective-permute-start(f32[2,64,1280]{2,1,0:T(8,128)S(1)} %pad_maximum_fusion), channel_id=1, source_target_pairs={{0,4},{4,0},{8,12},{12,8},{16,20},{20,16},{24,28},{28,24},{32,36},... | collective-permute-start | bytes 1966088 | tf_op jit(solution)/shard_map/ppermute | solution.py:33
  53.4 1.7 %collective-permute-start.15 = (f32[6,8,1280]{2,1,0:T(8,128)S(1)}, f32[6,8,1280]{2,1,0:T(8,128)S(1)}, u32[]{:S(2)}, u32[]{:S(2)}) collective-permute-start(f32[6,8,1280]{2,1,0:T(8,128)S(1)} %pad_maximum_fusion.2.refs_2_), channel_id=1, source_target_pairs={{0,8},{4,28},{8,0},{12,20},{16,24},{20,12},{24,16},{28,4},{32,40},... | collective-permute-start | bytes 737288 | tf_op jit(solution)/shard_map/ppermute | solution.py:33
  55.1 2.2 %collective-permute-start.13 = (f32[6,8,1280]{2,1,0:T(8,128)S(1)}, f32[6,8,1280]{2,1,0:T(8,128)S(1)}, u32[]{:S(2)}, u32[]{:S(2)}) collective-permute-start(f32[6,8,1280]{2,1,0:T(8,128)S(1)} %pad_maximum_fusion.2.refs_2_), channel_id=1, source_target_pairs={{0,16},{4,20},{8,24},{12,28},{16,0},{20,4},{24,8},{28,12},{32,48},... | collective-permute-start | bytes 737288 | tf_op jit(solution)/shard_map/ppermute | solution.py:33
  57.9 3.7 %mid_part.1 = (f32[512,1280]{1,0:T(8,128)S(1)}, f32[512,1280]{1,0:T(8,128)S(1)}, f32[512,128]{1,0:T(8,128)S(1)}) custom-call(bf16[512,128]{1,0:T(8,128)(2,1)S(1)} %get-tuple-element.88.q_ref, f32[10,8,1280]{2,1,0:T(8,128)S(1)} %get-tuple-element.80.w_ref, f32[512,768]{1,0:T(8,128)S(1)} %get-tuple-element.112.ma, f32[512,768]{1,0:T(8,128)S(1)} %get-tuple-element.113.da, ...), custom_call_target="tpu_custom_call" | custom-call | flops 1024 | bytes 1024 | tf_op jit(solution)/shard_map/mid_part/pallas_call | solution.py:344
  62.8 6.1 %collective-permute-done.13.refs_4_ = f32[6,8,1280]{2,1,0:T(8,128)S(1)} collective-permute-done((f32[6,8,1280]{2,1,0:T(8,128)S(1)}, f32[6,8,1280]{2,1,0:T(8,128)S(1)}, u32[]{:S(2)}, u32[]{:S(2)}) %collective-permute-start.13) | collective-permute-done | bytes 245792 | tf_op jit(solution)/shard_map/ppermute | solution.py:33
  71.1 1.3 %score_part.1 = (f32[256,128]{1,0:T(8,128)S(1)}, f32[256,128]{1,0:T(8,128)S(1)}, f32[3,128,1280]{2,1,0:T(8,128)S(1)}) custom-call(f32[512,128]{1,0:T(8,128)S(1)} %get-tuple-element.128.refs_0_, bf16[3,512,1280]{2,1,0:T(8,128)(2,1)S(1)} %get-tuple-element.129.refs_1_, f32[6,8,1280]{2,1,0:T(8,128)S(1)} %pad_maximum_fusion.2.refs_2_, ...), custom_call_target="tpu_custom_call" | custom-call | flops 1024 | bytes 1024 | tf_op jit(solution)/shard_map/score_part/pallas_call | solution.py:379
  72.4 2.8 %collective-permute-start.22 = (f32[256,128]{1,0:T(8,128)S(1)}, f32[256,128]{1,0:T(8,128)S(1)}, u32[]{:S(2)}, u32[]{:S(2)}) collective-permute-start(f32[256,128]{1,0:T(8,128)S(1)} %get-tuple-element.133), channel_id=1, source_target_pairs={{0,1},{1,0},{2,3},{3,2},{4,7},{5,6},{6,5},{7,4},{8,9},{9,8},{10,11... | collective-permute-start | bytes 393224 | tf_op jit(solution)/shard_map/ppermute | solution.py:43
  75.2 1.6 %last_values.1 = bf16[512,1280]{1,0:T(8,128)(2,1)} custom-call(bf16[512,128]{1,0:T(8,128)(2,1)S(1)} %get-tuple-element.88.q_ref, f32[512,1280]{1,0:T(8,128)S(1)} %get-tuple-element.135.d_in, f32[3,128,1280]{2,1,0:T(8,128)S(1)} %get-tuple-element.136.y_ref), custom_call_target="tpu_custom_call" | custom-call | flops 1024 | bytes 1024 | tf_op jit(solution)/shard_map/last_values/pallas_call | solution.py:401
  77.6 1.8 %collective-permute-done.23 = f32[256,128]{1,0:T(8,128)S(1)} collective-permute-done((f32[256,128]{1,0:T(8,128)S(1)}, f32[256,128]{1,0:T(8,128)S(1)}, u32[]{:S(2)}, u32[]{:S(2)}) %collective-permute-start.23) | collective-permute-done | bytes 131104 | tf_op jit(solution)/shard_map/ppermute | solution.py:43
  80.9 2.2 %last_mixed.1 = bf16[512,1280]{1,0:T(8,128)(2,1)} custom-call(bf16[512,128]{1,0:T(8,128)(2,1)S(1)} %get-tuple-element.88.q_ref, f32[10,8,1280]{2,1,0:T(8,128)S(1)} %get-tuple-element.80.w_ref, f32[512,1280]{1,0:T(8,128)S(1)} %get-tuple-element.142.m_in, f32[3,128,1280]{2,1,0:T(8,128)S(1)} %get-tuple-element.136.y_ref), custom_call_target="tpu_custom_call" | custom-call | flops 1024 | bytes 1024 | tf_op jit(solution)/shard_map/last_mixed/pallas_call | solution.py:426
  83.3 2.1 %collective-permute-done.25 = f32[256,128]{1,0:T(8,128)S(1)} collective-permute-done((f32[256,128]{1,0:T(8,128)S(1)}, f32[256,128]{1,0:T(8,128)S(1)}, u32[]{:S(2)}, u32[]{:S(2)}) %collective-permute-start.25) | collective-permute-done | bytes 131104 | tf_op jit(solution)/shard_map/ppermute | solution.py:43
  (59 shorter events, 13.3 us)
Async XLA Ops:
  5.8 5.9 %collective-permute-start = (f32[4,6,8,1280]{3,2,1,0:T(8,128)S(1)}, f32[4,6,8,1280]{3,2,1,0:T(8,128)S(1)}, u32[]{:S(2)}, u32[]{:S(2)}) collective-permute-start(f32[4,6,8,1280]{3,2,1,0:T(8,128)S(1)} %get-tuple-element.76), channel_id=1, source_target_pairs={{0,4},{4,0},{8,12},{12,8},{16,20},{20,16},{24,28},{28,24},{32,36},... | collective-permute-start | bytes 2949128 | tf_op jit(solution)/shard_map/ppermute | solution.py:33
  11.8 8.0 %collective-permute-start.4 = (f32[2,64,1280]{2,1,0:T(8,128)S(1)}, f32[2,64,1280]{2,1,0:T(8,128)S(1)}, u32[]{:S(2)}, u32[]{:S(2)}) collective-permute-start(f32[2,64,1280]{2,1,0:T(8,128)S(1)} %get-tuple-element.87), channel_id=1, source_target_pairs={{0,4},{4,0},{8,12},{12,8},{16,20},{20,16},{24,28},{28,24},{32,36},... | collective-permute-start | bytes 1966088 | tf_op jit(solution)/shard_map/ppermute | solution.py:33
  11.9 8.3 %collective-permute-start.1 = (f32[6,8,1280]{2,1,0:T(8,128)S(1)}, f32[6,8,1280]{2,1,0:T(8,128)S(1)}, u32[]{:S(2)}, u32[]{:S(2)}) collective-permute-start(f32[6,8,1280]{2,1,0:T(8,128)S(1)} %get-tuple-element.83), channel_id=1, source_target_pairs={{0,8},{4,28},{8,0},{12,20},{16,24},{20,12},{24,16},{28,4},{32,40},... | collective-permute-start | bytes 737288 | tf_op jit(solution)/shard_map/ppermute | solution.py:33
  13.0 9.5 %collective-permute-start.2 = (f32[6,8,1280]{2,1,0:T(8,128)S(1)}, f32[6,8,1280]{2,1,0:T(8,128)S(1)}, u32[]{:S(2)}, u32[]{:S(2)}) collective-permute-start(f32[6,8,1280]{2,1,0:T(8,128)S(1)} %get-tuple-element.84), channel_id=1, source_target_pairs={{0,16},{4,20},{8,24},{12,28},{16,0},{20,4},{24,8},{28,12},{32,48},... | collective-permute-start | bytes 737288 | tf_op jit(solution)/shard_map/ppermute | solution.py:33
  13.4 12.8 %collective-permute-start.3 = (f32[6,8,1280]{2,1,0:T(8,128)S(1)}, f32[6,8,1280]{2,1,0:T(8,128)S(1)}, u32[]{:S(2)}, u32[]{:S(2)}) collective-permute-start(f32[6,8,1280]{2,1,0:T(8,128)S(1)} %get-tuple-element.85), channel_id=1, source_target_pairs={{0,24},{4,12},{8,16},{12,4},{16,8},{20,28},{24,0},{28,20},{32,56},... | collective-permute-start | bytes 737288 | tf_op jit(solution)/shard_map/ppermute | solution.py:33
  26.2 6.7 %collective-permute-start.5 = (f32[3,8,1280]{2,1,0:T(8,128)S(1)}, f32[3,8,1280]{2,1,0:T(8,128)S(1)}, u32[]{:S(2)}, u32[]{:S(2)}) collective-permute-start(f32[3,8,1280]{2,1,0:T(8,128)S(1)} %slice_add_fusion.6), channel_id=1, source_target_pairs={{0,32},{4,36},{8,40},{12,44},{16,48},{20,52},{24,56},{28,60},{32,0... | collective-permute-start | bytes 368648 | tf_op jit(solution)/shard_map/ppermute | solution.py:33
  26.3 6.5 %collective-permute-start.6 = (f32[2,8,1280]{2,1,0:T(8,128)S(1)}, f32[2,8,1280]{2,1,0:T(8,128)S(1)}, u32[]{:S(2)}, u32[]{:S(2)}) collective-permute-start(f32[2,8,1280]{2,1,0:T(8,128)S(1)} %slice_add_fusion.8), channel_id=1, source_target_pairs={{0,64},{4,68},{8,72},{12,76},{16,80},{20,84},{24,88},{28,92},{32,9... | collective-permute-start | bytes 245768 | tf_op jit(solution)/shard_map/ppermute | solution.py:33
  29.5 18.6 %collective-permute-start.11 = (f32[64,1280]{1,0:T(8,128)S(1)}, f32[64,1280]{1,0:T(8,128)S(1)}, u32[]{:S(2)}, u32[]{:S(2)}) collective-permute-start(f32[64,1280]{1,0:T(8,128)S(1)} %get-tuple-element.110), channel_id=1, source_target_pairs={{0,24},{4,28},{8,16},{12,20},{16,8},{20,12},{24,0},{28,4},{32,56},... | collective-permute-start | bytes 983048 | tf_op jit(solution)/shard_map/ppermute | solution.py:33
  32.2 15.9 %collective-permute-start.12 = (f32[64,1280]{1,0:T(8,128)S(1)}, f32[64,1280]{1,0:T(8,128)S(1)}, u32[]{:S(2)}, u32[]{:S(2)}) collective-permute-start(f32[64,1280]{1,0:T(8,128)S(1)} %get-tuple-element.110), channel_id=1, source_target_pairs={{0,16},{4,20},{8,24},{12,28},{16,0},{20,4},{24,8},{28,12},{32,48},... | collective-permute-start | bytes 983048 | tf_op jit(solution)/shard_map/ppermute | solution.py:33
  32.6 15.5 %collective-permute-start.10 = (f32[64,1280]{1,0:T(8,128)S(1)}, f32[64,1280]{1,0:T(8,128)S(1)}, u32[]{:S(2)}, u32[]{:S(2)}) collective-permute-start(f32[64,1280]{1,0:T(8,128)S(1)} %get-tuple-element.109), channel_id=1, source_target_pairs={{0,8},{4,12},{8,0},{12,4},{16,24},{20,28},{24,16},{28,20},{32,40},... | collective-permute-start | bytes 983048 | tf_op jit(solution)/shard_map/ppermute | solution.py:33
  32.8 6.1 %collective-permute-start.7 = (f32[8,1280]{1,0:T(8,128)S(1)}, f32[8,1280]{1,0:T(8,128)S(1)}, u32[]{:S(2)}, u32[]{:S(2)}) collective-permute-start(f32[8,1280]{1,0:T(8,128)S(1)} %add_bitcast_fusion.1), channel_id=1, source_target_pairs={{0,128},{4,196},{8,136},{12,204},{16,144},{20,212},{24,152},{28,22... | collective-permute-start | bytes 122888 | tf_op jit(solution)/shard_map/ppermute | solution.py:33
  36.3 7.6 %collective-permute-start.8 = (f32[8,1280]{1,0:T(8,128)S(1)}, f32[8,1280]{1,0:T(8,128)S(1)}, u32[]{:S(2)}, u32[]{:S(2)}) collective-permute-start(f32[8,1280]{1,0:T(8,128)S(1)} %add_bitcast_fusion.1), channel_id=1, source_target_pairs={{0,192},{4,132},{8,200},{12,140},{16,208},{20,148},{24,216},{28,15... | collective-permute-start | bytes 122888 | tf_op jit(solution)/shard_map/ppermute | solution.py:33
  43.9 4.1 %collective-permute-start.9 = (f32[3,8,1280]{2,1,0:T(8,128)S(1)}, f32[3,8,1280]{2,1,0:T(8,128)S(1)}, u32[]{:S(2)}, u32[]{:S(2)}) collective-permute-start(f32[3,8,1280]{2,1,0:T(8,128)S(1)} %pad_maximum_fusion.3), channel_id=1, source_target_pairs={{0,32},{4,36},{8,40},{12,44},{16,48},{20,52},{24,56},{28,60},{32,0... | collective-permute-start | bytes 368648 | tf_op jit(solution)/shard_map/ppermute | solution.py:33
  48.2 9.1 %collective-permute-start.17 = (f32[2,64,1280]{2,1,0:T(8,128)S(1)}, f32[2,64,1280]{2,1,0:T(8,128)S(1)}, u32[]{:S(2)}, u32[]{:S(2)}) collective-permute-start(f32[2,64,1280]{2,1,0:T(8,128)S(1)} %pad_maximum_fusion), channel_id=1, source_target_pairs={{0,4},{4,0},{8,12},{12,8},{16,20},{20,16},{24,28},{28,24},{32,36},... | collective-permute-start | bytes 1966088 | tf_op jit(solution)/shard_map/ppermute | solution.py:33
  53.3 4.6 %collective-permute-start.16 = (f32[128,1280]{1,0:T(8,128)S(1)}, f32[128,1280]{1,0:T(8,128)S(1)}, u32[]{:S(2)}, u32[]{:S(2)}) collective-permute-start(f32[128,1280]{1,0:T(8,128)S(1)} %get-tuple-element.121), channel_id=1, source_target_pairs={{0,4},{4,0},{8,12},{12,8},{16,20},{20,16},{24,28},{28,24},{32,36},... | collective-permute-start | bytes 1966088 | tf_op jit(solution)/shard_map/ppermute | solution.py:33
  53.4 8.3 %collective-permute-start.15 = (f32[6,8,1280]{2,1,0:T(8,128)S(1)}, f32[6,8,1280]{2,1,0:T(8,128)S(1)}, u32[]{:S(2)}, u32[]{:S(2)}) collective-permute-start(f32[6,8,1280]{2,1,0:T(8,128)S(1)} %pad_maximum_fusion.2.refs_2_), channel_id=1, source_target_pairs={{0,8},{4,28},{8,0},{12,20},{16,24},{20,12},{24,16},{28,4},{32,40},... | collective-permute-start | bytes 737288 | tf_op jit(solution)/shard_map/ppermute | solution.py:33
  55.1 7.6 %collective-permute-start.14 = (f32[6,8,1280]{2,1,0:T(8,128)S(1)}, f32[6,8,1280]{2,1,0:T(8,128)S(1)}, u32[]{:S(2)}, u32[]{:S(2)}) collective-permute-start(f32[6,8,1280]{2,1,0:T(8,128)S(1)} %pad_maximum_fusion.2.refs_2_), channel_id=1, source_target_pairs={{0,24},{4,12},{8,16},{12,4},{16,8},{20,28},{24,0},{28,20},{32,56},... | collective-permute-start | bytes 737288 | tf_op jit(solution)/shard_map/ppermute | solution.py:33
  55.1 13.7 %collective-permute-start.13 = (f32[6,8,1280]{2,1,0:T(8,128)S(1)}, f32[6,8,1280]{2,1,0:T(8,128)S(1)}, u32[]{:S(2)}, u32[]{:S(2)}) collective-permute-start(f32[6,8,1280]{2,1,0:T(8,128)S(1)} %pad_maximum_fusion.2.refs_2_), channel_id=1, source_target_pairs={{0,16},{4,20},{8,24},{12,28},{16,0},{20,4},{24,8},{28,12},{32,48},... | collective-permute-start | bytes 737288 | tf_op jit(solution)/shard_map/ppermute | solution.py:33
  57.3 12.5 %collective-permute-start.18 = (f32[6,8,1280]{2,1,0:T(8,128)S(1)}, f32[6,8,1280]{2,1,0:T(8,128)S(1)}, u32[]{:S(2)}, u32[]{:S(2)}) collective-permute-start(f32[6,8,1280]{2,1,0:T(8,128)S(1)} %pad_maximum_fusion.2.refs_2_), channel_id=1, source_target_pairs={{0,4},{4,0},{8,12},{12,8},{16,20},{20,16},{24,28},{28,24},{32,36},... | collective-permute-start | bytes 737288 | tf_op jit(solution)/shard_map/ppermute | solution.py:33
  69.3 1.7 %collective-permute-start.19 = (f32[6,8,1280]{2,1,0:T(8,128)S(1)}, f32[6,8,1280]{2,1,0:T(8,128)S(1)}, u32[]{:S(2)}, u32[]{:S(2)}) collective-permute-start(f32[6,8,1280]{2,1,0:T(8,128)S(1)} %collective-permute-done.15.refs_3_), channel_id=1, source_target_pairs={{0,4},{4,0},{8,12},{12,8},{16,20},{20,16},{24,28},{28,24},{32,36},... | collective-permute-start | bytes 737288 | tf_op jit(solution)/shard_map/ppermute | solution.py:33
  72.4 5.2 %collective-permute-start.22 = (f32[256,128]{1,0:T(8,128)S(1)}, f32[256,128]{1,0:T(8,128)S(1)}, u32[]{:S(2)}, u32[]{:S(2)}) collective-permute-start(f32[256,128]{1,0:T(8,128)S(1)} %get-tuple-element.133), channel_id=1, source_target_pairs={{0,1},{1,0},{2,3},{3,2},{4,7},{5,6},{6,5},{7,4},{8,9},{9,8},{10,11... | collective-permute-start | bytes 393224 | tf_op jit(solution)/shard_map/ppermute | solution.py:43
  75.2 4.1 %collective-permute-start.23 = (f32[256,128]{1,0:T(8,128)S(1)}, f32[256,128]{1,0:T(8,128)S(1)}, u32[]{:S(2)}, u32[]{:S(2)}) collective-permute-start(f32[256,128]{1,0:T(8,128)S(1)} %get-tuple-element.134), channel_id=1, source_target_pairs={{0,3},{1,2},{2,1},{3,0},{4,5},{5,4},{6,7},{7,6},{8,11},{9,10},{10,... | collective-permute-start | bytes 393224 | tf_op jit(solution)/shard_map/ppermute | solution.py:43
  79.4 3.9 %collective-permute-start.24 = (f32[256,128]{1,0:T(8,128)S(1)}, f32[256,128]{1,0:T(8,128)S(1)}, u32[]{:S(2)}, u32[]{:S(2)}) collective-permute-start(f32[256,128]{1,0:T(8,128)S(1)} %add.119), channel_id=1, source_target_pairs={{0,3},{1,2},{2,1},{3,0},{4,5},{5,4},{6,7},{7,6},{8,11},{9,10},{10,... | collective-permute-start | bytes 393224 | tf_op jit(solution)/shard_map/ppermute | solution.py:43
  79.9 5.5 %collective-permute-start.25 = (f32[256,128]{1,0:T(8,128)S(1)}, f32[256,128]{1,0:T(8,128)S(1)}, u32[]{:S(2)}, u32[]{:S(2)}) collective-permute-start(f32[256,128]{1,0:T(8,128)S(1)} %add.120), channel_id=1, source_target_pairs={{0,1},{1,0},{2,3},{3,2},{4,7},{5,6},{6,5},{7,4},{8,9},{9,8},{10,11... | collective-permute-start | bytes 393224 | tf_op jit(solution)/shard_map/ppermute | solution.py:43
  (4 other events, 13.3 us)

commit v7 on v6

--- a/solution.py
+++ b/solution.py
@@ -456,7 +456,7 @@
     low = send(cross, 8)
     five = send(pair, 16)
     y2 = send(near[0], 2)
-    y3 = [send(near[1], 6), send(near[1], 4)]
+    y3 = [send(near[1], 6, 4), send(near[1], 4, 6)]
     low, five = tie((low, five))
     six = mine + low[0]
     six, v2 = tie((six, v1))

time: 86.3 us -> 86.3 us (level)
  no operation moved by 1% of the time
where the time goes in v7:
time: 86.3 us; the launch traced here: 86.2 us
  starting transfers between devices  33.5 us (39%)
  waiting for transfers between devices  27.2 us (32%)
  Pallas kernels  23.4 us (27%)
  other arithmetic  1.15 us (1%)
  between operations  0.9 us (1%)
    ppermute x22, starting transfers between devices, send(): return lax.ppermute(value, 'seq', pairs)  29.2 us
    ppermute x22, waiting for transfers between devices, send(): return lax.ppermute(value, 'seq', pairs)  22.4 us
    pallas_call x3, Pallas kernels, local_part(): pl.pallas_call(kernel, in_specs=[VMEM] * (4 + len(tables)), out_specs=[VM...  6.75 us
    pallas_call x1, Pallas kernels, far_states(): pl.pallas_call(far_kernel, in_specs=[HBM] * 5, out_specs=[VMEM] * 8, out_...  5.15 us
    ppermute x4, waiting for transfers between devices, send_head(): return lax.ppermute(value, ('seq', 'head'), pairs)  4.8 us
    ppermute x4, starting transfers between devices, send_head(): return lax.ppermute(value, ('seq', 'head'), pairs)  4.34 us
    pallas_call x1, Pallas kernels, mid_part(): pl.pallas_call(mid_kernel, in_specs=[VMEM] * 15, out_specs=[VMEM] * 3, ou...  3.74 us
    pallas_call x1, Pallas kernels, near_states(): pl.pallas_call(near_kernel, in_specs=[VMEM] * 4, out_specs=[VMEM] * 3, ou...  2.59 us
  transfers between devices with their start and end apart: 26, of which 14 were waited for; matrix products, arithmetic and copies ran while one was open for 0% of the time, Pallas kernels for 20%

profile of v7, /device:TPU:1, one launch (start us, length us, event | category | flops | bytes accessed | tf_op | source)
XLA Modules:
  0.0 86.2 jit_solution(7445905195045026542)
XLA Ops:
  0.6 5.1 %far_states.1 = (f32[10,8,1280]{2,1,0:T(8,128)S(1)}, bf16[512,128]{1,0:T(8,128)(2,1)S(1)}, bf16[128,512]{1,0:T(8,128)(2,1)S(1)}, bf16[512,1280]{1,0:T(8,128)(2,1...) custom-call(s32[8]{0:T(128)} %code_hbm.1, ...), custom_call_target="tpu_custom_call" | custom-call | flops 1024 | bytes 1024 | tf_op jit(solution)/shard_map/far_states/pallas_call | solution.py:140
  5.8 3.3 %collective-permute-start = (f32[4,6,8,1280]{3,2,1,0:T(8,128)S(1)}, f32[4,6,8,1280]{3,2,1,0:T(8,128)S(1)}, u32[]{:S(2)}, u32[]{:S(2)}) collective-permute-start(f32[4,6,8,1280]{3,2,1,0:T(8,128)S(1)} %get-tuple-element.76), channel_id=1, source_target_pairs={{0,4},{4,0},{8,12},{12,8},{16,20},{20,16},{24,28},{28,24},{32,36},... | collective-permute-start | bytes 2949128 | tf_op jit(solution)/shard_map/ppermute | solution.py:33
  9.1 2.6 %near_states.1 = (bf16[2,512,1280]{2,1,0:T(8,128)(2,1)S(1)}, f32[2,64,1280]{2,1,0:T(8,128)S(1)}, f32[2,64,1280]{2,1,0:T(8,128)S(1)}) custom-call(bf16[128,512]{1,0:T(8,128)(2,1)S(1)} %get-tuple-element.77.qt, bf16[512,1280]{1,0:T(8,128)(2,1)S(1)} %get-tuple-element.103.v_ref, bf16[512,1280]{1,0:T(8,128)(2,1)S(1)} %get-tuple-element.79.e_ref, ...), custom_call_target="tpu_custom_call" | custom-call | flops 1024 | bytes 1024 | tf_op jit(solution)/shard_map/near_states/pallas_call | solution.py:179
  13.4 1.9 %collective-permute-start.3 = (f32[6,8,1280]{2,1,0:T(8,128)S(1)}, f32[6,8,1280]{2,1,0:T(8,128)S(1)}, u32[]{:S(2)}, u32[]{:S(2)}) collective-permute-start(f32[6,8,1280]{2,1,0:T(8,128)S(1)} %get-tuple-element.85), channel_id=1, source_target_pairs={{0,24},{4,12},{8,16},{12,4},{16,8},{20,28},{24,0},{28,20},{32,56},... | collective-permute-start | bytes 737288 | tf_op jit(solution)/shard_map/ppermute | solution.py:33
  15.3 4.6 %first_local.1 = (f32[512,768]{1,0:T(8,128)S(1)}, f32[512,768]{1,0:T(8,128)S(1)}, bf16[7,256,256]{2,1,0:T(8,128)(2,1)S(1)}, bf16[7,256,256]{2,1,0:T(8,128)(2,1)S...) custom-call(bf16[512,128]{1,0:T(8,128)(2,1)S(1)} %get-tuple-element.88.q_ref, ...), custom_call_target="tpu_custom_call" | custom-call | flops 8589934592 | bytes 33554432 | tf_op jit(solution)/shard_map/first_local/pallas_call | solution.py:305
  20.3 2.2 %collective-permute-done.2 = f32[6,8,1280]{2,1,0:T(8,128)S(1)} collective-permute-done((f32[6,8,1280]{2,1,0:T(8,128)S(1)}, f32[6,8,1280]{2,1,0:T(8,128)S(1)}, u32[]{:S(2)}, u32[]{:S(2)}) %collective-permute-start.2) | collective-permute-done | bytes 245792 | tf_op jit(solution)/shard_map/ppermute | solution.py:33
  22.4 3.7 %collective-permute-done.3 = f32[6,8,1280]{2,1,0:T(8,128)S(1)} collective-permute-done((f32[6,8,1280]{2,1,0:T(8,128)S(1)}, f32[6,8,1280]{2,1,0:T(8,128)S(1)}, u32[]{:S(2)}, u32[]{:S(2)}) %collective-permute-start.3) | collective-permute-done | bytes 245792 | tf_op jit(solution)/shard_map/ppermute | solution.py:33
  26.3 3.2 %collective-permute-start.6 = (f32[2,8,1280]{2,1,0:T(8,128)S(1)}, f32[2,8,1280]{2,1,0:T(8,128)S(1)}, u32[]{:S(2)}, u32[]{:S(2)}) collective-permute-start(f32[2,8,1280]{2,1,0:T(8,128)S(1)} %slice_add_fusion.8), channel_id=1, source_target_pairs={{0,64},{4,68},{8,72},{12,76},{16,80},{20,84},{24,88},{28,92},{32,9... | collective-permute-start | bytes 245768 | tf_op jit(solution)/shard_map/ppermute | solution.py:33
  29.5 2.5 %collective-permute-start.11 = (f32[64,1280]{1,0:T(8,128)S(1)}, f32[64,1280]{1,0:T(8,128)S(1)}, u32[]{:S(2)}, u32[]{:S(2)}) collective-permute-start(f32[64,1280]{1,0:T(8,128)S(1)} %get-tuple-element.110), channel_id=1, source_target_pairs={{0,24},{4,20},{8,16},{12,28},{16,8},{20,4},{24,0},{28,12},{32,56},... | collective-permute-start | bytes 983048 | tf_op jit(solution)/shard_map/ppermute | solution.py:33
  33.2 3.4 %collective-permute-start.7 = (f32[8,1280]{1,0:T(8,128)S(1)}, f32[8,1280]{1,0:T(8,128)S(1)}, u32[]{:S(2)}, u32[]{:S(2)}) collective-permute-start(f32[8,1280]{1,0:T(8,128)S(1)} %add_bitcast_fusion.1), channel_id=1, source_target_pairs={{0,128},{4,196},{8,136},{12,204},{16,144},{20,212},{24,152},{28,22... | collective-permute-start | bytes 122888 | tf_op jit(solution)/shard_map/ppermute | solution.py:33
  36.6 1.4 %collective-permute-start.8 = (f32[8,1280]{1,0:T(8,128)S(1)}, f32[8,1280]{1,0:T(8,128)S(1)}, u32[]{:S(2)}, u32[]{:S(2)}) collective-permute-start(f32[8,1280]{1,0:T(8,128)S(1)} %add_bitcast_fusion.1), channel_id=1, source_target_pairs={{0,192},{4,132},{8,200},{12,140},{16,208},{20,148},{24,216},{28,15... | collective-permute-start | bytes 122888 | tf_op jit(solution)/shard_map/ppermute | solution.py:33
  38.9 5.6 %collective-permute-done.8 = f32[8,1280]{1,0:T(8,128)S(1)} collective-permute-done((f32[8,1280]{1,0:T(8,128)S(1)}, f32[8,1280]{1,0:T(8,128)S(1)}, u32[]{:S(2)}, u32[]{:S(2)}) %collective-permute-start.8) | collective-permute-done | bytes 40992 | tf_op jit(solution)/shard_map/ppermute | solution.py:33
  46.2 2.1 %collective-permute-done.9 = f32[3,8,1280]{2,1,0:T(8,128)S(1)} collective-permute-done((f32[3,8,1280]{2,1,0:T(8,128)S(1)}, f32[3,8,1280]{2,1,0:T(8,128)S(1)}, u32[]{:S(2)}, u32[]{:S(2)}) %collective-permute-start.9) | collective-permute-done | bytes 122912 | tf_op jit(solution)/shard_map/ppermute | solution.py:33
  48.5 4.8 %collective-permute-start.17 = (f32[2,64,1280]{2,1,0:T(8,128)S(1)}, f32[2,64,1280]{2,1,0:T(8,128)S(1)}, u32[]{:S(2)}, u32[]{:S(2)}) collective-permute-start(f32[2,64,1280]{2,1,0:T(8,128)S(1)} %pad_maximum_fusion), channel_id=1, source_target_pairs={{0,4},{4,0},{8,12},{12,8},{16,20},{20,16},{24,28},{28,24},{32,36},... | collective-permute-start | bytes 1966088 | tf_op jit(solution)/shard_map/ppermute | solution.py:33
  53.4 1.7 %collective-permute-start.15 = (f32[6,8,1280]{2,1,0:T(8,128)S(1)}, f32[6,8,1280]{2,1,0:T(8,128)S(1)}, u32[]{:S(2)}, u32[]{:S(2)}) collective-permute-start(f32[6,8,1280]{2,1,0:T(8,128)S(1)} %pad_maximum_fusion.2.refs_2_), channel_id=1, source_target_pairs={{0,8},{4,28},{8,0},{12,20},{16,24},{20,12},{24,16},{28,4},{32,40},... | collective-permute-start | bytes 737288 | tf_op jit(solution)/shard_map/ppermute | solution.py:33
  55.1 2.2 %collective-permute-start.13 = (f32[6,8,1280]{2,1,0:T(8,128)S(1)}, f32[6,8,1280]{2,1,0:T(8,128)S(1)}, u32[]{:S(2)}, u32[]{:S(2)}) collective-permute-start(f32[6,8,1280]{2,1,0:T(8,128)S(1)} %pad_maximum_fusion.2.refs_2_), channel_id=1, source_target_pairs={{0,16},{4,20},{8,24},{12,28},{16,0},{20,4},{24,8},{28,12},{32,48},... | collective-permute-start | bytes 737288 | tf_op jit(solution)/shard_map/ppermute | solution.py:33
  57.9 3.7 %mid_part.1 = (f32[512,1280]{1,0:T(8,128)S(1)}, f32[512,1280]{1,0:T(8,128)S(1)}, f32[512,128]{1,0:T(8,128)S(1)}) custom-call(bf16[512,128]{1,0:T(8,128)(2,1)S(1)} %get-tuple-element.88.q_ref, f32[10,8,1280]{2,1,0:T(8,128)S(1)} %get-tuple-element.80.w_ref, f32[512,768]{1,0:T(8,128)S(1)} %get-tuple-element.112.ma, f32[512,768]{1,0:T(8,128)S(1)} %get-tuple-element.113.da, ...), custom_call_target="tpu_custom_call" | custom-call | flops 1024 | bytes 1024 | tf_op jit(solution)/shard_map/mid_part/pallas_call | solution.py:344
  62.8 6.1 %collective-permute-done.13.refs_4_ = f32[6,8,1280]{2,1,0:T(8,128)S(1)} collective-permute-done((f32[6,8,1280]{2,1,0:T(8,128)S(1)}, f32[6,8,1280]{2,1,0:T(8,128)S(1)}, u32[]{:S(2)}, u32[]{:S(2)}) %collective-permute-start.13) | collective-permute-done | bytes 245792 | tf_op jit(solution)/shard_map/ppermute | solution.py:33
  71.1 1.3 %score_part.1 = (f32[256,128]{1,0:T(8,128)S(1)}, f32[256,128]{1,0:T(8,128)S(1)}, f32[3,128,1280]{2,1,0:T(8,128)S(1)}) custom-call(f32[512,128]{1,0:T(8,128)S(1)} %get-tuple-element.128.refs_0_, bf16[3,512,1280]{2,1,0:T(8,128)(2,1)S(1)} %get-tuple-element.129.refs_1_, f32[6,8,1280]{2,1,0:T(8,128)S(1)} %pad_maximum_fusion.2.refs_2_, ...), custom_call_target="tpu_custom_call" | custom-call | flops 1024 | bytes 1024 | tf_op jit(solution)/shard_map/score_part/pallas_call | solution.py:379
  72.4 2.8 %collective-permute-start.22 = (f32[256,128]{1,0:T(8,128)S(1)}, f32[256,128]{1,0:T(8,128)S(1)}, u32[]{:S(2)}, u32[]{:S(2)}) collective-permute-start(f32[256,128]{1,0:T(8,128)S(1)} %get-tuple-element.133), channel_id=1, source_target_pairs={{0,1},{1,0},{2,3},{3,2},{4,7},{5,6},{6,5},{7,4},{8,9},{9,8},{10,11... | collective-permute-start | bytes 393224 | tf_op jit(solution)/shard_map/ppermute | solution.py:43
  75.2 1.6 %last_values.1 = bf16[512,1280]{1,0:T(8,128)(2,1)} custom-call(bf16[512,128]{1,0:T(8,128)(2,1)S(1)} %get-tuple-element.88.q_ref, f32[512,1280]{1,0:T(8,128)S(1)} %get-tuple-element.135.d_in, f32[3,128,1280]{2,1,0:T(8,128)S(1)} %get-tuple-element.136.y_ref), custom_call_target="tpu_custom_call" | custom-call | flops 1024 | bytes 1024 | tf_op jit(solution)/shard_map/last_values/pallas_call | solution.py:401
  77.6 1.8 %collective-permute-done.23 = f32[256,128]{1,0:T(8,128)S(1)} collective-permute-done((f32[256,128]{1,0:T(8,128)S(1)}, f32[256,128]{1,0:T(8,128)S(1)}, u32[]{:S(2)}, u32[]{:S(2)}) %collective-permute-start.23) | collective-permute-done | bytes 131104 | tf_op jit(solution)/shard_map/ppermute | solution.py:43
  80.9 2.2 %last_mixed.1 = bf16[512,1280]{1,0:T(8,128)(2,1)} custom-call(bf16[512,128]{1,0:T(8,128)(2,1)S(1)} %get-tuple-element.88.q_ref, f32[10,8,1280]{2,1,0:T(8,128)S(1)} %get-tuple-element.80.w_ref, f32[512,1280]{1,0:T(8,128)S(1)} %get-tuple-element.142.m_in, f32[3,128,1280]{2,1,0:T(8,128)S(1)} %get-tuple-element.136.y_ref), custom_call_target="tpu_custom_call" | custom-call | flops 1024 | bytes 1024 | tf_op jit(solution)/shard_map/last_mixed/pallas_call | solution.py:426
  83.3 2.1 %collective-permute-done.25 = f32[256,128]{1,0:T(8,128)S(1)} collective-permute-done((f32[256,128]{1,0:T(8,128)S(1)}, f32[256,128]{1,0:T(8,128)S(1)}, u32[]{:S(2)}, u32[]{:S(2)}) %collective-permute-start.25) | collective-permute-done | bytes 131104 | tf_op jit(solution)/shard_map/ppermute | solution.py:43
  (59 shorter events, 13.4 us)
Async XLA Ops:
  5.8 5.9 %collective-permute-start = (f32[4,6,8,1280]{3,2,1,0:T(8,128)S(1)}, f32[4,6,8,1280]{3,2,1,0:T(8,128)S(1)}, u32[]{:S(2)}, u32[]{:S(2)}) collective-permute-start(f32[4,6,8,1280]{3,2,1,0:T(8,128)S(1)} %get-tuple-element.76), channel_id=1, source_target_pairs={{0,4},{4,0},{8,12},{12,8},{16,20},{20,16},{24,28},{28,24},{32,36},... | collective-permute-start | bytes 2949128 | tf_op jit(solution)/shard_map/ppermute | solution.py:33
  11.8 8.0 %collective-permute-start.4 = (f32[2,64,1280]{2,1,0:T(8,128)S(1)}, f32[2,64,1280]{2,1,0:T(8,128)S(1)}, u32[]{:S(2)}, u32[]{:S(2)}) collective-permute-start(f32[2,64,1280]{2,1,0:T(8,128)S(1)} %get-tuple-element.87), channel_id=1, source_target_pairs={{0,4},{4,0},{8,12},{12,8},{16,20},{20,16},{24,28},{28,24},{32,36},... | collective-permute-start | bytes 1966088 | tf_op jit(solution)/shard_map/ppermute | solution.py:33
  11.9 8.3 %collective-permute-start.1 = (f32[6,8,1280]{2,1,0:T(8,128)S(1)}, f32[6,8,1280]{2,1,0:T(8,128)S(1)}, u32[]{:S(2)}, u32[]{:S(2)}) collective-permute-start(f32[6,8,1280]{2,1,0:T(8,128)S(1)} %get-tuple-element.83), channel_id=1, source_target_pairs={{0,8},{4,28},{8,0},{12,20},{16,24},{20,12},{24,16},{28,4},{32,40},... | collective-permute-start | bytes 737288 | tf_op jit(solution)/shard_map/ppermute | solution.py:33
  13.0 9.5 %collective-permute-start.2 = (f32[6,8,1280]{2,1,0:T(8,128)S(1)}, f32[6,8,1280]{2,1,0:T(8,128)S(1)}, u32[]{:S(2)}, u32[]{:S(2)}) collective-permute-start(f32[6,8,1280]{2,1,0:T(8,128)S(1)} %get-tuple-element.84), channel_id=1, source_target_pairs={{0,16},{4,20},{8,24},{12,28},{16,0},{20,4},{24,8},{28,12},{32,48},... | collective-permute-start | bytes 737288 | tf_op jit(solution)/shard_map/ppermute | solution.py:33
  13.4 12.8 %collective-permute-start.3 = (f32[6,8,1280]{2,1,0:T(8,128)S(1)}, f32[6,8,1280]{2,1,0:T(8,128)S(1)}, u32[]{:S(2)}, u32[]{:S(2)}) collective-permute-start(f32[6,8,1280]{2,1,0:T(8,128)S(1)} %get-tuple-element.85), channel_id=1, source_target_pairs={{0,24},{4,12},{8,16},{12,4},{16,8},{20,28},{24,0},{28,20},{32,56},... | collective-permute-start | bytes 737288 | tf_op jit(solution)/shard_map/ppermute | solution.py:33
  26.2 7.0 %collective-permute-start.5 = (f32[3,8,1280]{2,1,0:T(8,128)S(1)}, f32[3,8,1280]{2,1,0:T(8,128)S(1)}, u32[]{:S(2)}, u32[]{:S(2)}) collective-permute-start(f32[3,8,1280]{2,1,0:T(8,128)S(1)} %slice_add_fusion.6), channel_id=1, source_target_pairs={{0,32},{4,36},{8,40},{12,44},{16,48},{20,52},{24,56},{28,60},{32,0... | collective-permute-start | bytes 368648 | tf_op jit(solution)/shard_map/ppermute | solution.py:33
  26.3 6.8 %collective-permute-start.6 = (f32[2,8,1280]{2,1,0:T(8,128)S(1)}, f32[2,8,1280]{2,1,0:T(8,128)S(1)}, u32[]{:S(2)}, u32[]{:S(2)}) collective-permute-start(f32[2,8,1280]{2,1,0:T(8,128)S(1)} %slice_add_fusion.8), channel_id=1, source_target_pairs={{0,64},{4,68},{8,72},{12,76},{16,80},{20,84},{24,88},{28,92},{32,9... | collective-permute-start | bytes 245768 | tf_op jit(solution)/shard_map/ppermute | solution.py:33
  29.5 18.9 %collective-permute-start.11 = (f32[64,1280]{1,0:T(8,128)S(1)}, f32[64,1280]{1,0:T(8,128)S(1)}, u32[]{:S(2)}, u32[]{:S(2)}) collective-permute-start(f32[64,1280]{1,0:T(8,128)S(1)} %get-tuple-element.110), channel_id=1, source_target_pairs={{0,24},{4,20},{8,16},{12,28},{16,8},{20,4},{24,0},{28,12},{32,56},... | collective-permute-start | bytes 983048 | tf_op jit(solution)/shard_map/ppermute | solution.py:33
  32.0 16.4 %collective-permute-start.12 = (f32[64,1280]{1,0:T(8,128)S(1)}, f32[64,1280]{1,0:T(8,128)S(1)}, u32[]{:S(2)}, u32[]{:S(2)}) collective-permute-start(f32[64,1280]{1,0:T(8,128)S(1)} %get-tuple-element.110), channel_id=1, source_target_pairs={{0,16},{4,28},{8,24},{12,20},{16,0},{20,12},{24,8},{28,4},{32,48},... | collective-permute-start | bytes 983048 | tf_op jit(solution)/shard_map/ppermute | solution.py:33
  33.2 15.2 %collective-permute-start.10 = (f32[64,1280]{1,0:T(8,128)S(1)}, f32[64,1280]{1,0:T(8,128)S(1)}, u32[]{:S(2)}, u32[]{:S(2)}) collective-permute-start(f32[64,1280]{1,0:T(8,128)S(1)} %get-tuple-element.109), channel_id=1, source_target_pairs={{0,8},{4,12},{8,0},{12,4},{16,24},{20,28},{24,16},{28,20},{32,40},... | collective-permute-start | bytes 983048 | tf_op jit(solution)/shard_map/ppermute | solution.py:33
  33.2 5.7 %collective-permute-start.7 = (f32[8,1280]{1,0:T(8,128)S(1)}, f32[8,1280]{1,0:T(8,128)S(1)}, u32[]{:S(2)}, u32[]{:S(2)}) collective-permute-start(f32[8,1280]{1,0:T(8,128)S(1)} %add_bitcast_fusion.1), channel_id=1, source_target_pairs={{0,128},{4,196},{8,136},{12,204},{16,144},{20,212},{24,152},{28,22... | collective-permute-start | bytes 122888 | tf_op jit(solution)/shard_map/ppermute | solution.py:33
  36.6 7.9 %collective-permute-start.8 = (f32[8,1280]{1,0:T(8,128)S(1)}, f32[8,1280]{1,0:T(8,128)S(1)}, u32[]{:S(2)}, u32[]{:S(2)}) collective-permute-start(f32[8,1280]{1,0:T(8,128)S(1)} %add_bitcast_fusion.1), channel_id=1, source_target_pairs={{0,192},{4,132},{8,200},{12,140},{16,208},{20,148},{24,216},{28,15... | collective-permute-start | bytes 122888 | tf_op jit(solution)/shard_map/ppermute | solution.py:33
  44.5 3.8 %collective-permute-start.9 = (f32[3,8,1280]{2,1,0:T(8,128)S(1)}, f32[3,8,1280]{2,1,0:T(8,128)S(1)}, u32[]{:S(2)}, u32[]{:S(2)}) collective-permute-start(f32[3,8,1280]{2,1,0:T(8,128)S(1)} %pad_maximum_fusion.3), channel_id=1, source_target_pairs={{0,32},{4,36},{8,40},{12,44},{16,48},{20,52},{24,56},{28,60},{32,0... | collective-permute-start | bytes 368648 | tf_op jit(solution)/shard_map/ppermute | solution.py:33
  48.5 8.7 %collective-permute-start.17 = (f32[2,64,1280]{2,1,0:T(8,128)S(1)}, f32[2,64,1280]{2,1,0:T(8,128)S(1)}, u32[]{:S(2)}, u32[]{:S(2)}) collective-permute-start(f32[2,64,1280]{2,1,0:T(8,128)S(1)} %pad_maximum_fusion), channel_id=1, source_target_pairs={{0,4},{4,0},{8,12},{12,8},{16,20},{20,16},{24,28},{28,24},{32,36},... | collective-permute-start | bytes 1966088 | tf_op jit(solution)/shard_map/ppermute | solution.py:33
  53.3 4.6 %collective-permute-start.16 = (f32[128,1280]{1,0:T(8,128)S(1)}, f32[128,1280]{1,0:T(8,128)S(1)}, u32[]{:S(2)}, u32[]{:S(2)}) collective-permute-start(f32[128,1280]{1,0:T(8,128)S(1)} %get-tuple-element.121), channel_id=1, source_target_pairs={{0,4},{4,0},{8,12},{12,8},{16,20},{20,16},{24,28},{28,24},{32,36},... | collective-permute-start | bytes 1966088 | tf_op jit(solution)/shard_map/ppermute | solution.py:33
  53.4 8.3 %collective-permute-start.15 = (f32[6,8,1280]{2,1,0:T(8,128)S(1)}, f32[6,8,1280]{2,1,0:T(8,128)S(1)}, u32[]{:S(2)}, u32[]{:S(2)}) collective-permute-start(f32[6,8,1280]{2,1,0:T(8,128)S(1)} %pad_maximum_fusion.2.refs_2_), channel_id=1, source_target_pairs={{0,8},{4,28},{8,0},{12,20},{16,24},{20,12},{24,16},{28,4},{32,40},... | collective-permute-start | bytes 737288 | tf_op jit(solution)/shard_map/ppermute | solution.py:33
  55.1 7.6 %collective-permute-start.14 = (f32[6,8,1280]{2,1,0:T(8,128)S(1)}, f32[6,8,1280]{2,1,0:T(8,128)S(1)}, u32[]{:S(2)}, u32[]{:S(2)}) collective-permute-start(f32[6,8,1280]{2,1,0:T(8,128)S(1)} %pad_maximum_fusion.2.refs_2_), channel_id=1, source_target_pairs={{0,24},{4,12},{8,16},{12,4},{16,8},{20,28},{24,0},{28,20},{32,56},... | collective-permute-start | bytes 737288 | tf_op jit(solution)/shard_map/ppermute | solution.py:33
  55.1 13.7 %collective-permute-start.13 = (f32[6,8,1280]{2,1,0:T(8,128)S(1)}, f32[6,8,1280]{2,1,0:T(8,128)S(1)}, u32[]{:S(2)}, u32[]{:S(2)}) collective-permute-start(f32[6,8,1280]{2,1,0:T(8,128)S(1)} %pad_maximum_fusion.2.refs_2_), channel_id=1, source_target_pairs={{0,16},{4,20},{8,24},{12,28},{16,0},{20,4},{24,8},{28,12},{32,48},... | collective-permute-start | bytes 737288 | tf_op jit(solution)/shard_map/ppermute | solution.py:33
  57.3 12.5 %collective-permute-start.18 = (f32[6,8,1280]{2,1,0:T(8,128)S(1)}, f32[6,8,1280]{2,1,0:T(8,128)S(1)}, u32[]{:S(2)}, u32[]{:S(2)}) collective-permute-start(f32[6,8,1280]{2,1,0:T(8,128)S(1)} %pad_maximum_fusion.2.refs_2_), channel_id=1, source_target_pairs={{0,4},{4,0},{8,12},{12,8},{16,20},{20,16},{24,28},{28,24},{32,36},... | collective-permute-start | bytes 737288 | tf_op jit(solution)/shard_map/ppermute | solution.py:33
  69.3 1.7 %collective-permute-start.19 = (f32[6,8,1280]{2,1,0:T(8,128)S(1)}, f32[6,8,1280]{2,1,0:T(8,128)S(1)}, u32[]{:S(2)}, u32[]{:S(2)}) collective-permute-start(f32[6,8,1280]{2,1,0:T(8,128)S(1)} %collective-permute-done.15.refs_3_), channel_id=1, source_target_pairs={{0,4},{4,0},{8,12},{12,8},{16,20},{20,16},{24,28},{28,24},{32,36},... | collective-permute-start | bytes 737288 | tf_op jit(solution)/shard_map/ppermute | solution.py:33
  72.4 5.2 %collective-permute-start.22 = (f32[256,128]{1,0:T(8,128)S(1)}, f32[256,128]{1,0:T(8,128)S(1)}, u32[]{:S(2)}, u32[]{:S(2)}) collective-permute-start(f32[256,128]{1,0:T(8,128)S(1)} %get-tuple-element.133), channel_id=1, source_target_pairs={{0,1},{1,0},{2,3},{3,2},{4,7},{5,6},{6,5},{7,4},{8,9},{9,8},{10,11... | collective-permute-start | bytes 393224 | tf_op jit(solution)/shard_map/ppermute | solution.py:43
  75.2 4.1 %collective-permute-start.23 = (f32[256,128]{1,0:T(8,128)S(1)}, f32[256,128]{1,0:T(8,128)S(1)}, u32[]{:S(2)}, u32[]{:S(2)}) collective-permute-start(f32[256,128]{1,0:T(8,128)S(1)} %get-tuple-element.134), channel_id=1, source_target_pairs={{0,3},{1,2},{2,1},{3,0},{4,5},{5,4},{6,7},{7,6},{8,11},{9,10},{10,... | collective-permute-start | bytes 393224 | tf_op jit(solution)/shard_map/ppermute | solution.py:43
  79.4 3.9 %collective-permute-start.24 = (f32[256,128]{1,0:T(8,128)S(1)}, f32[256,128]{1,0:T(8,128)S(1)}, u32[]{:S(2)}, u32[]{:S(2)}) collective-permute-start(f32[256,128]{1,0:T(8,128)S(1)} %add.119), channel_id=1, source_target_pairs={{0,3},{1,2},{2,1},{3,0},{4,5},{5,4},{6,7},{7,6},{8,11},{9,10},{10,... | collective-permute-start | bytes 393224 | tf_op jit(solution)/shard_map/ppermute | solution.py:43
  79.9 5.5 %collective-permute-start.25 = (f32[256,128]{1,0:T(8,128)S(1)}, f32[256,128]{1,0:T(8,128)S(1)}, u32[]{:S(2)}, u32[]{:S(2)}) collective-permute-start(f32[256,128]{1,0:T(8,128)S(1)} %add.120), channel_id=1, source_target_pairs={{0,1},{1,0},{2,3},{3,2},{4,7},{5,6},{6,5},{7,4},{8,9},{9,8},{10,11... | collective-permute-start | bytes 393224 | tf_op jit(solution)/shard_map/ppermute | solution.py:43
  (4 other events, 12.6 us)
